TPU v7x, 128 devices: a whole 4x4x4 slice. The times are simulated.
128 devices in a mesh: lat: 8 (over y, z_hi), lon: 16 (over z_lo, x, core).
Axes of the slice: x: 4, y: 4, z: 4 (z_hi: 2, z_lo: 2; z = z_hi * 2 + z_lo), core: 2. Of those that a mesh axis runs over, the one named last changes fastest.
Arguments:
- tokens: bfloat16 [1, 96, 384, 384], P(None, 'lat', 'lon'), may hold values from -6 to 6
- cotangent: bfloat16 [1, 48, 192, 768], P(None, 'lat', 'lon'), may hold values from -6 to 6
- bias_one: float32 [17, 6, 3312], replicated, may hold values from -4 to 324
- qkv_one: bfloat16 [192, 576], replicated, may hold values from -0.4375 to 0.4375
- proj_one: bfloat16 [192, 192], replicated, may hold values from -0.4375 to 0.4375
- up_one: bfloat16 [192, 768], replicated, may hold values from -0.4375 to 0.4375
- down_one: bfloat16 [768, 192], replicated, may hold values from -0.21875 to 0.21875
- merge_weight: bfloat16 [768, 384], replicated, may hold values from -0.21875 to 0.21875
- bias_two: float32 [9, 12, 3312], replicated, may hold values from -4 to 324
- qkv_two: bfloat16 [384, 1152], replicated, may hold values from -0.3125 to 0.3125
- proj_two: bfloat16 [384, 384], replicated, may hold values from -0.3125 to 0.3125
- up_two: bfloat16 [384, 1536], replicated, may hold values from -0.3125 to 0.3125
- down_two: bfloat16 [1536, 384], replicated, may hold values from -0.15625 to 0.15625
Outputs:
- level_two_out: float32 [1, 48, 192, 768], P(None, 'lat', 'lon')
- token_grad: float32 [1, 96, 384, 384], P(None, 'lat', 'lon')
- qkv_one_grad: float32 [192, 576], replicated
- proj_one_grad: float32 [192, 192], replicated
- up_one_grad: float32 [192, 768], replicated
- down_one_grad: float32 [768, 192], replicated
- merge_grad: float32 [768, 384], replicated
- qkv_two_grad: float32 [384, 1152], replicated
- proj_two_grad: float32 [384, 384], replicated
- up_two_grad: float32 [384, 1536], replicated
- down_two_grad: float32 [1536, 384], replicated
All inputs are finite; a program needn't handle non-finite values.
Results may differ from a plain program's by a relative error of at most 0.025.
Values may be sent and summed in bfloat16 or wider, within the bound.
No kernel may reach another device: no remote copies, remote signals or barrier semaphores. Data moves between devices by JAX's collectives and lax.ppermute only.
A program may use at most 256 MiB of HBM per device.

v0:
```python
import jax
import jax.numpy as jnp
from jax import lax
from jax.sharding import PartitionSpec as P

C1 = 192
C2 = 384
HEAD = 32
LEVELS = 2
WLAT = 6
WLON = 12
WINDOW = 144


EPSILON = 1e-05
MASKED = -1e30
HIGHEST = lax.Precision.HIGHEST


def padded_2(value, sides, width, wrap):
    for axis, dim in sides:
        size, length = (lax.axis_size(axis), value.shape[dim])
        up = [(i, (i + 1) % size) for i in range(size if wrap else size - 1)]
        down = [(j, i) for i, j in up]
        last = lax.slice_in_dim(value, length - width, length, axis=dim)
        first = lax.slice_in_dim(value, 0, width, axis=dim)
        before = lax.ppermute(last, axis, up)
        after = lax.ppermute(first, axis, down)
        value = jnp.concatenate([before, value, after], axis=dim)
    return value


def normalize(values):
    average = jnp.mean(values, axis=-1, keepdims=True)
    centred = values - average
    spread = jnp.mean(centred * centred, axis=-1, keepdims=True)
    return centred * lax.rsqrt(spread + EPSILON)


def product(left, right):
    return jnp.dot(left, right, preferred_element_type=jnp.float32)


def product_back(left, right):
    return lax.dot_general(
        left, right, (((1,), (1,)), ((), ())), preferred_element_type=jnp.float32
    )


def contract(left, right):
    return lax.dot_general(
        left, right, (((0,), (0,)), ((), ())), preferred_element_type=jnp.float32
    )


def offset_matrix(bias_rows):
    leading = bias_rows.shape[:-1]
    split_rows = bias_rows.reshape(leading + (LEVELS, LEVELS, WLAT, WLAT, 2 * WLON - 1))
    relative = jnp.arange(2 * WLON - 1).reshape(2 * WLON - 1, 1, 1)
    first_col = jnp.arange(WLON).reshape(1, WLON, 1)
    second_col = jnp.arange(WLON).reshape(1, 1, WLON)
    selector = (first_col - second_col + WLON - 1 == relative).astype(jnp.float32)
    spread_out = jnp.einsum("...xyabr,rpq->...xapybq", split_rows, selector, precision=HIGHEST)
    return spread_out.reshape(leading + (WINDOW, WINDOW))


def to_windows(grid):
    batch_size, row_count, col_count, level_count, feat_count = grid.shape
    lat_count = row_count // WLAT
    lon_count = col_count // WLON
    blocks = grid.reshape(batch_size, lat_count, WLAT, lon_count, WLON, level_count, feat_count)
    blocks = blocks.transpose(1, 0, 3, 5, 2, 4, 6)
    return blocks.reshape(lat_count, batch_size * lon_count, level_count * WLAT * WLON, feat_count)


def from_windows(blocks, batch_size, row_count, col_count):
    lat_count = blocks.shape[0]
    feat_count = blocks.shape[-1]
    lon_count = col_count // WLON
    grid = blocks.reshape(lat_count, batch_size, lon_count, LEVELS, WLAT, WLON, feat_count)
    grid = grid.transpose(1, 0, 4, 2, 5, 3, 6)
    return grid.reshape(batch_size, row_count, col_count, LEVELS, feat_count)


def split_heads(blocks, width):
    head_shape = blocks.shape[:-1] + (width // HEAD, HEAD)
    return (
        blocks[..., :width].reshape(head_shape),
        blocks[..., width : 2 * width].reshape(head_shape),
        blocks[..., 2 * width :].reshape(head_shape),
    )


def attend(queries, key_rows, value_rows, offsets, usable):
    factor = HEAD ** (-0.5)
    scores = (
        jnp.einsum("aoqhd,aokhd->aohqk", queries, key_rows, preferred_element_type=jnp.float32)
        * factor
        + offsets
    )
    scores = jnp.where(usable, scores, MASKED)
    chances = jax.nn.softmax(scores, axis=-1)
    weighted = jnp.einsum(
        "aohqk,aokhd->aoqhd",
        chances.astype(jnp.bfloat16),
        value_rows,
        preferred_element_type=jnp.float32,
    )
    return (weighted.astype(jnp.bfloat16), chances)


def attend_back(queries, key_rows, value_rows, chances, grad_weighted):
    factor = HEAD ** (-0.5)
    rounded = chances.astype(jnp.bfloat16)
    grad_rounded = grad_weighted.astype(jnp.bfloat16)
    grad_chances = jnp.einsum(
        "aoqhd,aokhd->aohqk", grad_rounded, value_rows, preferred_element_type=jnp.float32
    )
    grad_values = jnp.einsum(
        "aohqk,aoqhd->aokhd", rounded, grad_rounded, preferred_element_type=jnp.float32
    )
    inner = jnp.sum(grad_chances * chances, axis=-1, keepdims=True)
    grad_scores = (chances * (grad_chances - inner) * factor).astype(jnp.bfloat16)
    grad_queries = jnp.einsum(
        "aohqk,aokhd->aoqhd", grad_scores, key_rows, preferred_element_type=jnp.float32
    )
    grad_keys = jnp.einsum(
        "aohqk,aoqhd->aokhd", grad_scores, queries, preferred_element_type=jnp.float32
    )
    return (grad_queries, grad_keys, grad_values)


def extend(grid):
    wrapped = padded_2(grid, (("lon", 2),), WLON // 2, True)
    return padded_2(wrapped, (("lat", 1),), WLAT // 2, False)


def give_back(padded):
    half_lat = WLAT // 2
    rim_width = WLON // 2
    row_count = padded.shape[1] - WLAT
    col_count = padded.shape[2] - WLON
    framed = jnp.pad(padded, ((0, 0), (half_lat, half_lat), (0, 0), (0, 0)))
    arrived = padded_2(
        framed.astype(jnp.bfloat16), (("lat", 1), ("lon", 2)), rim_width, True
    ).astype(framed.dtype)
    row_sources = (
        (0, rim_width, 0),
        (2 * rim_width, row_count, 0),
        (row_count + 3 * rim_width, rim_width, row_count - rim_width),
    )
    col_sources = (
        (0, rim_width, 0),
        (2 * rim_width, col_count, 0),
        (col_count + 3 * rim_width, rim_width, col_count - rim_width),
    )
    summed = None
    for row_start, row_length, row_target in row_sources:
        for col_start, col_length, col_target in col_sources:
            portion = arrived[
                :, row_start : row_start + row_length, col_start : col_start + col_length
            ]
            widened = jnp.pad(
                portion,
                (
                    (0, 0),
                    (row_target, row_count - row_target - row_length),
                    (col_target, col_count - col_target - col_length),
                    (0, 0),
                ),
            )
            summed = widened if summed is None else summed + widened
    return summed


def level_forward(grid, weights, bias_table, width):
    qkv_weight, proj_weight, up_weight, down_weight = weights
    batch_size, row_count, col_count = grid.shape[:3]
    half_lat = WLAT // 2
    half_lon = WLON // 2
    normed = normalize(grid).astype(jnp.bfloat16)
    projected = product(normed.reshape(-1, width), qkv_weight).astype(jnp.bfloat16)
    projected = projected.reshape(grid.shape[:4] + (3 * width,))
    pairs = projected[..., width:].reshape(batch_size, row_count, col_count, LEVELS * 2 * width)
    pairs_wide = extend(pairs).reshape(
        batch_size, row_count + WLAT, col_count + WLON, LEVELS, 2 * width
    )
    queries_wide = jnp.pad(
        projected[..., :width], ((0, 0), (half_lat, half_lat), (half_lon, half_lon), (0, 0), (0, 0))
    )
    stacked = jnp.concatenate([queries_wide, pairs_wide], axis=-1)
    blocks = to_windows(stacked)
    lat_count = blocks.shape[0]
    band_index = lax.axis_index("lat")
    lat_total = row_count * lax.axis_size("lat")
    global_rows = band_index * row_count - half_lat + jnp.arange(row_count + WLAT)
    inside = ((global_rows >= 0) & (global_rows < lat_total)).reshape(lat_count, 1, WLAT, 1)
    usable = jnp.broadcast_to(inside, (lat_count, LEVELS, WLAT, WLON)).reshape(
        lat_count, 1, 1, 1, WINDOW
    )
    bias_rows = lax.dynamic_slice_in_dim(bias_table, band_index * (row_count // WLAT), lat_count, 0)
    offsets = offset_matrix(bias_rows)[:, None]
    queries, key_rows, value_rows = split_heads(blocks, width)
    weighted, chances = attend(queries, key_rows, value_rows, offsets, usable)
    attended = from_windows(
        weighted.reshape(weighted.shape[:3] + (width,)),
        batch_size,
        row_count + WLAT,
        col_count + WLON,
    )
    attended = attended[:, half_lat : half_lat + row_count, half_lon : half_lon + col_count]
    middle = grid + product(attended.reshape(-1, width), proj_weight).reshape(grid.shape)
    normed_two = normalize(middle).astype(jnp.bfloat16)
    raised = product(normed_two.reshape(-1, width), up_weight)
    activated = jax.nn.gelu(raised).astype(jnp.bfloat16)
    result = middle + product(activated, down_weight).reshape(grid.shape)
    return (result, (normed, blocks, chances, attended, middle, normed_two, raised, activated))


def level_backward(grid, saved, grad_result, weights, width):
    qkv_weight, proj_weight, up_weight, down_weight = weights
    normed, blocks, chances, attended, middle, normed_two, raised, activated = saved
    batch_size, row_count, col_count = grid.shape[:3]
    half_lat = WLAT // 2
    half_lon = WLON // 2
    grad_flat = grad_result.reshape(-1, width).astype(jnp.bfloat16)
    grad_down = contract(activated, grad_flat)
    grad_active = product_back(grad_flat, down_weight)
    grad_raised = jax.vjp(jax.nn.gelu, raised)[1](grad_active)[0].astype(jnp.bfloat16)
    grad_up = contract(normed_two.reshape(-1, width), grad_raised)
    grad_normed_two = product_back(grad_raised, up_weight).reshape(grid.shape)
    grad_middle = grad_result + jax.vjp(normalize, middle)[1](grad_normed_two)[0]
    grad_middle_flat = grad_middle.reshape(-1, width).astype(jnp.bfloat16)
    grad_proj = contract(attended.reshape(-1, width), grad_middle_flat)
    grad_attended = product_back(grad_middle_flat, proj_weight).reshape(grid.shape)
    queries, key_rows, value_rows = split_heads(blocks, width)
    grad_wide = jnp.pad(
        grad_attended, ((0, 0), (half_lat, half_lat), (half_lon, half_lon), (0, 0), (0, 0))
    )
    grad_windows = to_windows(grad_wide).reshape(queries.shape)
    grad_parts = attend_back(queries, key_rows, value_rows, chances, grad_windows)
    joined = jnp.concatenate(
        [grad_part.reshape(grad_part.shape[:3] + (width,)) for grad_part in grad_parts], axis=-1
    )
    grad_stacked = from_windows(joined, batch_size, row_count + WLAT, col_count + WLON)
    grad_pairs = give_back(
        grad_stacked[..., width:].reshape(
            batch_size, row_count + WLAT, col_count + WLON, LEVELS * 2 * width
        )
    )
    grad_pairs = grad_pairs.reshape(batch_size, row_count, col_count, LEVELS, 2 * width)
    grad_queries_own = grad_stacked[
        :, half_lat : half_lat + row_count, half_lon : half_lon + col_count, :, :width
    ]
    grad_projected = (
        jnp.concatenate([grad_queries_own, grad_pairs], axis=-1)
        .astype(jnp.bfloat16)
        .reshape(-1, 3 * width)
    )
    grad_qkv = contract(normed.reshape(-1, width), grad_projected)
    grad_normed = product_back(grad_projected, qkv_weight).reshape(grid.shape)
    grad_grid = grad_middle + jax.vjp(normalize, grid)[1](grad_normed)[0]
    return (grad_grid, (grad_qkv, grad_proj, grad_up, grad_down))


def merge_forward(grid, merge_weight):
    batch_size, row_count, col_count = grid.shape[:3]
    grouped = grid.reshape(batch_size, row_count // 2, 2, col_count // 2, 2, LEVELS, -1)
    grouped = grouped.transpose(0, 1, 3, 5, 2, 4, 6).reshape(
        batch_size, row_count // 2, col_count // 2, LEVELS, -1
    )
    merged_norm = normalize(grouped).astype(jnp.bfloat16)
    merged = product(merged_norm.reshape(-1, merge_weight.shape[0]), merge_weight)
    return (merged.reshape(grouped.shape[:4] + (merge_weight.shape[1],)), grouped, merged_norm)


def merge_backward(grouped, merged_norm, grad_merged, merge_weight):
    grad_flat = grad_merged.reshape(-1, merge_weight.shape[1]).astype(jnp.bfloat16)
    grad_weight = contract(merged_norm.reshape(-1, merge_weight.shape[0]), grad_flat)
    grad_norm = product_back(grad_flat, merge_weight).reshape(grouped.shape)
    grad_grouped = jax.vjp(normalize, grouped)[1](grad_norm)[0]
    batch_size, half_rows, half_cols = grouped.shape[:3]
    regrid = grad_grouped.reshape(batch_size, half_rows, half_cols, LEVELS, 2, 2, -1)
    regrid = regrid.transpose(0, 1, 4, 2, 5, 3, 6)
    return (regrid.reshape(batch_size, 2 * half_rows, 2 * half_cols, LEVELS, -1), grad_weight)


def sum_upper(grad_merge, grads_two):
    return lax.psum(
        (grad_merge, grads_two[0], grads_two[1], grads_two[2], grads_two[3]), ("lat", "lon")
    )


def per_device(
    tokens,
    cotangent,
    bias_one,
    qkv_one,
    proj_one,
    up_one,
    down_one,
    merge_weight,
    bias_two,
    qkv_two,
    proj_two,
    up_two,
    down_two,
):
    batch_size, row_count, col_count = tokens.shape[:3]
    weights_one = (qkv_one, proj_one, up_one, down_one)
    weights_two = (qkv_two, proj_two, up_two, down_two)
    grid_one = tokens.astype(jnp.float32).reshape(batch_size, row_count, col_count, LEVELS, C1)
    out_one, saved_one = level_forward(grid_one, weights_one, bias_one, C1)
    grid_two, grouped, merged_norm = merge_forward(out_one, merge_weight)
    out_two, saved_two = level_forward(grid_two, weights_two, bias_two, C2)
    grad_two = cotangent.astype(jnp.float32).reshape(out_two.shape)
    grad_grid_two, grads_two = level_backward(grid_two, saved_two, grad_two, weights_two, C2)
    grad_out_one, grad_merge = merge_backward(grouped, merged_norm, grad_grid_two, merge_weight)
    grad_grid_one, grads_one = level_backward(grid_one, saved_one, grad_out_one, weights_one, C1)
    upper = sum_upper(grad_merge, grads_two)
    lower = lax.psum((grads_one[0], grads_one[1], grads_one[2], grads_one[3]), ("lat", "lon"))
    cell_count = (
        batch_size
        * (row_count // 2)
        * (col_count // 2)
        * LEVELS
        * lax.axis_size("lat")
        * lax.axis_size("lon")
    )
    factor = cell_count ** (-0.5)
    return (
        out_two.reshape(batch_size, row_count // 2, col_count // 2, LEVELS * C2),
        grad_grid_one.reshape(batch_size, row_count, col_count, LEVELS * C1),
        lower[0] * factor,
        lower[1] * factor,
        lower[2] * factor,
        lower[3] * factor,
        upper[0] * factor,
        upper[1] * factor,
        upper[2] * factor,
        upper[3] * factor,
        upper[4] * factor,
    )


def solution(mesh):
    return jax.shard_map(
        per_device,
        mesh=mesh,
        in_specs=(
            P(None, "lat", "lon", None),
            P(None, "lat", "lon", None),
            P(),
            P(),
            P(),
            P(),
            P(),
            P(),
            P(),
            P(),
            P(),
            P(),
            P(),
        ),
        out_specs=(
            P(None, "lat", "lon", None),
            P(None, "lat", "lon", None),
            P(),
            P(),
            P(),
            P(),
            P(),
            P(),
            P(),
            P(),
            P(),
        ),
        check_vma=False,
    )
```

profile of v0, /device:TPU:1, one launch (start us, length us, event | category | flops | bytes accessed | tf_op | source)
XLA Modules:
  0.0 773.5 jit_solution(13151702641760611288)
XLA Ops:
  19.7 2.8 reshape.929
  25.4 2.6 collective-permute-start
  28.3 3.1 reshape.979
  31.4 46.5 %convolution_bitcast_fusion = f32[2,12,2,6,12,2,6,12]{1,7,6,3,5,2,0,4:T(8,128)} fusion(f32[2,12,2,2,6,6,23]{6,5,4,3,2,1,0:T(8,128)} %reshape.979, s32[12,12]{1,0:T(8,128)S(1)} %subtract_add_fusion), kind=kOutput, calls=%fused_computation.4 | convolution fusion | flops 137358576 | bytes 2309184 | tf_op jit(solution)/shard_map/...xyabr,rpq->...xapybq/dot_general | solution.py:63
  81.6 5.5 collective-permute-start.2
  88.8 12.0 %convolution_bitcast_fusion.1 = f32[3,6,2,6,12,2,6,12]{7,6,3,5,2,1,0,4:T(8,128)} fusion(f32[3,6,2,2,6,6,23,1]{6,5,4,3,2,1,0,7:T(8,128)S(1)} %reshape.969, s32[12,12]{1,0:T(8,128)S(1)} %subtract_add_fusion), kind=kOutput, calls=%fused_computation.5 | convolution fusion | flops 103019760 | bytes 1732032 | tf_op jit(solution)/shard_map/...xyabr,rpq->...xapybq/dot_general | solution.py:63
  102.3 30.0 %copy.546 = f32[3,6,2,6,12,2,6,12]{4,3,2,7,6,5,1,0:T(8,128)} copy(f32[3,6,2,6,12,2,6,12]{7,6,3,5,2,1,0,4:T(8,128)} %convolution_bitcast_fusion.1) | data formatting | bytes 2985984 | tf_op jit(solution)/shard_map/add | solution.py:97
  132.3 14.9 %reshape.978 = f32[3,6,144,144]{2,3,1,0:T(8,128)} reshape(f32[3,6,2,6,12,2,6,12]{4,3,2,7,6,5,1,0:T(8,128)} %copy.546) | data formatting | bytes 2985984 | tf_op jit(solution)/shard_map/add | solution.py:97
  147.3 41.5 %copy.549 = f32[2,12,2,6,12,2,6,12]{4,3,2,7,6,5,1,0:T(8,128)} copy(f32[2,12,2,6,12,2,6,12]{1,7,6,3,5,2,0,4:T(8,128)} %convolution_bitcast_fusion) | data formatting | bytes 3981312 | tf_op jit(solution)/shard_map/add | solution.py:97
  188.8 19.6 %reshape.980 = f32[2,12,144,144]{2,3,1,0:T(8,128)} reshape(f32[2,12,2,6,12,2,6,12]{4,3,2,7,6,5,1,0:T(8,128)} %copy.549) | data formatting | bytes 3981312 | tf_op jit(solution)/shard_map/add | solution.py:97
  211.3 3.5 maximum_bitcast_fusion.2
  216.6 3.3 reshape.931
  222.7 2.7 copy.438
  225.8 9.4 %fusion.197 = (f32[3,3,6,144]{3,2,1,0:T(8,128)S(1)}, f32[3,3,6,144,144]{3,4,2,1,0:T(8,128)}) fusion(f32[3,6,144,144]{2,3,1,0:T(8,128)} %reshape.978, pred[3,144]{1,0:T(4,128)(4,1)S(1)} %broadcast_in_dim.59, bf16[3,3,144,6,32]{2,4,3,1,0:T(8,128)(2,1)S(1)} %bitcast.238, bf16[3,3,144,6,32]{2,4,3,1,0:T(8,128)(2,1)} %bitcast.240), kind=kOutput, calls=%fused_computation.310 | convolution fusion | flops 77262480 | bytes 6998832 | tf_op jit(solution)/shard_map/sub | solution.py:102
  235.2 4.0 fusion.79
  239.2 2.7 copy.442
  241.9 3.8 reshape_reshape.4
  265.3 5.8 collective-permute-start.6
  275.1 4.6 collective-permute-done.7
  293.1 8.7 %fusion.200 = (f32[2,2,12,144]{3,2,1,0:T(8,128)S(1)}, f32[2,2,12,144,144]{3,4,2,1,0:T(8,128)}) fusion(bf16[2,2,144,12,32]{2,4,3,1,0:T(8,128)(2,1)} %bitcast.242, bf16[2,2,144,12,32]{2,4,3,1,0:T(8,128)(2,1)} %bitcast.244, f32[2,12,144,144]{2,3,1,0:T(8,128)} %reshape.980, pred[2,144]{1,0:T(4,128)(4,1)S(1)} %copy-done.114), kind=kOutput, calls=%fused_computation.313 | convolution fusion | flops 68677776 | bytes 6884640 | tf_op jit(solution)/shard_map/sub | solution.py:102
  301.8 4.7 fusion.82
  306.5 5.1 copy.464
  311.6 4.4 reshape_reshape.5
  318.3 3.3 fusion.93
  324.7 2.6 convert_element_type.236
  327.4 4.3 copy.476
  331.6 5.2 fusion.205
  336.8 12.6 %fusion.67 = bf16[2,2,144,12,32]{2,4,3,1,0:T(8,128)(2,1)} fusion(bf16[2,2,144,12,32]{2,4,3,1,0:T(8,128)(2,1)} %bitcast.245, f32[2,2,12,144,144]{3,4,2,1,0:T(8,128)} %fusion.205, f32[2,2,12,144,144]{3,4,2,1,0:T(8,128)} %get-tuple-element.134, f32[2,2,12,144]{3,2,1,0:T(8,128)S(1)} %copy-done.116), kind=kOutput, calls=%fused_computation.68 | convolution fusion | flops 70675344 | bytes 8875008 | tf_op jit(solution)/shard_map/aohqk,aokhd->aoqhd/dot_general | solution.py:124
  349.4 12.3 %fusion.70 = bf16[2,2,144,12,32]{2,4,3,1,0:T(8,128)(2,1)} fusion(bf16[2,2,144,12,32]{2,4,3,1,0:T(8,128)(2,1)} %bitcast.243, f32[2,2,12,144,144]{3,4,2,1,0:T(8,128)} %fusion.205, f32[2,2,12,144,144]{3,4,2,1,0:T(8,128)} %get-tuple-element.134, f32[2,2,12,144]{3,2,1,0:T(8,128)S(1)} %copy-done.116), kind=kOutput, calls=%fused_computation.69 | convolution fusion | flops 70675344 | bytes 8875008 | tf_op jit(solution)/shard_map/aohqk,aoqhd->aokhd/dot_general | solution.py:127
  361.7 5.1 fusion.64
  366.8 5.1 copy.478
  371.9 3.6 concatenate.128
  375.5 5.1 copy.480
  380.7 4.7 concatenate.129
  385.4 4.1 copy.483
  389.5 4.3 concatenate.130
  393.8 2.8 maximum_bitcast_fusion.1
  400.3 2.6 reshape.957
  406.2 2.8 collective-permute-start.9
  412.0 3.0 fusion.211
  415.0 14.2 %collective-permute-done.9 = bf16[1,6,24,1536]{3,2,1,0:T(8,128)(2,1)} collective-permute-done((bf16[1,6,24,1536]{3,2,1,0:T(8,128)(2,1)}, bf16[1,6,24,1536]{3,2,1,0:T(8,128)(2,1)}, u32[]{:S(2)}, u32[]{:S(2)}) %collective-permute-start.9) | collective-permute-done | bytes 442400 | tf_op jit(solution)/shard_map/ppermute | solution.py:28
  431.4 3.8 collective-permute-start.10
  466.7 2.8 fusion.189
  471.4 2.8 fusion.50
  479.5 2.6 convert_element_type.247
  482.2 3.2 copy.509
  485.4 4.4 fusion.207
  489.8 13.6 %fusion.55 = bf16[3,3,144,6,32]{2,4,3,1,0:T(8,128)(2,1)} fusion(bf16[3,3,144,6,32]{2,4,3,1,0:T(8,128)(2,1)S(1)} %bitcast.241, f32[3,3,6,144,144]{3,4,2,1,0:T(8,128)} %fusion.207, f32[3,3,6,144,144]{3,4,2,1,0:T(8,128)} %get-tuple-element.126, f32[3,3,6,144]{3,2,1,0:T(8,128)S(1)} %copy-done.118), kind=kOutput, calls=%fused_computation.64 | convolution fusion | flops 79509744 | bytes 9984384 | tf_op jit(solution)/shard_map/aohqk,aokhd->aoqhd/dot_general | solution.py:124
  503.4 12.6 %fusion.58 = bf16[3,3,144,6,32]{2,4,3,1,0:T(8,128)(2,1)} fusion(bf16[3,3,144,6,32]{2,4,3,1,0:T(8,128)(2,1)S(1)} %bitcast.239, f32[3,3,6,144,144]{3,4,2,1,0:T(8,128)} %fusion.207, f32[3,3,6,144,144]{3,4,2,1,0:T(8,128)} %get-tuple-element.126, f32[3,3,6,144]{3,2,1,0:T(8,128)S(1)} %copy-done.118), kind=kOutput, calls=%fused_computation.65 | convolution fusion | flops 79509744 | bytes 9984384 | tf_op jit(solution)/shard_map/aohqk,aoqhd->aokhd/dot_general | solution.py:127
  516.0 4.7 fusion.61
  522.4 2.7 copy.511
  525.1 3.6 concatenate.137
  528.7 2.7 copy.513
  531.5 3.5 concatenate.138
  535.0 2.7 copy.516
  537.8 3.5 concatenate.139
  543.5 2.8 slice.236
  549.8 4.2 collective-permute-start.13
  564.9 3.7 collective-permute-done.13
  568.8 3.2 collective-permute-start.14
  573.9 3.4 collective-permute-done.14
  577.3 2.8 collective-permute-done.15
  593.0 160.9 %all-reduce.23.cloned.1.call-done = (f32[192,576]{1,0:T(8,128)}, f32[192,192]{1,0:T(8,128)}, f32[192,768]{1,0:T(8,128)}, f32[768,192]{0,1:T(8,128)}, f32[768,384...) async-done(((f32[192,576]{1,0:T(8,128)}, f32[192,192]{1,0:T(8,128)}, f32[192,768]{1,0:T(8,128)}, ...) | async-done | bytes 10027024 | tf_op jit(solution)/shard_map/psum | solution.py:321
  753.9 3.4 broadcast_multiply_fusion
  (486 shorter events, 164.3 us)
Async XLA Ops:
  7.2 21.0 %copy-start = (f32[9,12,3312]{2,1,0:T(8,128)S(1)}, f32[9,12,3312]{2,1,0:T(8,128)}, u32[]{:S(2)}) copy-start(f32[9,12,3312]{2,1,0:T(8,128)} %param.21) | copy-start | bytes 4292356
  7.2 746.7 %all-reduce.23.cloned.1.call-start = ((), (), s32[]{:S(2)}) async-start(), calls=%async_computation | async-start | bytes 20250624 | tf_op jit(solution)/shard_map/psum | solution.py:321
  8.8 237.8 %copy-start.2 = (f32[12,24,2,192]{3,2,1,0:T(2,128)}, f32[12,24,2,192]{3,2,1,0:T(2,128)S(1)}, u32[]{:S(2)}) copy-start(f32[12,24,2,192]{3,2,1,0:T(2,128)S(1)} %reshape.926) | copy-start | bytes 1327108
  13.6 6.1 copy-start.96
  17.3 5.2 copy-start.14
  25.4 54.7 %collective-permute-start = (bf16[1,12,6,768]{3,2,1,0:T(8,128)(2,1)}, bf16[1,12,6,768]{3,2,1,0:T(8,128)(2,1)S(1)}, u32[]{:S(2)}, u32[]{:S(2)}) collective-permute-start(bf16[1,12,6,768]{3,2,1,0:T(8,128)(2,1)} %get-tuple-element.111), channel_id=1, source_target_pairs={{0,1},{1,2},{2,3},{3,4},{4,5},{5,6},{6,7},{7,8},{8,9},{9,10},{10,1... | collective-permute-start | bytes 331784 | tf_op jit(solution)/shard_map/ppermute | solution.py:27
  28.0 52.1 %collective-permute-start.1 = (bf16[1,12,6,768]{3,2,1,0:T(8,128)(2,1)}, bf16[1,12,6,768]{3,2,1,0:T(8,128)(2,1)}, u32[]{:S(2)}, u32[]{:S(2)}) collective-permute-start(bf16[1,12,6,768]{3,2,1,0:T(8,128)(2,1)} %get-tuple-element.112), channel_id=1, source_target_pairs={{1,0},{2,1},{3,2},{4,3},{5,4},{6,5},{7,6},{8,7},{9,8},{10,9},{11,1... | collective-permute-start | bytes 331784 | tf_op jit(solution)/shard_map/ppermute | solution.py:28
  81.6 128.0 %collective-permute-start.2 = (bf16[1,3,36,768]{3,2,1,0:T(8,128)(2,1)}, bf16[1,3,36,768]{3,2,1,0:T(8,128)(2,1)S(1)}, u32[]{:S(2)}, u32[]{:S(2)}) collective-permute-start(bf16[1,3,36,768]{3,2,1,0:T(8,128)(2,1)} %get-tuple-element.106), channel_id=1, source_target_pairs={{0,16},{16,32},{32,48},{48,64},{64,80},{80,96},{96,112},{1,17},{17... | collective-permute-start | bytes 497672 | tf_op jit(solution)/shard_map/ppermute | solution.py:27
  87.1 13.7 %copy-start.64 = (bf16[1,6,12,768]{3,2,1,0:T(8,128)(2,1)S(1)}, bf16[1,6,12,768]{3,2,1,0:T(8,128)(2,1)}, u32[]{:S(2)}) copy-start(bf16[1,6,12,768]{3,2,1,0:T(8,128)(2,1)} %param.14) | copy-start | bytes 331780
  87.2 122.5 %collective-permute-start.3 = (bf16[1,3,36,768]{3,2,1,0:T(8,128)(2,1)S(1)}, bf16[1,3,36,768]{3,2,1,0:T(8,128)(2,1)}, u32[]{:S(2)}, u32[]{:S(2)}) collective-permute-start(bf16[1,3,36,768]{3,2,1,0:T(8,128)(2,1)S(1)} %get-tuple-element.107), channel_id=1, source_target_pairs={{16,0},{32,16},{48,32},{64,48},{80,64},{96,80},{112,96},{17,1},{33... | collective-permute-start | bytes 497672 | tf_op jit(solution)/shard_map/ppermute | solution.py:28
  188.8 19.6 %slice-start = ((bf16[1,12,24,2,576]{4,3,2,1,0:T(2,128)(2,1)}), bf16[1,12,24,2,192]{4,3,2,1,0:T(2,128)(2,1)S(1)}, s32[]{:S(2)}) async-start(bf16[1,12,24,2,576]{4,3,2,1,0:T(2,128)(2,1)} %reshape.929), calls=%async_computation.1 | async-start | bytes 589824 | tf_op jit(solution)/shard_map/slice | solution.py:189
  222.7 12.5 %copy-start.49 = (bf16[3,3,144,192]{2,3,1,0:T(8,128)(2,1)}, bf16[3,3,144,192]{2,3,1,0:T(8,128)(2,1)S(1)}, u32[]{:S(2)}) copy-start(bf16[3,3,144,192]{2,3,1,0:T(8,128)(2,1)S(1)} %copy.437) | copy-start | bytes 1492996
  225.8 9.4 %copy-start.17 = (bf16[3,3,144,192]{2,3,1,0:T(8,128)(2,1)}, bf16[3,3,144,192]{2,3,1,0:T(8,128)(2,1)S(1)}, u32[]{:S(2)}) copy-start(bf16[3,3,144,192]{2,3,1,0:T(8,128)(2,1)S(1)} %copy.436) | copy-start | bytes 1492996
  241.9 4.7 copy-start.67
  251.7 5.1 copy-start.23
  257.2 15.2 %copy-start.45 = (bf16[144,384]{1,0:T(8,128)(2,1)S(1)}, bf16[144,384]{1,0:T(8,128)(2,1)}, u32[]{:S(2)}) copy-start(bf16[144,384]{1,0:T(8,128)(2,1)} %convert_element_type.231) | copy-start | bytes 331780
  257.8 4.2 collective-permute-start.4
  259.8 4.6 collective-permute-start.5
  261.6 10.8 %copy-start.38 = (bf16[1536,384]{1,0:T(8,128)(2,1)S(1)}, bf16[1536,384]{1,0:T(8,128)(2,1)}, u32[]{:S(2)}) copy-start(bf16[1536,384]{1,0:T(8,128)(2,1)} %param.25) | copy-start | bytes 3538948
  265.3 9.0 %collective-permute-start.6 = (bf16[1,3,24,1536]{3,2,1,0:T(8,128)(2,1)}, bf16[1,3,24,1536]{3,2,1,0:T(8,128)(2,1)S(1)}, u32[]{:S(2)}, u32[]{:S(2)}) collective-permute-start(bf16[1,3,24,1536]{3,2,1,0:T(8,128)(2,1)} %get-tuple-element.109), channel_id=1, source_target_pairs={{0,16},{16,32},{32,48},{48,64},{64,80},{80,96},{96,112},{1,17},{17... | collective-permute-start | bytes 663560 | tf_op jit(solution)/shard_map/ppermute | solution.py:27
  271.1 8.5 %collective-permute-start.7 = (bf16[1,3,24,1536]{3,2,1,0:T(8,128)(2,1)}, bf16[1,3,24,1536]{3,2,1,0:T(8,128)(2,1)}, u32[]{:S(2)}, u32[]{:S(2)}) collective-permute-start(bf16[1,3,24,1536]{3,2,1,0:T(8,128)(2,1)} %get-tuple-element.110), channel_id=1, source_target_pairs={{16,0},{32,16},{48,32},{64,48},{80,64},{96,80},{112,96},{17,1},{33... | collective-permute-start | bytes 663560 | tf_op jit(solution)/shard_map/ppermute | solution.py:28
  274.1 43.3 %copy-start.25 = (f32[6,12,2,384]{3,2,1,0:T(2,128)}, f32[6,12,2,384]{3,2,1,0:T(2,128)S(1)}, u32[]{:S(2)}) copy-start(f32[6,12,2,384]{3,2,1,0:T(2,128)S(1)} %reshape.941) | copy-start | bytes 663556
  287.2 5.9 copy-start.114
  311.6 5.8 copy-start.41
  317.8 5.7 copy-start.69
  318.0 5.5 copy-start.80
  331.6 5.2 copy-start.116
  349.4 12.3 %copy-start.24 = (bf16[2,2,144,12,32]{2,4,3,1,0:T(8,128)(2,1)S(1)}, bf16[2,2,144,12,32]{2,4,3,1,0:T(8,128)(2,1)}, u32[]{:S(2)}) copy-start(bf16[2,2,144,12,32]{2,4,3,1,0:T(8,128)(2,1)} %copy.476) | copy-start | bytes 1327108
  375.5 9.9 %copy-start.56 = (bf16[2,2,144,12,32]{2,4,3,1,0:T(8,128)(2,1)S(1)}, bf16[2,2,144,12,32]{2,4,3,1,0:T(8,128)(2,1)}, u32[]{:S(2)}) copy-start(bf16[2,2,144,12,32]{2,4,3,1,0:T(8,128)(2,1)} %fusion.64) | copy-start | bytes 1327108
  398.7 10.4 %copy-start.113 = (f32[144]{0:T(256)S(1)}, f32[144]{0:T(256)}, u32[]{:S(2)}) copy-start(f32[144]{0:T(256)} %get-tuple-element.123) | copy-start | bytes 1732
  402.9 7.1 copy-start.4
  403.9 11.1 %collective-permute-start.8 = (bf16[1,6,24,1536]{3,2,1,0:T(8,128)(2,1)}, bf16[1,6,24,1536]{3,2,1,0:T(8,128)(2,1)S(1)}, u32[]{:S(2)}, u32[]{:S(2)}) collective-permute-start(bf16[1,6,24,1536]{3,2,1,0:T(8,128)(2,1)} %get-tuple-element.104), channel_id=1, source_target_pairs={{0,16},{16,32},{32,48},{48,64},{64,80},{80,96},{96,112},{112,0},{1... | collective-permute-start | bytes 1327112 | tf_op jit(solution)/shard_map/ppermute | solution.py:27
  406.2 23.1 %collective-permute-start.9 = (bf16[1,6,24,1536]{3,2,1,0:T(8,128)(2,1)}, bf16[1,6,24,1536]{3,2,1,0:T(8,128)(2,1)}, u32[]{:S(2)}, u32[]{:S(2)}) collective-permute-start(bf16[1,6,24,1536]{3,2,1,0:T(8,128)(2,1)} %get-tuple-element.105), channel_id=1, source_target_pairs={{16,0},{32,16},{48,32},{64,48},{80,64},{96,80},{112,96},{0,112},{1... | collective-permute-start | bytes 1327112 | tf_op jit(solution)/shard_map/ppermute | solution.py:28
  414.9 21.2 %copy-start.39 = (bf16[1536,384]{1,0:T(8,128)(2,1)S(1)}, bf16[1536,384]{1,0:T(8,128)(2,1)}, u32[]{:S(2)}) copy-start(bf16[1536,384]{1,0:T(8,128)(2,1)} %param.25) | copy-start | bytes 3538948
  414.9 21.2 %copy-start.52 = (f32[144,1536]{1,0:T(8,128)S(1)}, f32[144,1536]{1,0:T(8,128)}, u32[]{:S(2)}) copy-start(f32[144,1536]{1,0:T(8,128)} %get-tuple-element.138) | copy-start | bytes 2654212
  431.4 15.9 %collective-permute-start.10 = (bf16[1,30,6,1536]{3,1,2,0:T(8,128)(2,1)}, bf16[1,30,6,1536]{3,1,2,0:T(8,128)(2,1)}, u32[]{:S(2)}, u32[]{:S(2)}) collective-permute-start(bf16[1,30,6,1536]{3,1,2,0:T(8,128)(2,1)} %copy.487), channel_id=1, source_target_pairs={{0,1},{1,2},{2,3},{3,4},{4,5},{5,6},{6,7},{7,8},{8,9},{9,10},{10,1... | collective-permute-start | bytes 1658888 | tf_op jit(solution)/shard_map/ppermute | solution.py:27
  436.2 12.5 %collective-permute-start.11 = (bf16[1,30,6,1536]{3,1,2,0:T(8,128)(2,1)}, bf16[1,30,6,1536]{3,1,2,0:T(8,128)(2,1)}, u32[]{:S(2)}, u32[]{:S(2)}) collective-permute-start(bf16[1,30,6,1536]{3,1,2,0:T(8,128)(2,1)} %copy.488), channel_id=1, source_target_pairs={{1,0},{2,1},{3,2},{4,3},{5,4},{6,5},{7,6},{8,7},{9,8},{10,9},{11,1... | collective-permute-start | bytes 1658888 | tf_op jit(solution)/shard_map/ppermute | solution.py:28
  452.6 8.4 %copy-start.8 = (f32[6,12,2,384]{3,2,1,0:T(2,128)S(1)}, f32[6,12,2,384]{3,2,1,0:T(2,128)}, u32[]{:S(2)}) copy-start(f32[6,12,2,384]{3,2,1,0:T(2,128)} %copy-done.7) | copy-start | bytes 663556
  452.6 8.4 %copy-start.26 = (f32[6,12,2,384]{3,2,1,0:T(2,128)S(1)}, f32[6,12,2,384]{3,2,1,0:T(2,128)}, u32[]{:S(2)}) copy-start(f32[6,12,2,384]{3,2,1,0:T(2,128)} %copy-done.25) | copy-start | bytes 663556
  452.6 8.4 %copy-start.31 = (f32[6,12,2,384]{3,2,1,0:T(2,128)S(1)}, f32[6,12,2,384]{3,2,1,0:T(2,128)}, u32[]{:S(2)}) copy-start(f32[6,12,2,384]{3,2,1,0:T(2,128)} %reshape.967) | copy-start | bytes 663556
  452.6 8.4 %copy-start.55 = (f32[6,12,2,384]{3,2,1,0:T(2,128)S(1)}, f32[6,12,2,384]{3,2,1,0:T(2,128)}, u32[]{:S(2)}) copy-start(f32[6,12,2,384]{3,2,1,0:T(2,128)} %reshape.951) | copy-start | bytes 663556
  452.6 8.4 %copy-start.70 = (f32[6,12,2]{1,2,0:T(2,128)S(1)}, f32[6,12,2]{1,2,0:T(2,128)}, u32[]{:S(2)}) copy-start(f32[6,12,2]{1,2,0:T(2,128)} %copy-done.69) | copy-start | bytes 1732
  452.6 8.4 %copy-start.81 = (f32[6,12,2]{1,2,0:T(2,128)S(1)}, f32[6,12,2]{1,2,0:T(2,128)}, u32[]{:S(2)}) copy-start(f32[6,12,2]{1,2,0:T(2,128)} %copy-done.80) | copy-start | bytes 1732
  452.6 8.4 %copy-start.92 = (f32[6,12,2]{1,2,0:T(2,128)S(1)}, f32[6,12,2]{1,2,0:T(2,128)}, u32[]{:S(2)}) copy-start(f32[6,12,2]{1,2,0:T(2,128)} %copy-done.91) | copy-start | bytes 1732
  453.8 9.1 %copy-start.6 = (f32[144,768]{1,0:T(8,128)S(1)}, f32[144,768]{1,0:T(8,128)}, u32[]{:S(2)}) copy-start(f32[144,768]{1,0:T(8,128)} %copy-done.5) | copy-start | bytes 1327108
  461.0 4.9 copy-start.103
  461.1 5.0 copy-start.94
  461.1 5.2 copy-start.106
  489.8 13.6 %copy-start.50 = (bf16[3,3,144,192]{2,3,1,0:T(8,128)(2,1)S(1)}, bf16[3,3,144,192]{2,3,1,0:T(8,128)(2,1)}, u32[]{:S(2)}) copy-start(bf16[3,3,144,192]{2,3,1,0:T(8,128)(2,1)} %copy-done.49) | copy-start | bytes 1492996
  516.0 4.7 copy-start.34
  543.5 5.4 copy-start.13
  548.9 16.0 %collective-permute-start.12 = (bf16[1,6,36,768]{3,2,1,0:T(8,128)(2,1)}, bf16[1,6,36,768]{3,2,1,0:T(8,128)(2,1)S(1)}, u32[]{:S(2)}, u32[]{:S(2)}) collective-permute-start(bf16[1,6,36,768]{3,2,1,0:T(8,128)(2,1)} %get-tuple-element.102), channel_id=1, source_target_pairs={{0,16},{16,32},{32,48},{48,64},{64,80},{80,96},{96,112},{112,0},{1... | collective-permute-start | bytes 995336 | tf_op jit(solution)/shard_map/ppermute | solution.py:27
  549.8 18.8 %collective-permute-start.13 = (bf16[1,6,36,768]{3,2,1,0:T(8,128)(2,1)}, bf16[1,6,36,768]{3,2,1,0:T(8,128)(2,1)S(1)}, u32[]{:S(2)}, u32[]{:S(2)}) collective-permute-start(bf16[1,6,36,768]{3,2,1,0:T(8,128)(2,1)} %get-tuple-element.103), channel_id=1, source_target_pairs={{16,0},{32,16},{48,32},{64,48},{80,64},{96,80},{112,96},{0,112},{1... | collective-permute-start | bytes 995336 | tf_op jit(solution)/shard_map/ppermute | solution.py:28
  557.8 5.7 copy-start.22
  557.8 5.7 copy-start.37
  563.6 8.5 %copy-start.27 = (f32[6,12,2,384]{3,2,1,0:T(2,128)S(1)}, f32[6,12,2,384]{3,2,1,0:T(2,128)}, u32[]{:S(2)}) copy-start(f32[6,12,2,384]{3,2,1,0:T(2,128)} %copy-done.25) | copy-start | bytes 663556
  563.6 8.5 %copy-start.77 = (bf16[6,12,2,768]{3,1,2,0:T(8,128)(2,1)S(1)}, bf16[6,12,2,768]{3,1,2,0:T(8,128)(2,1)}, u32[]{:S(2)}) copy-start(bf16[6,12,2,768]{3,1,2,0:T(8,128)(2,1)} %copy.527) | copy-start | bytes 663556
  563.6 8.5 %copy-start.82 = (bf16[1,6,12,2,384]{4,2,3,1,0:T(8,128)(2,1)S(1)}, bf16[1,6,12,2,384]{4,2,3,1,0:T(8,128)(2,1)}, u32[]{:S(2)}) copy-start(bf16[1,6,12,2,384]{4,2,3,1,0:T(8,128)(2,1)} %copy.642) | copy-start | bytes 331780
  563.6 8.5 %copy-start.102 = (f32[6,12,2]{1,2,0:T(2,128)S(1)}, f32[6,12,2]{1,2,0:T(2,128)}, u32[]{:S(2)}) copy-start(f32[6,12,2]{1,2,0:T(2,128)} %copy.493) | copy-start | bytes 1732
  563.6 8.5 %copy-start.104 = (f32[6,12,2]{1,2,0:T(2,128)S(1)}, f32[6,12,2]{1,2,0:T(2,128)}, u32[]{:S(2)}) copy-start(f32[6,12,2]{1,2,0:T(2,128)} %copy-done.103) | copy-start | bytes 1732
  568.8 8.5 %collective-permute-start.14 = (bf16[1,36,6,768]{3,2,1,0:T(8,128)(2,1)S(1)}, bf16[1,36,6,768]{3,2,1,0:T(8,128)(2,1)S(1)}, u32[]{:S(2)}, u32[]{:S(2)}) collective-permute-start(bf16[1,36,6,768]{3,2,1,0:T(8,128)(2,1)S(1)} %get-tuple-element.92), channel_id=1, source_target_pairs={{0,1},{1,2},{2,3},{3,4},{4,5},{5,6},{6,7},{7,8},{8,9},{9,10},{10,1... | collective-permute-start | bytes 995336 | tf_op jit(solution)/shard_map/ppermute | solution.py:27
  572.0 8.0 %collective-permute-start.15 = (bf16[1,36,6,768]{3,2,1,0:T(8,128)(2,1)S(1)}, bf16[1,36,6,768]{3,2,1,0:T(8,128)(2,1)S(1)}, u32[]{:S(2)}, u32[]{:S(2)}) collective-permute-start(bf16[1,36,6,768]{3,2,1,0:T(8,128)(2,1)S(1)} %get-tuple-element.93), channel_id=1, source_target_pairs={{1,0},{2,1},{3,2},{4,3},{5,4},{6,5},{7,6},{8,7},{9,8},{10,9},{11,1... | collective-permute-start | bytes 995336 | tf_op jit(solution)/shard_map/ppermute | solution.py:28
  585.8 5.2 copy-start.10
  585.8 5.2 copy-start.12
  (73 other events, 169.8 us)
Sparse Core Ops, SparseCore 0:
  585.9 167.9 all-reduce.22
where the time goes:
time: 783 us; the launch traced here: 773 us
  local copies, waits for them, and re-layouts  286 us (37%)
  matrix products  196 us (25%)
  waiting for transfers between devices  192 us (25%)
  other arithmetic  44.7 us (6%)
  starting transfers between devices  37.4 us (5%)
  between operations  16.6 us (2%)
    psum x1, waiting for transfers between devices, per_device(): lax.psum((grads_one[0], grads_one[1], grads_one[2], grads_one[3]), ('lat'...  161 us
    add x4, local copies, waits for them, and re-layouts, attend(): jnp.einsum('aoqhd,aokhd->aohqk', queries, key_rows, preferred_element_typ...  106 us
    dot_general x2, matrix products, offset_matrix(): jnp.einsum('...xyabr,rpq->...xapybq', split_rows, selector, precision=HIG...  58.5 us
    ppermute x8, waiting for transfers between devices, padded_2(): after = lax.ppermute(first, axis, down)  27.8 us
    dot_general x2, matrix products, attend_back(): jnp.einsum('aohqk,aokhd->aoqhd', grad_scores, key_rows, preferred_element...  26.2 us
    ppermute x8, starting transfers between devices, padded_2(): before = lax.ppermute(last, axis, up)  26.1 us
    dot_general x2, matrix products, attend_back(): jnp.einsum('aohqk,aoqhd->aokhd', grad_scores, queries, preferred_element_...  24.9 us
    concatenate x6, local copies, waits for them, and re-layouts, level_backward(): jnp.concatenate([grad_part.reshape(grad_part.shape[:3] + (width,)) for gr...  23.3 us
  transfers between devices with their start and end apart: 17, of which 8 were waited for; matrix products, arithmetic and copies ran while one was open for 28% of the time, Pallas kernels for 0%

commit v1 on v0

v1 whole, which is shorter than its diff:
```python
import functools

import jax
import jax.numpy as jnp
import numpy as np
from jax import lax
from jax.experimental import pallas as pl
from jax.experimental.pallas import tpu as pltpu
from jax.sharding import Mesh, PartitionSpec as P

C1 = 192
C2 = 384
HEAD = 32
LEVELS = 2
WLAT = 6
WLON = 12
WINDOW = 144
REL = 2 * WLON - 1
COLUMN = LEVELS * WLAT
FACTOR = HEAD**-0.5
EPSILON = 1e-05
MASKED = -1e30
GROUPS_ONE = ((0, 4), (4, 2))
GROUPS_TWO = ((0, 4), (4, 4), (8, 4))
STRIPS = (112, 112, 48)
VMEM_BYTES = 60 * 1024 * 1024
LANES = 128
CHIPS = 64
UPPER_BLOCK = 128
LOWER_BLOCK = 32
F32 = jnp.float32
BF16 = jnp.bfloat16


def constants():
    select = np.zeros((2, 432, 288), np.float32)
    for col in range(36):
        half, source = (0, 6 + col) if col < 18 else (1, col - 18)
        for level in range(2):
            for a in range(6):
                select[level, col * 12 + level * 6 + a, half * 144 + a * 24 + source] = 1
    own = {}
    gather = np.zeros((3, 576, 432), np.float32)
    for pr in range(2):
        for pc in range(2):
            for out_col in range(12):
                for level in range(2):
                    for out_row in range(6):
                        row, col = 3 + 2 * out_row + pr, 6 + 2 * out_col + pc
                        place = (pr * 2 + pc) * 144 + out_col * 12 + level * 6 + out_row
                        gather[row // 6, place, col * 12 + level * 6 + row % 6] = 1
                        own[row, col, level] = place
    cot_select = np.zeros((144, 288), np.float32)
    for out_col in range(12):
        for out_row in range(6):
            for level in range(2):
                up, right = out_row < 3, out_col >= 6
                block = (2 if up else 0) + (1 if right else 0)
                col = out_col - 6 if right else 6 + out_col
                place = out_col * 12 + level * 6 + out_row
                cot_select[place, block * 72 + out_row % 3 * 24 + level * 12 + col] = 1
    strips = np.zeros((sum(STRIPS), 576), np.float32)
    back_own = np.zeros((576, 576), np.float32)
    back_strips = np.zeros((576, sum(STRIPS)), np.float32)
    for row in range(6, 18):
        for col in range(24):
            for level in range(2):
                target = (row - 6) // 6 * 288 + col * 12 + level * 6 + row % 6
                if row <= 14 and col >= 6:
                    back_own[target, own[row, col, level]] = 1
                    continue
                if row <= 14:
                    place = (row - 6) * 12 + col * 2 + level
                    sent = (row, 24 + col, level)
                elif col >= 6:
                    place = STRIPS[0] + (row - 15) * 36 + (col - 6) * 2 + level
                    sent = (row - 12, col, level)
                else:
                    place = STRIPS[0] + STRIPS[1] + (row - 15) * 12 + col * 2 + level
                    sent = (row - 12, 24 + col, level)
                back_strips[target, place] = 1
                strips[place, own[sent]] = 1
    return tuple(jnp.asarray(v, BF16) for v in (select, gather, cot_select, strips, back_own, back_strips))


def bias_constants():
    z1, z2, a1, a2, r = (v.reshape(-1) for v in np.indices((LEVELS, LEVELS, WLAT, WLAT, REL)))
    half = WLAT // 2
    kind = np.where((a1 < half) & (a2 < half), 0.0, np.where((a1 >= half) & (a2 >= half), 1.0, 2.0))
    rows = (z2 * WLAT + a2)[None] == np.arange(16)[:, None]
    lanes = (r * COLUMN + z1 * WLAT + a1)[:, None] == np.arange(REL * COLUMN)[None]
    return (
        jnp.asarray(kind[None], F32),
        jnp.asarray(rows, F32),
        jnp.asarray(lanes.astype(np.float32), BF16),
    )


def blocks_of_heads():
    mask = (np.arange(576)[:, None] // WINDOW == np.arange(128)[None] // HEAD).astype(np.float32)
    fold = (np.arange(WINDOW)[:, None] == np.arange(576)[None] % WINDOW).astype(np.float32)
    return tuple(jnp.asarray(v, BF16) for v in (mask, mask.T, fold))


def nn(left, right):
    return jnp.dot(left, right, preferred_element_type=F32)


def nt(left, right):
    return lax.dot_general(left, right, (((1,), (1,)), ((), ())), preferred_element_type=F32)


def tn(left, right):
    return lax.dot_general(left, right, (((0,), (0,)), ((), ())), preferred_element_type=F32)


def layer_norm(values):
    average = jnp.mean(values, axis=-1, keepdims=True)
    centred = values - average
    scale = lax.rsqrt(jnp.mean(centred * centred, axis=-1, keepdims=True) + EPSILON)
    return centred * scale, scale


def layer_norm_back(grad, normed, scale):
    first = jnp.mean(grad, axis=-1, keepdims=True)
    second = jnp.mean(grad * normed, axis=-1, keepdims=True)
    return scale * (grad - first - normed * second)


GELU_A = (2.0 / np.pi) ** 0.5
GELU_B = 0.044715


def gelu(values):
    tanh = jnp.tanh(GELU_A * (values + GELU_B * (values * values * values)))
    return 0.5 * values * (1.0 + tanh)


def gelu_both(values):
    square = values * values
    tanh = jnp.tanh(GELU_A * values * (1.0 + GELU_B * square))
    half = 0.5 * (1.0 + tanh)
    slope = half + 0.5 * values * (1.0 - tanh * tanh) * (GELU_A * (1.0 + 3.0 * GELU_B * square))
    return values * half, slope


def spread(values, mask, heads):
    return jnp.concatenate([values] * heads, axis=0) * mask[: heads * WINDOW, : heads * HEAD]


def pull(left, right, mask_t, fold, heads):
    both = tn(left, right).astype(BF16) * mask_t[: heads * HEAD, : heads * WINDOW]
    return nt(fold[:, : heads * WINDOW], both)


def attend(queries, keys, values, bias, mask, mask_t, fold, heads):
    scores = nt(keys, spread(queries, mask, heads)) * FACTOR + bias
    powers = jnp.exp(scores - jnp.max(scores, axis=0, keepdims=True))
    chances = powers * (1.0 / jnp.sum(powers, axis=0, keepdims=True))
    return pull(values, chances.astype(BF16), mask_t, fold, heads), chances


def attend_back(queries, keys, values, chances, grad, mask, mask_t, fold, heads):
    grads = spread(grad, mask, heads)
    grad_chances = nt(values, grads)
    grad_values = nn(chances.astype(BF16), grads)
    inner = jnp.sum(grad_chances * chances, axis=0, keepdims=True)
    grad_scores = (chances * (grad_chances - inner) * FACTOR).astype(BF16)
    grad_keys = nn(grad_scores, spread(queries, mask, heads))
    grad_queries = pull(keys, grad_scores, mask_t, fold, heads)
    return grad_queries, grad_keys, grad_values


def bias_kernel(ids, one, two, kind, rows, lanes, first_ref, second_ref, two_out_ref, pieces, table):
    band = ids[0]

    def window(source, index):
        count = source.shape[0] - 1
        value = source[lax.rem(index + count, count)]
        mixed = jnp.where(
            kind[...] == 0.0, source[count], jnp.where(kind[...] == 1.0, source[0], MASKED)
        )
        return jnp.where(lax.rem(index + count, count) == 0, mixed, value)

    slot = 0
    for source, index in ((one, 2 * band - 1), (one, 2 * band), (one, 2 * band + 1), (two, band)):
        rest = window(source, index)
        for piece in range(3):
            taken = rest.astype(BF16).astype(F32)
            rest = rest - taken
            for h in range(taken.shape[0]):
                low = (slot + h) * 16
                value = jnp.where(rows[...] > 0.0, taken[h : h + 1, :], 0.0)
                pieces[piece, low : low + 16, :] = value.astype(BF16)
        slot += source.shape[1]
    table[...] = nn(pieces[0], lanes[...]) + nn(pieces[1], lanes[...]) + nn(pieces[2], lanes[...])

    for base, count, groups, targets in (
        (0, 3, GROUPS_ONE, (first_ref, second_ref)),
        (18, 1, GROUPS_TWO, (two_out_ref, two_out_ref, two_out_ref)),
    ):
        for row in range(count):
            for index, (start, heads) in enumerate(groups):
                target = targets[index]
                place = row if count == 3 else index
                low = [(base + row * 6 + start + h) * 16 for h in range(heads)]
                for o2 in range(WLON):
                    left = (WLON - 1 - o2) * COLUMN
                    piece = [table[at : at + COLUMN, left : left + WINDOW] for at in low]
                    target[place, o2 * COLUMN : (o2 + 1) * COLUMN, :] = jnp.concatenate(piece, axis=1)


def expand_bias(*operands):
    return pl.pallas_call(
        bias_kernel,
        in_specs=specs(len(operands)),
        out_shape=(
            jax.ShapeDtypeStruct((3, WINDOW, 576), F32),
            jax.ShapeDtypeStruct((3, WINDOW, 288), F32),
            jax.ShapeDtypeStruct((3, WINDOW, 576), F32),
        ),
        scratch_shapes=[
            pltpu.VMEM((3, 480, operands[1].shape[2]), BF16),
            pltpu.VMEM((480, REL * COLUMN), F32),
        ],
        compiler_params=pltpu.CompilerParams(vmem_limit_bytes=VMEM_BYTES),
        name="bias_expand",
    )(*operands)


def pack_kernel(tokens, cot, right_ref, up_ref):
    for out, row, cot_row in ((right_ref, 0, 0), (up_ref, 3, 3)):
        out[:9] = tokens[row : row + 9]
        for r in range(3):
            value = cot[cot_row + r].astype(F32)
            out[9 + r] = jnp.concatenate([value[:, :C2], value[:, C2:]], axis=0).astype(BF16)


def pack(tokens, cot):
    shape = jax.ShapeDtypeStruct((12, 24, 2 * C1), BF16)
    return pl.pallas_call(pack_kernel, out_shape=(shape, shape), name="pack")(tokens, cot)


def put(packed, base, value):
    half, count = packed.shape[1], value.shape[0]
    for j in range(value.shape[1] // LANES):
        start, stop = base + j * count, base + (j + 1) * count
        lanes = value[:, j * LANES : (j + 1) * LANES]
        for part in range(2):
            low, high = max(start, part * half), min(stop, (part + 1) * half)
            if low < high:
                packed[part, low - part * half : high - part * half, :] = lanes[low - start : high - start]
    return base + value.shape[0] * value.shape[1] // LANES


def take(packed, base, count, columns):
    half, lanes = packed.shape[1], []
    for j in range(columns):
        start, stop, rows = base + j * count, base + (j + 1) * count, []
        for part in range(2):
            low, high = max(start, part * half), min(stop, (part + 1) * half)
            if low < high:
                rows.append(packed[part, low - part * half : high - part * half, :])
        lanes.append(rows[0] if len(rows) == 1 else jnp.concatenate(rows, axis=0))
    return jnp.concatenate(lanes, axis=1).astype(F32)


def send_halves(ids, packed, mine_ref, theirs_ref, sems):
    copies = [
        pltpu.make_async_copy(packed.at[ids[2]], mine_ref, sems.at[0]),
        pltpu.make_async_copy(packed.at[1 - ids[2]], theirs_ref, sems.at[1]),
    ]
    for copy in copies:
        copy.start()
    for copy in copies:
        copy.wait()


def upper_kernel(
    ids, own, cot_own, right, up, diag,
    bias_a, bias_b, bias_two,
    qkv_one, proj_one, up_one, down_one, merge, qkv_two, proj_two, up_two, down_two,
    select, gather, cot_select, strips, mask_ref, mask_t_ref, fold_ref,
    out_ref, xw_ref, grad_ref, lon_ref, lat_ref, corner_ref, mine_ref, theirs_ref,
    q_ref, k_ref, v_ref, att_ref, xm_ref, am_ref, one_ref, p_ref, packed, sems,
):
    mask, mask_t, fold = mask_ref[...], mask_t_ref[...], fold_ref[...]

    def rows_of(block, start, count):
        return [block[start + r].astype(F32) for r in range(count)]

    for wr in range(3):
        if wr == 0:
            left, other = rows_of(up, 0, 6), rows_of(diag, 0, 6)
        elif wr == 1:
            left = rows_of(up, 6, 3) + rows_of(own, 0, 3)
            other = rows_of(diag, 6, 3) + rows_of(right, 0, 3)
        else:
            left, other = rows_of(own, 3, 6), rows_of(right, 3, 6)
        source = jnp.concatenate(left + other, axis=0).astype(BF16)
        cells = nn(select[0], source[:, :C1]) + nn(select[1], source[:, C1:])
        xw_ref[wr] = cells.astype(BF16)
        normed = layer_norm(cells)[0].astype(BF16)
        projected = nn(normed, qkv_one[...]).astype(BF16)
        q_ref[wr] = projected[:, :C1]
        k_ref[wr] = projected[:, C1 : 2 * C1]
        v_ref[wr] = projected[:, 2 * C1 :]

    @pl.loop(0, 3)
    def _(wr):
        for wc in range(3):
            rows = slice(wc * WINDOW, (wc + 1) * WINDOW)
            for start, heads in GROUPS_ONE:
                lanes = slice(start * HEAD, (start + heads) * HEAD)
                bias = bias_a[wr] if heads == 4 else bias_b[wr]
                att_ref[wr, rows, lanes] = attend(
                    q_ref[wr, rows, lanes], k_ref[wr, rows, lanes], v_ref[wr, rows, lanes],
                    bias, mask, mask_t, fold, heads,
                )[0].astype(BF16)

    xm_ref[...] = nn(gather[0], xw_ref[0]) + nn(gather[1], xw_ref[1]) + nn(gather[2], xw_ref[2])
    am_ref[...] = (
        nn(gather[0], att_ref[0]) + nn(gather[1], att_ref[1]) + nn(gather[2], att_ref[2])
    ).astype(BF16)

    @pl.loop(0, 4)
    def _(g):
        rows = pl.ds(pl.multiple_of(g * WINDOW, WINDOW), WINDOW)
        middle = xm_ref[rows, :] + nn(am_ref[rows, :], proj_one[...])
        normed = layer_norm(middle)[0].astype(BF16)
        active = gelu(nn(normed, up_one[...])).astype(BF16)
        one_ref[rows, :] = middle + nn(active, down_one[...])

    parts = [one_ref[g * WINDOW : (g + 1) * WINDOW, :] for g in range(4)]
    average = sum(jnp.sum(part, axis=-1, keepdims=True) for part in parts) / (4 * C1)
    spread_of = sum(
        jnp.sum((part - average) * (part - average), axis=-1, keepdims=True) for part in parts
    ) / (4 * C1)
    merge_scale = lax.rsqrt(spread_of + EPSILON)
    merged = [((part - average) * merge_scale) for part in parts]
    merged_low = [part.astype(BF16) for part in merged]
    grid = sum(nn(merged_low[g], merge[g * C1 : (g + 1) * C1, :]) for g in range(4))

    normed_full, scale = layer_norm(grid)
    normed = normed_full.astype(BF16)
    q, k, v = (nn(normed, qkv_two[:, j * C2 : (j + 1) * C2]).astype(BF16) for j in range(3))
    attended = []
    for index, (start, heads) in enumerate(GROUPS_TWO):
        lanes = slice(start * HEAD, (start + heads) * HEAD)
        taken, chances = attend(
            q[:, lanes], k[:, lanes], v[:, lanes], bias_two[index], mask, mask_t, fold, heads
        )
        p_ref[index] = chances
        attended.append(taken.astype(BF16))
    attended = jnp.concatenate(attended, axis=1)
    middle = grid + nn(attended, proj_two[...])
    normed_two_full, scale_two = layer_norm(middle)
    normed_two = normed_two_full.astype(BF16)
    active, slope = gelu_both(nn(normed_two, up_two[...]))
    active = active.astype(BF16)
    out_ref[...] = middle + nn(active, down_two[...])

    cot = []
    for r in range(3):
        value = cot_own[r].astype(F32)
        cot += [value[:, :C2], value[:, C2:]]
    for block in (right, up, diag):
        cot += rows_of(block, 9, 3)
    grad = nn(cot_select[...], jnp.concatenate(cot, axis=0).astype(BF16))
    grad_low = grad.astype(BF16)
    put(packed, 4608, tn(active, grad_low).astype(BF16))
    grad_raised = (nt(grad_low, down_two[...]) * slope).astype(BF16)
    put(packed, 0, tn(normed_two, grad_raised).astype(BF16))
    grad_middle = grad + layer_norm_back(nt(grad_raised, up_two[...]), normed_two_full, scale_two)
    grad_middle_low = grad_middle.astype(BF16)
    put(packed, 9216, tn(attended, grad_middle_low).astype(BF16))
    grad_attended = nt(grad_middle_low, proj_two[...]).astype(BF16)
    pieces = []
    for index, (start, heads) in enumerate(GROUPS_TWO):
        lanes = slice(start * HEAD, (start + heads) * HEAD)
        pieces.append(
            attend_back(
                q[:, lanes], k[:, lanes], v[:, lanes], p_ref[index], grad_attended[:, lanes],
                mask, mask_t, fold, heads,
            )
        )
    grad_normed = None
    for j in range(3):
        part = jnp.concatenate([piece[j].astype(BF16) for piece in pieces], axis=1)
        put(packed, 10368 + j * 1152, tn(normed, part).astype(BF16))
        term = nt(part, qkv_two[:, j * C2 : (j + 1) * C2])
        grad_normed = term if grad_normed is None else grad_normed + term
    grad_grid = (grad_middle + layer_norm_back(grad_normed, normed_full, scale)).astype(BF16)

    grad_parts = []
    grad_merge = [tn(merged_low[g], grad_grid).astype(BF16) for g in range(4)]
    put(packed, 13824, jnp.concatenate(grad_merge, axis=0))
    packed[1, 16128 - packed.shape[1] :, :] = jnp.zeros((256, LANES), BF16)
    for g in range(4):
        grad_parts.append(nt(grad_grid, merge[g * C1 : (g + 1) * C1, :]))
    first = sum(jnp.sum(part, axis=-1, keepdims=True) for part in grad_parts) / (4 * C1)
    second = sum(
        jnp.sum(part * kept, axis=-1, keepdims=True) for part, kept in zip(grad_parts, merged)
    ) / (4 * C1)
    for g in range(4):
        grad_ref[g * WINDOW : (g + 1) * WINDOW, :] = (
            merge_scale * (grad_parts[g] - first - merged[g] * second)
        ).astype(BF16)
    sent = nn(strips[...], grad_ref[...]).astype(BF16)
    lon_ref[...] = sent[: STRIPS[0]]
    lat_ref[...] = sent[STRIPS[0] : STRIPS[0] + STRIPS[1]]
    corner_ref[...] = sent[STRIPS[0] + STRIPS[1] :]
    send_halves(ids, packed, mine_ref, theirs_ref, sems)


def packed_shape(block):
    return jax.ShapeDtypeStruct((CHIPS * block, LANES), BF16)


def specs(count):
    vmem = pl.BlockSpec(memory_space=pltpu.VMEM)
    return [pl.BlockSpec(memory_space=pltpu.SMEM)] + [vmem] * (count - 1)


def out_specs(count, last_any):
    vmem, left = pl.BlockSpec(memory_space=pltpu.VMEM), pl.BlockSpec(memory_space=pl.ANY)
    return tuple([vmem] * (count - last_any) + [left] * last_any)


def upper(*operands):
    shape = jax.ShapeDtypeStruct
    return pl.pallas_call(
        upper_kernel,
        in_specs=specs(len(operands)),
        out_specs=out_specs(8, 2),
        out_shape=(
            shape((WINDOW, C2), F32),
            shape((3, 432, C1), BF16),
            shape((576, C1), BF16),
            shape((STRIPS[0], C1), BF16),
            shape((STRIPS[1], C1), BF16),
            shape((STRIPS[2], C1), BF16),
            packed_shape(UPPER_BLOCK),
            packed_shape(UPPER_BLOCK),
        ),
        scratch_shapes=[
            pltpu.VMEM((3, 432, C1), BF16),
            pltpu.VMEM((3, 432, C1), BF16),
            pltpu.VMEM((3, 432, C1), BF16),
            pltpu.VMEM((3, 432, C1), BF16),
            pltpu.VMEM((576, C1), F32),
            pltpu.VMEM((576, C1), BF16),
            pltpu.VMEM((576, C1), F32),
            pltpu.VMEM((3, WINDOW, 576), F32),
            pltpu.VMEM((2, CHIPS * UPPER_BLOCK, LANES), BF16),
            pltpu.SemaphoreType.DMA((2,)),
        ],
        compiler_params=pltpu.CompilerParams(vmem_limit_bytes=VMEM_BYTES),
        name="upper",
    )(*operands)


def lower_kernel(
    ids, xw, own, lon, lat, corner, bias_a, bias_b,
    qkv_one, proj_one, up_one, down_one,
    back_own, back_strips, mask_ref, mask_t_ref, fold_ref,
    out_ref, mine_ref, theirs_ref,
    gs_ref, normed_ref, full_ref, scale_ref, q_ref, k_ref, v_ref, pa_ref, pb_ref, att_ref,
    normed_two_ref, act_ref, raised_ref, gm_ref, gml_ref, gq_ref, gk_ref, gv_ref,
    packed, sems,
):
    mask, mask_t, fold = mask_ref[...], mask_t_ref[...], fold_ref[...]
    arrived = jnp.concatenate([lon[...], lat[...], corner[...]], axis=0)
    gs_ref[...] = nn(back_own[...], own[...]) + nn(back_strips[...], arrived)

    for row in range(2):
        rows = slice(row * 288, (row + 1) * 288)
        cells = xw[1 + row, :288, :].astype(F32)
        full, scale = layer_norm(cells)
        full_ref[rows, :] = full
        scale_ref[rows, :] = scale
        normed = full.astype(BF16)
        normed_ref[rows, :] = normed
        projected = nn(normed, qkv_one[...]).astype(BF16)
        q_ref[rows, :] = projected[:, :C1]
        k_ref[rows, :] = projected[:, C1 : 2 * C1]
        v_ref[rows, :] = projected[:, 2 * C1 :]

    @pl.loop(0, 2)
    def _(row):
        for wc in range(2):
            window = row * 2 + wc
            rows = pl.ds(pl.multiple_of(row * 288 + wc * WINDOW, WINDOW), WINDOW)
            for start, heads in GROUPS_ONE:
                lanes = slice(start * HEAD, (start + heads) * HEAD)
                bias = bias_a[1 + row] if heads == 4 else bias_b[1 + row]
                taken, chances = attend(
                    q_ref[rows, lanes], k_ref[rows, lanes], v_ref[rows, lanes],
                    bias, mask, mask_t, fold, heads,
                )
                att_ref[rows, lanes] = taken.astype(BF16)
                if heads == 4:
                    pa_ref[window] = chances
                else:
                    pb_ref[window] = chances

    @pl.loop(0, 4)
    def _(window):
        rows = pl.ds(pl.multiple_of(window * WINDOW, WINDOW), WINDOW)
        cells = xw[1 + window // 2, pl.ds(pl.multiple_of(window % 2 * WINDOW, WINDOW), WINDOW), :]
        middle = cells.astype(F32) + nn(att_ref[rows, :], proj_one[...])
        full, scale = layer_norm(middle)
        normed_two = full.astype(BF16)
        normed_two_ref[rows, :] = normed_two
        active, slope = gelu_both(nn(normed_two, up_one[...]))
        act_ref[rows, :] = active.astype(BF16)
        grad = gs_ref[rows, :]
        grad_raised = (nt(grad.astype(BF16), down_one[...]) * slope).astype(BF16)
        raised_ref[rows, :] = grad_raised
        grad_middle = grad + layer_norm_back(nt(grad_raised, up_one[...]), full, scale)
        gm_ref[rows, :] = grad_middle
        low = grad_middle.astype(BF16)
        gml_ref[rows, :] = low
        grad_attended = nt(low, proj_one[...]).astype(BF16)
        for start, heads in GROUPS_ONE:
            lanes = slice(start * HEAD, (start + heads) * HEAD)
            chances = pa_ref[window] if heads == 4 else pb_ref[window]
            gq, gk, gv = attend_back(
                q_ref[rows, lanes], k_ref[rows, lanes], v_ref[rows, lanes], chances,
                grad_attended[:, lanes], mask, mask_t, fold, heads,
            )
            gq_ref[rows, lanes] = gq.astype(BF16)
            gk_ref[rows, lanes] = gk.astype(BF16)
            gv_ref[rows, lanes] = gv.astype(BF16)
        grad_normed = (
            nt(gq_ref[rows, :], qkv_one[:, :C1])
            + nt(gk_ref[rows, :], qkv_one[:, C1 : 2 * C1])
            + nt(gv_ref[rows, :], qkv_one[:, 2 * C1 :])
        )
        out_ref[rows, :] = grad_middle + layer_norm_back(
            grad_normed, full_ref[rows, :], scale_ref[rows, :]
        )

    normed = normed_ref[...]
    grads = [tn(normed, ref[...]) for ref in (gq_ref, gk_ref, gv_ref)]
    grads = jnp.concatenate(grads + [tn(att_ref[...], gml_ref[...])], axis=1)
    put(packed, 0, grads.astype(BF16))
    put(packed, 1152, tn(normed_two_ref[...], raised_ref[...]).astype(BF16))
    low = gs_ref[...].astype(BF16)
    grads = [tn(act_ref[:, j * C1 : (j + 1) * C1], low) for j in range(4)]
    put(packed, 2304, jnp.concatenate(grads, axis=1).astype(BF16))
    packed[1, 3456 - packed.shape[1] :, :] = jnp.zeros((640, LANES), BF16)
    send_halves(ids, packed, mine_ref, theirs_ref, sems)


def lower(*operands):
    shape = jax.ShapeDtypeStruct
    wide = pltpu.VMEM((576, C1), BF16)
    return pl.pallas_call(
        lower_kernel,
        in_specs=specs(len(operands)),
        out_specs=out_specs(3, 2),
        out_shape=(
            shape((576, C1), F32), packed_shape(LOWER_BLOCK), packed_shape(LOWER_BLOCK)
        ),
        scratch_shapes=[
            pltpu.VMEM((576, C1), F32),
            wide,
            pltpu.VMEM((576, C1), F32),
            pltpu.VMEM((576, 1), F32),
            wide, wide, wide,
            pltpu.VMEM((4, WINDOW, 576), F32),
            pltpu.VMEM((4, WINDOW, 288), F32),
            wide,
            wide,
            pltpu.VMEM((576, 768), BF16),
            pltpu.VMEM((576, 768), BF16),
            pltpu.VMEM((576, C1), F32),
            wide, wide, wide, wide,
            pltpu.VMEM((2, CHIPS * LOWER_BLOCK, LANES), BF16),
            pltpu.SemaphoreType.DMA((2,)),
        ],
        compiler_params=pltpu.CompilerParams(vmem_limit_bytes=VMEM_BYTES),
        name="lower",
    )(*operands)


def call(kernel, name, out_shape, operands, scratch=()):
    return pl.pallas_call(
        kernel,
        in_specs=specs(len(operands)),
        out_shape=out_shape,
        scratch_shapes=scratch,
        compiler_params=pltpu.CompilerParams(vmem_limit_bytes=VMEM_BYTES),
        name=name,
    )(*operands)


def chip_kernel(ids, mine_two, theirs_two, mine_one, theirs_one, out):
    for low, mine, theirs in ((0, mine_two, theirs_two), (UPPER_BLOCK, mine_one, theirs_one)):
        rows = mine.shape[0] // CHIPS
        for block in range(CHIPS):
            at = slice(block * rows, (block + 1) * rows)
            value = mine[at].astype(F32) + theirs[at].astype(F32)
            out[block, low : low + rows, :] = value.astype(BF16)


def total_kernel(ids, blocks, out):
    value = blocks[0].astype(F32)
    for block in range(1, CHIPS):
        value = value + blocks[block].astype(F32)
    value = value.astype(BF16)
    for block in range(CHIPS):
        out[block] = value


def last_kernel(factor, ids, mine, theirs, qkv, proj, up, down, merge, qkv_two, proj_two, up_two, down_two, upper, lower):
    for half, source in ((ids[2], mine), (1 - ids[2], theirs)):
        for block in range(CHIPS):
            upper[half, block * UPPER_BLOCK : (block + 1) * UPPER_BLOCK, :] = source[block, :UPPER_BLOCK, :]
            lower[half, block * LOWER_BLOCK : (block + 1) * LOWER_BLOCK, :] = source[block, UPPER_BLOCK:, :]
    for out, base in ((up_two, 0), (down_two, 4608), (proj_two, 9216), (merge, 13824)):
        out[...] = take(upper, base, out.shape[0], out.shape[1] // LANES) * factor
    for j in range(3):
        qkv_two[:, j * C2 : (j + 1) * C2] = take(upper, 10368 + j * 1152, C2, 3) * factor
    joined = take(lower, 0, C1, 6) * factor
    qkv[...] = joined[:, : 3 * C1]
    proj[...] = joined[:, 3 * C1 :]
    up[...] = take(lower, 1152, C1, 6) * factor
    joined = take(lower, 2304, C1, 6) * factor
    for j in range(4):
        down[j * C1 : (j + 1) * C1, :] = joined[:, j * C1 : (j + 1) * C1]


def per_device(
    tokens, cotangent, bias_one, qkv_one, proj_one, up_one, down_one,
    merge_weight, bias_two, qkv_two, proj_two, up_two, down_two,
):
    lon = ("chip", "core")
    both = ("lat", "chip", "core")
    lats, lons = lax.axis_size("lat"), lax.axis_size(lon)
    ids = jnp.stack([lax.axis_index(name) for name in both]).astype(jnp.int32)
    factor = (WINDOW * lats * lons) ** -0.5
    from_right = [((i + 1) % lons, i) for i in range(lons)]
    to_right = [(i, (i + 1) % lons) for i in range(lons)]
    from_up = [(i, (i + 1) % lats) for i in range(lats)]
    to_up = [((i + 1) % lats, i) for i in range(lats)]
    other_core = [(i, 1 - i) for i in range(2)]
    corner_in = [
        (i * lons + (j + 1) % lons, (i + 1) % lats * lons + j) for i in range(lats) for j in range(lons)
    ]
    corner_out = [
        ((i + 1) % lats * lons + j, i * lons + (j + 1) % lons) for i in range(lats) for j in range(lons)
    ]
    for_left, for_down = pack(tokens[0], cotangent[0])
    right = lax.ppermute(for_left, lon, from_right)
    up = lax.ppermute(for_down, "lat", from_up)
    diag = lax.ppermute(for_down, both, corner_in)

    bias_a, bias_b, bias_c = expand_bias(ids, bias_one, bias_two, *bias_constants())
    select, gather, cot_select, strips, back_own, back_strips = constants()
    mask, mask_t, fold = blocks_of_heads()
    out_two, xw, grad_own, lon_strip, lat_strip, corner, mine_two, theirs_two = upper(
        ids, tokens[0], cotangent[0], right, up, diag, bias_a, bias_b, bias_c,
        qkv_one, proj_one, up_one, down_one, merge_weight, qkv_two, proj_two, up_two, down_two,
        select, gather, cot_select, strips, mask, mask_t, fold,
    )
    lon_strip = lax.ppermute(lon_strip, lon, to_right)
    lat_strip = lax.ppermute(lat_strip, "lat", to_up)
    corner = lax.ppermute(corner, both, corner_out)
    theirs_two = lax.ppermute(theirs_two, "core", other_core)
    grad_cells, mine_one, theirs_one = lower(
        ids, xw, grad_own, lon_strip, lat_strip, corner, bias_a, bias_b,
        qkv_one, proj_one, up_one, down_one,
        back_own, back_strips, mask, mask_t, fold,
    )
    theirs_one = lax.ppermute(theirs_one, "core", other_core)
    result = jax.ShapeDtypeStruct
    blocks = result((CHIPS, UPPER_BLOCK + LOWER_BLOCK, LANES), BF16)
    packed = call(chip_kernel, "chip", blocks, (ids, mine_two, theirs_two, mine_one, theirs_one))
    packed = lax.all_to_all(packed, ("lat", "chip"), 0, 0, tiled=True)
    packed = call(total_kernel, "total", blocks, (ids, packed))
    packed = lax.all_to_all(packed, ("lat", "chip"), 0, 0, tiled=True)
    weights = (
        qkv_one, proj_one, up_one, down_one, merge_weight, qkv_two, proj_two, up_two, down_two
    )
    sums = call(
        functools.partial(last_kernel, factor), "last", tuple(result(w.shape, F32) for w in weights),
        (ids, packed, lax.ppermute(packed, "core", other_core)),
        [
            pltpu.VMEM((2, CHIPS * UPPER_BLOCK, LANES), BF16),
            pltpu.VMEM((2, CHIPS * LOWER_BLOCK, LANES), BF16),
        ],
    )

    def shift_back(value, half_rows, half_cols):
        arrived = lax.ppermute(value[:, value.shape[1] - half_cols :], lon, to_right)
        value = jnp.concatenate([arrived, value[:, : value.shape[1] - half_cols]], axis=1)
        arrived = lax.ppermute(value[:half_rows], "lat", to_up)
        return jnp.concatenate([value[half_rows:], arrived], axis=0)

    out_two = out_two.reshape(12, LEVELS, WLAT, C2).transpose(2, 0, 1, 3).reshape(6, 12, LEVELS * C2)
    out_two = shift_back(out_two, WLAT // 2, WLON // 2)[None]
    grad_cells = grad_cells.reshape(2, 24, LEVELS, WLAT, C1).transpose(0, 3, 1, 2, 4)
    grad_tokens = shift_back(grad_cells.reshape(12, 24, LEVELS * C1), WLAT // 2, WLON // 2)[None]
    return (out_two, grad_tokens, *sums)


def solution(mesh):
    lats, lons = mesh.devices.shape
    mesh = Mesh(mesh.devices.reshape(lats, lons // 2, 2), ("lat", "chip", "core"))
    sharded, copied = P(None, "lat", ("chip", "core"), None), P()
    return jax.shard_map(
        per_device,
        mesh=mesh,
        in_specs=(sharded, sharded) + (copied,) * 11,
        out_specs=(sharded, sharded) + (copied,) * 9,
        check_vma=False,
    )
```

time: 783 us -> 210 us (0.27)
  local copies, waits for them, and re-layouts: 286 us -> 12.7 us
  matrix products: 196 us -> 0 us
  waiting for transfers between devices: 192 us -> 10.9 us
  blocking collectives: 0 us -> 81 us
  Pallas kernels: 0 us -> 76.4 us
  other arithmetic: 44.7 us -> 2.51 us
  between operations: 16.6 us -> 0.79 us
  starting transfers between devices: 37.4 us -> 22.3 us
    dot_general x39 -> x0, matrix products: 178 us -> none  [the longest x2 58.5 us: offset_matrix(): jnp.einsum('...xyabr,rpq->...xapybq', split_rows, selector, precision=HIG...]
    psum x1 -> x0, waiting for transfers between devices: 161 us -> none  [per_device(): lax.psum((grads_one[0], grads_one[1], grads_one[2], grads_one[3]), ('lat'...]
    add x12 -> x0, local copies, waits for them, and re-layouts: 108 us -> none  [the longest x4 106 us: attend(): jnp.einsum('aoqhd,aokhd->aohqk', queries, key_rows, preferred_element_typ...]
    all_to_all x0 -> x2, blocking collectives: none -> 81 us  [per_device(): packed = lax.all_to_all(packed, ('lat', 'chip'), 0, 0, tiled=True)]
    pallas_call x0 -> x7, Pallas kernels: none -> 76.4 us  [the longest x1 29 us: upper(): pl.pallas_call(upper_kernel, in_specs=specs(len(operands)), out_specs=out...]
    concatenate x16 -> x0, local copies, waits for them, and re-layouts: 32.3 us -> none  [the longest x6 23.3 us: level_backward(): jnp.concatenate([grad_part.reshape(grad_part.shape[:3] + (width,)) for gr...]
    transpose x13 -> x2, local copies, waits for them, and re-layouts: 29.9 us -> 1.23 us  [the longest x1 1.12 us: per_device(): grad_cells.reshape(2, 24, LEVELS, WLAT, C1).transpose(0, 3, 1, 2, 4)]
    reshape x30 -> x4, local copies, waits for them, and re-layouts: 30.9 us -> 2.85 us  [the longest x1 1.51 us: per_device(): grad_cells.reshape(12, 24, LEVELS * C1)]
  transfers between devices with their start and end apart: 17 -> 13, of which waited for: 8 -> 5; matrix products, arithmetic and copies ran while one was open for 28% -> 5% of each run, Pallas kernels for 0% -> 15%
where the time goes in v1:
time: 210 us; the launch traced here: 207 us
  blocking collectives  81 us (39%)
  Pallas kernels  76.4 us (36%)
  starting transfers between devices  22.3 us (11%)
  local copies, waits for them, and re-layouts  12.7 us (6%)
  waiting for transfers between devices  10.9 us (5%)
  other arithmetic  2.51 us (1%)
    all_to_all x2, blocking collectives, per_device(): packed = lax.all_to_all(packed, ('lat', 'chip'), 0, 0, tiled=True)  81 us
    pallas_call x1, Pallas kernels, upper(): pl.pallas_call(upper_kernel, in_specs=specs(len(operands)), out_specs=out...  29 us
    pallas_call x1, Pallas kernels, lower(): pl.pallas_call(lower_kernel, in_specs=specs(len(operands)), out_specs=out...  19.4 us
    pallas_call x3, Pallas kernels, call(): pl.pallas_call(kernel, in_specs=specs(len(operands)), out_shape=out_shape...  15.2 us
    pallas_call x1, Pallas kernels, expand_bias(): pl.pallas_call(bias_kernel, in_specs=specs(len(operands)), out_shape=(jax...  11 us
    unnamed x23, local copies, waits for them, and re-layouts  7.91 us
    ppermute x1, starting transfers between devices, per_device(): diag = lax.ppermute(for_down, both, corner_in)  6.82 us
    ppermute x1, waiting for transfers between devices, per_device(): corner = lax.ppermute(corner, both, corner_out)  4.96 us
  transfers between devices with their start and end apart: 13, of which 5 were waited for; matrix products, arithmetic and copies ran while one was open for 5% of the time, Pallas kernels for 15%

profile of v1, /device:TPU:1, one launch (start us, length us, event | category | flops | bytes accessed | tf_op | source)
XLA Modules:
  0.0 206.6 jit_solution(12811042683510338403)
XLA Ops:
  0.6 1.8 pack.1
  2.5 1.4 collective-permute-start
  3.9 6.8 %collective-permute-start.2 = (bf16[12,24,384]{2,1,0:T(8,128)(2,1)}, bf16[12,24,384]{2,1,0:T(8,128)(2,1)S(1)}, u32[]{:S(2)}, u32[]{:S(2)}) collective-permute-start(bf16[12,24,384]{2,1,0:T(8,128)(2,1)} %get-tuple-element.37), channel_id=1, source_target_pairs={{1,16},{2,17},{3,18},{4,19},{5,20},{6,21},{7,22},{8,23},{9,24},{10... | collective-permute-start | bytes 663560 | tf_op jit(solution)/shard_map/ppermute | solution.py:658
  10.7 0.7 collective-permute-start.1
  11.4 1.9 copy.44.down_one
  13.3 0.7 pad_add_fusion.ids
  13.9 11.0 %bias_expand.1 = (f32[3,144,576]{2,1,0:T(8,128)}, f32[3,144,288]{2,1,0:T(8,128)}, f32[3,144,576]{2,1,0:T(8,128)}) custom-call(s32[3]{0:T(128)} %pad_add_fusion.ids, f32[17,6,3312]{2,1,0:T(8,128)} %one.1, f32[9,12,3312]{2,1,0:T(8,128)} %two.1, f32[1,3312]{1,0:T(1,128)} %constant.36.clone.kind, f32[16,3312]{1,0:T(8,128)} %constant.37.clone.rows, ...), custom_call_target="tpu_custom_call" | custom-call | tf_op jit(solution)/shard_map/bias_expand/pallas_call | solution.py:214
  25.0 0.0 collective-permute-done.right
  25.0 0.0 copy-start.4
  25.0 0.0 collective-permute-done.2.diag
  25.0 0.0 copy-start.5
  25.0 0.0 collective-permute-done.1.up
  25.0 0.0 copy-start.6
  25.0 0.6 copy-done.4
  25.7 0.1 copy-done.5
  25.7 0.1 copy-done.6
  25.8 29.0 %upper.1 = (f32[144,384]{1,0:T(8,128)}, bf16[3,432,192]{2,1,0:T(8,128)(2,1)}, bf16[576,192]{1,0:T(8,128)(2,1)}, bf16[112,192]{1,0:T(8,128)(2,1)}, bf16[112,192]{...) custom-call(s32[3]{0:T(128)} %pad_add_fusion.ids, ...), custom_call_target="tpu_custom_call" | custom-call | tf_op jit(solution)/shard_map/upper/pallas_call | solution.py:432
  54.8 0.1 collective-permute-start.10
  54.9 0.1 collective-permute-start.5
  55.0 4.5 %collective-permute-start.6 = (bf16[112,192]{1,0:T(8,128)(2,1)}, bf16[112,192]{1,0:T(8,128)(2,1)S(1)}, u32[]{:S(2)}, u32[]{:S(2)}) collective-permute-start(bf16[112,192]{1,0:T(8,128)(2,1)} %get-tuple-element.45), channel_id=1, source_target_pairs={{16,0},{32,16},{48,32},{64,48},{80,64},{96,80},{112,96},{0,112},{1... | collective-permute-start | bytes 129032 | tf_op jit(solution)/shard_map/ppermute | solution.py:669
  59.4 0.0 collective-permute-start.7
  59.4 5.0 %collective-permute-done.7.corner = bf16[48,192]{1,0:T(8,128)(2,1)S(1)} collective-permute-done((bf16[48,192]{1,0:T(8,128)(2,1)}, bf16[48,192]{1,0:T(8,128)(2,1)S(1)}, u32[]{:S(2)}, u32[]{:S(2)}) %collective-permute-start.7) | collective-permute-done | bytes 18464 | tf_op jit(solution)/shard_map/ppermute | solution.py:670
  64.4 0.0 copy-start.9
  64.4 0.0 collective-permute-done.5.lon
  64.4 0.0 copy-start.7
  64.4 0.0 collective-permute-done.6.lat
  64.4 0.0 copy-start.8
  64.4 0.6 copy-done.9
  65.0 0.0 copy-done.7
  65.0 0.0 copy-done.8
  65.0 19.4 %lower.1 = (f32[576,192]{1,0:T(8,128)}, bf16[2048,128]{1,0:T(8,128)(2,1)}, bf16[2048,128]{1,0:T(8,128)(2,1)}) custom-call(s32[3]{0:T(128)} %pad_add_fusion.ids, bf16[3,432,192]{2,1,0:T(8,128)(2,1)} %get-tuple-element.42.xw, bf16[576,192]{1,0:T(8,128)(2,1)} %get-tuple-element.43.own, bf16[112,192]{1,0:T(8,128)(2,1)} %copy-done.7, bf16[112,192]{1,0:T(8,128)(2,1)} %copy-done.8, ...), custom_call_target="tpu_custom_call" | custom-call | tf_op jit(solution)/shard_map/lower/pallas_call | solution.py:559
  84.4 2.6 %collective-permute-start.11 = (bf16[2048,128]{1,0:T(8,128)(2,1)}, bf16[2048,128]{1,0:T(8,128)(2,1)S(1)}, u32[]{:S(2)}, u32[]{:S(2)}) collective-permute-start(bf16[2048,128]{1,0:T(8,128)(2,1)} %get-tuple-element.51), channel_id=1, source_target_pairs={{0,1},{1,0},{2,3},{3,2},{4,5},{5,4},{6,7},{7,6},{8,9},{9,8},{10,11... | collective-permute-start | bytes 1572872 | tf_op jit(solution)/shard_map/ppermute | solution.py:677
  87.0 1.7 collective-permute-done.11.theirs_one
  88.8 0.0 copy-start.2
  88.8 0.0 collective-permute-done.10.theirs_two
  88.8 0.8 copy-done.2
  89.6 0.7 copy-done.1
  90.3 4.6 %chip.1 = bf16[64,160,128]{2,1,0:T(8,128)(2,1)} custom-call(s32[3]{0:T(128)} %pad_add_fusion.ids, bf16[8192,128]{1,0:T(8,128)(2,1)} %get-tuple-element.48.mine_two, bf16[8192,128]{1,0:T(8,128)(2,1)} %copy-done.1, bf16[2048,128]{1,0:T(8,128)(2,1)} %get-tuple-element.50.mine_one, bf16[2048,128]{1,0:T(8,128)(2,1)} %copy-done.2), custom_call_target="tpu_custom_call" | custom-call | tf_op jit(solution)/shard_map/chip/pallas_call | solution.py:589
  94.9 41.2 %all_to_all.10.blocks = bf16[64,160,128]{2,1,0:T(8,128)(2,1)} all-to-all(bf16[64,160,128]{2,1,0:T(8,128)(2,1)} %chip.1), channel_id=1, replica_groups=mesh['lat'=8,'chip'=8,'core'=2] {'lat','chip'}, dimensions={0} | all-to-all | bytes 5242880 | tf_op jit(solution)/shard_map/all_to_all | solution.py:681
  136.1 3.7 %total.1 = bf16[64,160,128]{2,1,0:T(8,128)(2,1)} custom-call(s32[3]{0:T(128)} %pad_add_fusion.ids, bf16[64,160,128]{2,1,0:T(8,128)(2,1)} %all_to_all.10.blocks), custom_call_target="tpu_custom_call" | custom-call | tf_op jit(solution)/shard_map/total/pallas_call | solution.py:589
  139.8 39.8 %all_to_all.11.mine = bf16[64,160,128]{2,1,0:T(8,128)(2,1)S(1)} all-to-all(bf16[64,160,128]{2,1,0:T(8,128)(2,1)} %total.1), channel_id=1, replica_groups=mesh['lat'=8,'chip'=8,'core'=2] {'lat','chip'}, dimensions={0} | all-to-all | bytes 5242880 | tf_op jit(solution)/shard_map/all_to_all | solution.py:683
  179.6 2.5 %collective-permute-start.12 = (bf16[64,160,128]{2,1,0:T(8,128)(2,1)S(1)}, bf16[64,160,128]{2,1,0:T(8,128)(2,1)}, u32[]{:S(2)}, u32[]{:S(2)}) collective-permute-start(bf16[64,160,128]{2,1,0:T(8,128)(2,1)S(1)} %all_to_all.11.mine), channel_id=1, source_target_pairs={{0,1},{1,0},{2,3},{3,2},{4,5},{5,4},{6,7},{7,6},{8,9},{9,8},{10,11... | collective-permute-start | bytes 7864328 | tf_op jit(solution)/shard_map/ppermute | solution.py:689
  182.1 0.0 copy-done.3
  182.2 0.1 copy.45
  182.3 0.2 reshape.35
  182.5 0.7 fusion.2
  183.2 0.4 collective-permute-start.3
  183.6 1.1 reshape.36
  184.7 1.1 copy.47
  185.8 0.0 copy-done
  185.8 1.5 reshape.37
  187.4 0.2 collective-permute-start.8
  187.6 0.0 collective-permute-done.3
  187.6 1.0 fusion.1
  188.6 0.7 collective-permute-start.4
  189.3 0.5 collective-permute-done.8
  189.8 2.3 %collective-permute-start.9 = (f32[3,24,384]{2,1,0:T(8,128)S(1)}, f32[3,24,384]{2,1,0:T(8,128)S(1)}, u32[]{:S(2)}, u32[]{:S(2)}) collective-permute-start(f32[3,24,384]{2,1,0:T(8,128)S(1)} %pad_maximum_fusion.1), channel_id=1, source_target_pairs={{16,0},{32,16},{48,32},{64,48},{80,64},{96,80},{112,96},{0,112},{1... | collective-permute-start | bytes 331784 | tf_op jit(solution)/shard_map/ppermute | solution.py:699
  192.0 3.0 %collective-permute-done.4 = f32[3,12,768]{2,1,0:T(8,128)S(1)} collective-permute-done((f32[3,12,768]{2,1,0:T(8,128)S(1)}, f32[3,12,768]{2,1,0:T(8,128)S(1)}, u32[]{:S(2)}, u32[]{:S(2)}) %collective-permute-start.4) | collective-permute-done | bytes 110624 | tf_op jit(solution)/shard_map/ppermute | solution.py:699
  195.0 0.9 copy.48
  196.0 0.8 collective-permute-done.9
  196.7 0.8 maximum_bitcast_fusion
  197.5 0.0 collective-permute-done.12.theirs
  197.5 6.9 %last.1 = (f32[192,576]{1,0:T(8,128)}, f32[192,192]{1,0:T(8,128)}, f32[192,768]{1,0:T(8,128)}, f32[768,192]{1,0:T(8,128)}, f32[768,384]{1,0:T(8,128)}, /*index=5...) custom-call(s32[3]{0:T(128)} %pad_add_fusion.ids, bf16[64,160,128]{2,1,0:T(8,128)(2,1)} %copy-done, ...), custom_call_target="tpu_custom_call" | custom-call | tf_op jit(solution)/shard_map/last/pallas_call | solution.py:589
  204.4 2.2 %copy.49 = f32[768,192]{0,1:T(8,128)} copy(f32[768,192]{1,0:T(8,128)} %get-tuple-element.88) | data formatting | bytes 1179648
  (8 shorter events, 0.1 us)
Async XLA Ops:
  2.5 22.5 %collective-permute-start = (bf16[12,24,384]{2,1,0:T(8,128)(2,1)}, bf16[12,24,384]{2,1,0:T(8,128)(2,1)S(1)}, u32[]{:S(2)}, u32[]{:S(2)}) collective-permute-start(bf16[12,24,384]{2,1,0:T(8,128)(2,1)} %get-tuple-element.36), channel_id=1, source_target_pairs={{1,0},{2,1},{3,2},{4,3},{5,4},{6,5},{7,6},{8,7},{9,8},{10,9},{11,1... | collective-permute-start | bytes 663560 | tf_op jit(solution)/shard_map/ppermute | solution.py:656
  3.9 21.1 %collective-permute-start.2 = (bf16[12,24,384]{2,1,0:T(8,128)(2,1)}, bf16[12,24,384]{2,1,0:T(8,128)(2,1)S(1)}, u32[]{:S(2)}, u32[]{:S(2)}) collective-permute-start(bf16[12,24,384]{2,1,0:T(8,128)(2,1)} %get-tuple-element.37), channel_id=1, source_target_pairs={{1,16},{2,17},{3,18},{4,19},{5,20},{6,21},{7,22},{8,23},{9,24},{10... | collective-permute-start | bytes 663560 | tf_op jit(solution)/shard_map/ppermute | solution.py:658
  10.7 14.3 %collective-permute-start.1 = (bf16[12,24,384]{2,1,0:T(8,128)(2,1)}, bf16[12,24,384]{2,1,0:T(8,128)(2,1)S(1)}, u32[]{:S(2)}, u32[]{:S(2)}) collective-permute-start(bf16[12,24,384]{2,1,0:T(8,128)(2,1)} %get-tuple-element.37), channel_id=1, source_target_pairs={{0,16},{16,32},{32,48},{48,64},{64,80},{80,96},{96,112},{112,0},{1... | collective-permute-start | bytes 663560 | tf_op jit(solution)/shard_map/ppermute | solution.py:657
  25.0 0.7 copy-start.4
  25.0 0.8 copy-start.5
  25.0 0.8 copy-start.6
  54.8 34.0 %collective-permute-start.10 = (bf16[8192,128]{1,0:T(8,128)(2,1)}, bf16[8192,128]{1,0:T(8,128)(2,1)S(1)}, u32[]{:S(2)}, u32[]{:S(2)}) collective-permute-start(bf16[8192,128]{1,0:T(8,128)(2,1)} %get-tuple-element.49), channel_id=1, source_target_pairs={{0,1},{1,0},{2,3},{3,2},{4,5},{5,4},{6,7},{7,6},{8,9},{9,8},{10,11... | collective-permute-start | bytes 6291464 | tf_op jit(solution)/shard_map/ppermute | solution.py:671
  54.9 9.5 %collective-permute-start.5 = (bf16[112,192]{1,0:T(8,128)(2,1)}, bf16[112,192]{1,0:T(8,128)(2,1)S(1)}, u32[]{:S(2)}, u32[]{:S(2)}) collective-permute-start(bf16[112,192]{1,0:T(8,128)(2,1)} %get-tuple-element.44), channel_id=1, source_target_pairs={{0,1},{1,2},{2,3},{3,4},{4,5},{5,6},{6,7},{7,8},{8,9},{9,10},{10,1... | collective-permute-start | bytes 129032 | tf_op jit(solution)/shard_map/ppermute | solution.py:668
  55.0 9.4 %collective-permute-start.6 = (bf16[112,192]{1,0:T(8,128)(2,1)}, bf16[112,192]{1,0:T(8,128)(2,1)S(1)}, u32[]{:S(2)}, u32[]{:S(2)}) collective-permute-start(bf16[112,192]{1,0:T(8,128)(2,1)} %get-tuple-element.45), channel_id=1, source_target_pairs={{16,0},{32,16},{48,32},{64,48},{80,64},{96,80},{112,96},{0,112},{1... | collective-permute-start | bytes 129032 | tf_op jit(solution)/shard_map/ppermute | solution.py:669
  59.4 5.0 %collective-permute-start.7 = (bf16[48,192]{1,0:T(8,128)(2,1)}, bf16[48,192]{1,0:T(8,128)(2,1)S(1)}, u32[]{:S(2)}, u32[]{:S(2)}) collective-permute-start(bf16[48,192]{1,0:T(8,128)(2,1)} %get-tuple-element.46), channel_id=1, source_target_pairs={{16,1},{17,2},{18,3},{19,4},{20,5},{21,6},{22,7},{23,8},{24,9},{25... | collective-permute-start | bytes 55304 | tf_op jit(solution)/shard_map/ppermute | solution.py:670
  64.4 0.6 copy-start.9
  64.4 0.6 copy-start.7
  64.4 0.6 copy-start.8
  84.4 4.4 %collective-permute-start.11 = (bf16[2048,128]{1,0:T(8,128)(2,1)}, bf16[2048,128]{1,0:T(8,128)(2,1)S(1)}, u32[]{:S(2)}, u32[]{:S(2)}) collective-permute-start(bf16[2048,128]{1,0:T(8,128)(2,1)} %get-tuple-element.51), channel_id=1, source_target_pairs={{0,1},{1,0},{2,3},{3,2},{4,5},{5,4},{6,7},{7,6},{8,9},{9,8},{10,11... | collective-permute-start | bytes 1572872 | tf_op jit(solution)/shard_map/ppermute | solution.py:677
  88.8 0.8 copy-start.2
  88.8 1.5 copy-start.1
  139.8 42.3 %copy-start.3 = (f32[144,384]{1,0:T(8,128)S(1)}, f32[144,384]{1,0:T(8,128)}, u32[]{:S(2)}) copy-start(f32[144,384]{1,0:T(8,128)} %get-tuple-element.41) | copy-start | bytes 663556
  179.6 6.3 %copy-start = (bf16[64,160,128]{2,1,0:T(8,128)(2,1)}, bf16[64,160,128]{2,1,0:T(8,128)(2,1)S(1)}, u32[]{:S(2)}) copy-start(bf16[64,160,128]{2,1,0:T(8,128)(2,1)S(1)} %all_to_all.11.mine) | copy-start | bytes 7864324
  179.6 17.9 %collective-permute-start.12 = (bf16[64,160,128]{2,1,0:T(8,128)(2,1)S(1)}, bf16[64,160,128]{2,1,0:T(8,128)(2,1)}, u32[]{:S(2)}, u32[]{:S(2)}) collective-permute-start(bf16[64,160,128]{2,1,0:T(8,128)(2,1)S(1)} %all_to_all.11.mine), channel_id=1, source_target_pairs={{0,1},{1,0},{2,3},{3,2},{4,5},{5,4},{6,7},{7,6},{8,9},{9,8},{10,11... | collective-permute-start | bytes 7864328 | tf_op jit(solution)/shard_map/ppermute | solution.py:689
  183.2 4.5 %collective-permute-start.3 = (f32[6,6,768]{2,1,0:T(8,128)}, f32[6,6,768]{2,1,0:T(8,128)}, u32[]{:S(2)}, u32[]{:S(2)}) collective-permute-start(f32[6,6,768]{2,1,0:T(8,128)} %get-tuple-element.96), channel_id=1, source_target_pairs={{0,1},{1,2},{2,3},{3,4},{4,5},{5,6},{6,7},{7,8},{8,9},{9,10},{10,1... | collective-permute-start | bytes 331784 | tf_op jit(solution)/shard_map/ppermute | solution.py:697
  187.4 2.3 %collective-permute-start.8 = (f32[12,6,384]{2,1,0:T(8,128)S(1)}, f32[12,6,384]{2,1,0:T(8,128)S(1)}, u32[]{:S(2)}, u32[]{:S(2)}) collective-permute-start(f32[12,6,384]{2,1,0:T(8,128)S(1)} %slice.36), channel_id=1, source_target_pairs={{0,1},{1,2},{2,3},{3,4},{4,5},{5,6},{6,7},{7,8},{8,9},{9,10},{10,1... | collective-permute-start | bytes 331784 | tf_op jit(solution)/shard_map/ppermute | solution.py:697
  188.6 6.4 %collective-permute-start.4 = (f32[3,12,768]{2,1,0:T(8,128)S(1)}, f32[3,12,768]{2,1,0:T(8,128)S(1)}, u32[]{:S(2)}, u32[]{:S(2)}) collective-permute-start(f32[3,12,768]{2,1,0:T(8,128)S(1)} %get-tuple-element.95), channel_id=1, source_target_pairs={{16,0},{32,16},{48,32},{64,48},{80,64},{96,80},{112,96},{0,112},{1... | collective-permute-start | bytes 331784 | tf_op jit(solution)/shard_map/ppermute | solution.py:699
  189.8 7.0 %collective-permute-start.9 = (f32[3,24,384]{2,1,0:T(8,128)S(1)}, f32[3,24,384]{2,1,0:T(8,128)S(1)}, u32[]{:S(2)}, u32[]{:S(2)}) collective-permute-start(f32[3,24,384]{2,1,0:T(8,128)S(1)} %pad_maximum_fusion.1), channel_id=1, source_target_pairs={{16,0},{32,16},{48,32},{64,48},{80,64},{96,80},{112,96},{0,112},{1... | collective-permute-start | bytes 331784 | tf_op jit(solution)/shard_map/ppermute | solution.py:699

commit v2 on v1

--- a/solution.py
+++ b/solution.py
@@ -23,7 +23,9 @@
 GROUPS_ONE = ((0, 4), (4, 2))
 GROUPS_TWO = ((0, 4), (4, 4), (8, 4))
 STRIPS = (112, 112, 48)
-VMEM_BYTES = 60 * 1024 * 1024
+MIB = 1024 * 1024
+SHIFT = (96, 96, 64)
+SHIFT_TOKENS = (56, 56, 24)
 LANES = 128
 CHIPS = 64
 UPPER_BLOCK = 128
@@ -83,11 +85,55 @@
     return tuple(jnp.asarray(v, BF16) for v in (select, gather, cot_select, strips, back_own, back_strips))
 
 
+def output_constants():
+    starts = (0, SHIFT[0], SHIFT[0] + SHIFT[1])
+    tokens = np.zeros((2, 288 + sum(SHIFT_TOKENS), 576), np.float32)
+    place = np.zeros((288, sum(SHIFT)), np.float32)
+    two = np.zeros((144 + sum(SHIFT) - sum(SHIFT_TOKENS), WINDOW), np.float32)
+    place_two = np.zeros((144, sum(SHIFT)), np.float32)
+
+    def strip(row, col, rows, cols):
+        if row < rows:
+            return (None, row, col - cols) if col >= cols else (0, row, col)
+        return (1, row - rows, col - cols) if col >= cols else (2, row - rows, col)
+
+    for row in range(12):
+        for col in range(24):
+            kind, sub_row, sub_col = strip(row, col, 9, 6)
+            source_row = row + 3 if row < 9 else row - 9
+            source_col = col - 6 if col >= 6 else col + 18
+            if kind is None:
+                target = row * 24 + col
+            else:
+                at = sub_row * (18 if kind == 1 else 6) + sub_col
+                target = 288 + sum(SHIFT_TOKENS[:kind]) + at
+                place[row * 24 + col, starts[kind] + at] = 1
+            for level in range(2):
+                source = source_row // 6 * 288 + source_col * 12 + level * 6 + source_row % 6
+                tokens[level, target, source] = 1
+    for row in range(6):
+        for col in range(12):
+            kind, sub_row, sub_col = strip(row, col, 3, 6)
+            source_row = row + 3 if row < 3 else row - 3
+            source_col = col - 6 if col >= 6 else col + 6
+            for level in range(2):
+                if kind is None:
+                    target = level * 72 + row * 12 + col
+                else:
+                    at = level * 18 + sub_row * 6 + sub_col
+                    target = 144 + kind * 40 + at
+                    place_two[level * 72 + row * 12 + col, starts[kind] + SHIFT_TOKENS[kind] + at] = 1
+                two[target, source_col * 12 + level * 6 + source_row] = 1
+    return tuple(jnp.asarray(v, BF16) for v in (tokens, two, place, place_two))
+
+
 def bias_constants():
     z1, z2, a1, a2, r = (v.reshape(-1) for v in np.indices((LEVELS, LEVELS, WLAT, WLAT, REL)))
     half = WLAT // 2
     kind = np.where((a1 < half) & (a2 < half), 0.0, np.where((a1 >= half) & (a2 >= half), 1.0, 2.0))
-    rows = (z2 * WLAT + a2)[None] == np.arange(16)[:, None]
+    rows = np.stack(
+        [(z2 == level)[None] & (a2[None] + 2 * (1 - level) == np.arange(8)[:, None]) for level in range(2)]
+    )
     lanes = (r * COLUMN + z1 * WLAT + a1)[:, None] == np.arange(REL * COLUMN)[None]
     return (
         jnp.asarray(kind[None], F32),
@@ -100,6 +146,15 @@
     mask = (np.arange(576)[:, None] // WINDOW == np.arange(128)[None] // HEAD).astype(np.float32)
     fold = (np.arange(WINDOW)[:, None] == np.arange(576)[None] % WINDOW).astype(np.float32)
     return tuple(jnp.asarray(v, BF16) for v in (mask, mask.T, fold))
+
+
+def params(microseconds, vmem):
+    return {
+        "compiler_params": pltpu.CompilerParams(vmem_limit_bytes=vmem * MIB),
+        "cost_estimate": pl.CostEstimate(
+            flops=int(microseconds * 1e9), bytes_accessed=int(microseconds * 3e6), transcendentals=0
+        ),
+    }
 
 
 def nn(left, right):
@@ -153,22 +208,35 @@
     return nt(fold[:, : heads * WINDOW], both)
 
 
-def attend(queries, keys, values, bias, mask, mask_t, fold, heads):
-    scores = nt(keys, spread(queries, mask, heads)) * FACTOR + bias
-    powers = jnp.exp(scores - jnp.max(scores, axis=0, keepdims=True))
-    chances = powers * (1.0 / jnp.sum(powers, axis=0, keepdims=True))
-    return pull(values, chances.astype(BF16), mask_t, fold, heads), chances
-
-
-def attend_back(queries, keys, values, chances, grad, mask, mask_t, fold, heads):
-    grads = spread(grad, mask, heads)
-    grad_chances = nt(values, grads)
-    grad_values = nn(chances.astype(BF16), grads)
-    inner = jnp.sum(grad_chances * chances, axis=0, keepdims=True)
-    grad_scores = (chances * (grad_chances - inner) * FACTOR).astype(BF16)
-    grad_keys = nn(grad_scores, spread(queries, mask, heads))
-    grad_queries = pull(keys, grad_scores, mask_t, fold, heads)
+def attend(parts, mask, mask_t, fold):
+    scores = [
+        nt(keys, spread(queries, mask, heads)) * FACTOR + bias for queries, keys, _, bias, heads in parts
+    ]
+    powers = [jnp.exp(score - jnp.max(score, axis=0, keepdims=True)) for score in scores]
+    chances = [power * (1.0 / jnp.sum(power, axis=0, keepdims=True)) for power in powers]
+    taken = [
+        pull(part[2], chance.astype(BF16), mask_t, fold, part[4]) for part, chance in zip(parts, chances)
+    ]
+    return taken, chances
+
+
+def attend_back(parts, mask, mask_t, fold):
+    grads = [spread(part[4], mask, part[5]) for part in parts]
+    grad_chances = [nt(part[2], grad) for part, grad in zip(parts, grads)]
+    grad_values = [nn(part[3].astype(BF16), grad) for part, grad in zip(parts, grads)]
+    products = [grad * part[3] for part, grad in zip(parts, grad_chances)]
+    grad_scores = [
+        ((product - part[3] * jnp.sum(product, axis=0, keepdims=True)) * FACTOR).astype(BF16)
+        for part, product in zip(parts, products)
+    ]
+    grad_keys = [nn(grad, spread(part[0], mask, part[5])) for part, grad in zip(parts, grad_scores)]
+    grad_queries = [
+        pull(part[1], grad, mask_t, fold, part[5]) for part, grad in zip(parts, grad_scores)
+    ]
     return grad_queries, grad_keys, grad_values
+
+
+SPANS = (((0, 896), (1536, 2560)), ((768, 1664), (2432, 3312)))
 
 
 def bias_kernel(ids, one, two, kind, rows, lanes, first_ref, second_ref, two_out_ref, pieces, table):
@@ -176,24 +244,43 @@
 
     def window(source, index):
         count = source.shape[0] - 1
-        value = source[lax.rem(index + count, count)]
+        index = lax.rem(index + count, count)
         mixed = jnp.where(
             kind[...] == 0.0, source[count], jnp.where(kind[...] == 1.0, source[0], MASKED)
         )
-        return jnp.where(lax.rem(index + count, count) == 0, mixed, value)
-
-    slot = 0
-    for source, index in ((one, 2 * band - 1), (one, 2 * band), (one, 2 * band + 1), (two, band)):
-        rest = window(source, index)
-        for piece in range(3):
-            taken = rest.astype(BF16).astype(F32)
-            rest = rest - taken
-            for h in range(taken.shape[0]):
-                low = (slot + h) * 16
-                value = jnp.where(rows[...] > 0.0, taken[h : h + 1, :], 0.0)
-                pieces[piece, low : low + 16, :] = value.astype(BF16)
-        slot += source.shape[1]
-    table[...] = nn(pieces[0], lanes[...]) + nn(pieces[1], lanes[...]) + nn(pieces[2], lanes[...])
+        return jnp.where(index == 0, mixed, source[index])
+
+    values = [
+        window(one, 2 * band - 1), window(one, 2 * band), window(one, 2 * band + 1), window(two, band)
+    ]
+    heads = sum(value.shape[0] for value in values)
+    for level in range(2):
+        slot = 0
+        for value in values:
+            high = value.astype(BF16).astype(F32)
+            low = value - high
+            for h in range(0, value.shape[0], 2):
+                for piece, taken in enumerate((high, low)):
+                    at = 0
+                    for start, stop in SPANS[level]:
+                        chosen = rows[level, :, start:stop] > 0.0
+                        pair = [
+                            jnp.where(chosen, taken[h + i : h + i + 1, start:stop], 0.0) for i in range(2)
+                        ]
+                        pieces[piece, (slot + h) * 8 : (slot + h) * 8 + 16, at : at + stop - start] = (
+                            jnp.concatenate(pair, axis=0).astype(BF16)
+                        )
+                        at += stop - start
+            slot += value.shape[0]
+        total = None
+        for piece in range(2):
+            at = 0
+            for start, stop in SPANS[level]:
+                term = nn(pieces[piece, :, at : at + stop - start], lanes[start:stop, :])
+                total = term if total is None else total + term
+                at += stop - start
+        for h in range(heads):
+            table[h, level * 8 : level * 8 + 8, :] = total[h * 8 : h * 8 + 8]
 
     for base, count, groups, targets in (
         (0, 3, GROUPS_ONE, (first_ref, second_ref)),
@@ -203,10 +290,10 @@
             for index, (start, heads) in enumerate(groups):
                 target = targets[index]
                 place = row if count == 3 else index
-                low = [(base + row * 6 + start + h) * 16 for h in range(heads)]
+                which = [base + row * 6 + start + h for h in range(heads)]
                 for o2 in range(WLON):
                     left = (WLON - 1 - o2) * COLUMN
-                    piece = [table[at : at + COLUMN, left : left + WINDOW] for at in low]
+                    piece = [table[h, 2 : 2 + COLUMN, left : left + WINDOW] for h in which]
                     target[place, o2 * COLUMN : (o2 + 1) * COLUMN, :] = jnp.concatenate(piece, axis=1)
 
 
@@ -220,10 +307,10 @@
             jax.ShapeDtypeStruct((3, WINDOW, 576), F32),
         ),
         scratch_shapes=[
-            pltpu.VMEM((3, 480, operands[1].shape[2]), BF16),
-            pltpu.VMEM((480, REL * COLUMN), F32),
+            pltpu.VMEM((2, 240, 1920), BF16),
+            pltpu.VMEM((30, 16, REL * COLUMN), F32),
         ],
-        compiler_params=pltpu.CompilerParams(vmem_limit_bytes=VMEM_BYTES),
+        **params(7, 24),
         name="bias_expand",
     )(*operands)
 
@@ -238,7 +325,9 @@
 
 def pack(tokens, cot):
     shape = jax.ShapeDtypeStruct((12, 24, 2 * C1), BF16)
-    return pl.pallas_call(pack_kernel, out_shape=(shape, shape), name="pack")(tokens, cot)
+    return pl.pallas_call(
+        pack_kernel, out_shape=(shape, shape), name="pack", **params(2, 8)
+    )(tokens, cot)
 
 
 def put(packed, base, value):
@@ -265,15 +354,16 @@
     return jnp.concatenate(lanes, axis=1).astype(F32)
 
 
-def send_halves(ids, packed, mine_ref, theirs_ref, sems):
-    copies = [
-        pltpu.make_async_copy(packed.at[ids[2]], mine_ref, sems.at[0]),
-        pltpu.make_async_copy(packed.at[1 - ids[2]], theirs_ref, sems.at[1]),
-    ]
-    for copy in copies:
-        copy.start()
-    for copy in copies:
-        copy.wait()
+def send_half(ids, packed, half, mine_ref, theirs_ref, sems, start):
+    for target, own in ((mine_ref, half), (theirs_ref, 1 - half)):
+
+        @pl.when(ids[2] == own)
+        def _():
+            copy = pltpu.make_async_copy(packed.at[half], target, sems.at[half])
+            if start:
+                copy.start()
+            else:
+                copy.wait()
 
 
 def upper_kernel(
@@ -308,28 +398,33 @@
 
     @pl.loop(0, 3)
     def _(wr):
-        for wc in range(3):
-            rows = slice(wc * WINDOW, (wc + 1) * WINDOW)
-            for start, heads in GROUPS_ONE:
-                lanes = slice(start * HEAD, (start + heads) * HEAD)
-                bias = bias_a[wr] if heads == 4 else bias_b[wr]
-                att_ref[wr, rows, lanes] = attend(
-                    q_ref[wr, rows, lanes], k_ref[wr, rows, lanes], v_ref[wr, rows, lanes],
-                    bias, mask, mask_t, fold, heads,
-                )[0].astype(BF16)
+        places = [
+            (slice(wc * WINDOW, (wc + 1) * WINDOW), slice(start * HEAD, (start + heads) * HEAD), heads)
+            for wc in range(3)
+            for start, heads in GROUPS_ONE
+        ]
+        parts = [
+            (
+                q_ref[wr, rows, lanes], k_ref[wr, rows, lanes], v_ref[wr, rows, lanes],
+                bias_a[wr] if heads == 4 else bias_b[wr], heads,
+            )
+            for rows, lanes, heads in places
+        ]
+        taken, _ = attend(parts, mask, mask_t, fold)
+        for (rows, lanes, heads), value in zip(places, taken):
+            att_ref[wr, rows, lanes] = value.astype(BF16)
 
     xm_ref[...] = nn(gather[0], xw_ref[0]) + nn(gather[1], xw_ref[1]) + nn(gather[2], xw_ref[2])
     am_ref[...] = (
         nn(gather[0], att_ref[0]) + nn(gather[1], att_ref[1]) + nn(gather[2], att_ref[2])
     ).astype(BF16)
 
-    @pl.loop(0, 4)
-    def _(g):
-        rows = pl.ds(pl.multiple_of(g * WINDOW, WINDOW), WINDOW)
+    for half in range(2):
+        rows = slice(half * 288, (half + 1) * 288)
         middle = xm_ref[rows, :] + nn(am_ref[rows, :], proj_one[...])
         normed = layer_norm(middle)[0].astype(BF16)
         active = gelu(nn(normed, up_one[...])).astype(BF16)
-        one_ref[rows, :] = middle + nn(active, down_one[...])
+        one_ref[rows, :] = middle + nt(active, down_one[...])
 
     parts = [one_ref[g * WINDOW : (g + 1) * WINDOW, :] for g in range(4)]
     average = sum(jnp.sum(part, axis=-1, keepdims=True) for part in parts) / (4 * C1)
@@ -344,15 +439,14 @@
     normed_full, scale = layer_norm(grid)
     normed = normed_full.astype(BF16)
     q, k, v = (nn(normed, qkv_two[:, j * C2 : (j + 1) * C2]).astype(BF16) for j in range(3))
-    attended = []
-    for index, (start, heads) in enumerate(GROUPS_TWO):
-        lanes = slice(start * HEAD, (start + heads) * HEAD)
-        taken, chances = attend(
-            q[:, lanes], k[:, lanes], v[:, lanes], bias_two[index], mask, mask_t, fold, heads
-        )
-        p_ref[index] = chances
-        attended.append(taken.astype(BF16))
-    attended = jnp.concatenate(attended, axis=1)
+    lanes_of = [slice(start * HEAD, (start + heads) * HEAD) for start, heads in GROUPS_TWO]
+    taken, chances = attend(
+        [(q[:, at], k[:, at], v[:, at], bias_two[index], 4) for index, at in enumerate(lanes_of)],
+        mask, mask_t, fold,
+    )
+    for index in range(3):
+        p_ref[index] = chances[index]
+    attended = jnp.concatenate([value.astype(BF16) for value in taken], axis=1)
     middle = grid + nn(attended, proj_two[...])
     normed_two_full, scale_two = layer_norm(middle)
     normed_two = normed_two_full.astype(BF16)
@@ -371,22 +465,21 @@
     put(packed, 4608, tn(active, grad_low).astype(BF16))
     grad_raised = (nt(grad_low, down_two[...]) * slope).astype(BF16)
     put(packed, 0, tn(normed_two, grad_raised).astype(BF16))
+    send_half(ids, packed, 0, mine_ref, theirs_ref, sems, True)
     grad_middle = grad + layer_norm_back(nt(grad_raised, up_two[...]), normed_two_full, scale_two)
     grad_middle_low = grad_middle.astype(BF16)
     put(packed, 9216, tn(attended, grad_middle_low).astype(BF16))
     grad_attended = nt(grad_middle_low, proj_two[...]).astype(BF16)
-    pieces = []
-    for index, (start, heads) in enumerate(GROUPS_TWO):
-        lanes = slice(start * HEAD, (start + heads) * HEAD)
-        pieces.append(
-            attend_back(
-                q[:, lanes], k[:, lanes], v[:, lanes], p_ref[index], grad_attended[:, lanes],
-                mask, mask_t, fold, heads,
-            )
-        )
+    pieces = attend_back(
+        [
+            (q[:, at], k[:, at], v[:, at], p_ref[index], grad_attended[:, at], 4)
+            for index, at in enumerate(lanes_of)
+        ],
+        mask, mask_t, fold,
+    )
     grad_normed = None
     for j in range(3):
-        part = jnp.concatenate([piece[j].astype(BF16) for piece in pieces], axis=1)
+        part = jnp.concatenate([value.astype(BF16) for value in pieces[j]], axis=1)
         put(packed, 10368 + j * 1152, tn(normed, part).astype(BF16))
         term = nt(part, qkv_two[:, j * C2 : (j + 1) * C2])
         grad_normed = term if grad_normed is None else grad_normed + term
@@ -396,6 +489,7 @@
     grad_merge = [tn(merged_low[g], grad_grid).astype(BF16) for g in range(4)]
     put(packed, 13824, jnp.concatenate(grad_merge, axis=0))
     packed[1, 16128 - packed.shape[1] :, :] = jnp.zeros((256, LANES), BF16)
+    send_half(ids, packed, 1, mine_ref, theirs_ref, sems, True)
     for g in range(4):
         grad_parts.append(nt(grad_grid, merge[g * C1 : (g + 1) * C1, :]))
     first = sum(jnp.sum(part, axis=-1, keepdims=True) for part in grad_parts) / (4 * C1)
@@ -410,7 +504,8 @@
     lon_ref[...] = sent[: STRIPS[0]]
     lat_ref[...] = sent[STRIPS[0] : STRIPS[0] + STRIPS[1]]
     corner_ref[...] = sent[STRIPS[0] + STRIPS[1] :]
-    send_halves(ids, packed, mine_ref, theirs_ref, sems)
+    for half in range(2):
+        send_half(ids, packed, half, mine_ref, theirs_ref, sems, False)
 
 
 def packed_shape(block):
@@ -455,28 +550,32 @@
             pltpu.VMEM((2, CHIPS * UPPER_BLOCK, LANES), BF16),
             pltpu.SemaphoreType.DMA((2,)),
         ],
-        compiler_params=pltpu.CompilerParams(vmem_limit_bytes=VMEM_BYTES),
+        **params(25, 40),
         name="upper",
     )(*operands)
 
 
+def halves(value):
+    high = value.astype(BF16)
+    return high, (value - high.astype(F32)).astype(BF16)
+
+
 def lower_kernel(
-    ids, xw, own, lon, lat, corner, bias_a, bias_b,
+    ids, xw, out_two, own, lon, lat, corner, bias_a, bias_b,
     qkv_one, proj_one, up_one, down_one,
-    back_own, back_strips, mask_ref, mask_t_ref, fold_ref,
-    out_ref, mine_ref, theirs_ref,
+    back_own, back_strips, to_tokens, to_two, mask_ref, mask_t_ref, fold_ref,
+    out_ref, out_two_ref, lon_ref, lat_ref, corner_ref, mine_ref, theirs_ref,
     gs_ref, normed_ref, full_ref, scale_ref, q_ref, k_ref, v_ref, pa_ref, pb_ref, att_ref,
-    normed_two_ref, act_ref, raised_ref, gm_ref, gml_ref, gq_ref, gk_ref, gv_ref,
+    normed_two_ref, act_ref, raised_ref, gm_ref, gml_ref, ga_ref, gq_ref, gk_ref, gv_ref, gx_ref,
     packed, sems,
 ):
     mask, mask_t, fold = mask_ref[...], mask_t_ref[...], fold_ref[...]
     arrived = jnp.concatenate([lon[...], lat[...], corner[...]], axis=0)
     gs_ref[...] = nn(back_own[...], own[...]) + nn(back_strips[...], arrived)
-
-    for row in range(2):
-        rows = slice(row * 288, (row + 1) * 288)
-        cells = xw[1 + row, :288, :].astype(F32)
-        full, scale = layer_norm(cells)
+    row_slices = [slice(row * 288, (row + 1) * 288) for row in range(2)]
+
+    for row, rows in enumerate(row_slices):
+        full, scale = layer_norm(xw[1 + row, :288, :].astype(F32))
         full_ref[rows, :] = full
         scale_ref[rows, :] = scale
         normed = full.astype(BF16)
@@ -486,71 +585,92 @@
         k_ref[rows, :] = projected[:, C1 : 2 * C1]
         v_ref[rows, :] = projected[:, 2 * C1 :]
 
+    def places(row):
+        return [
+            (
+                pl.ds(pl.multiple_of(row * 288 + wc * WINDOW, WINDOW), WINDOW),
+                slice(start * HEAD, (start + heads) * HEAD),
+                heads,
+                (pa_ref if heads == 4 else pb_ref, row * 2 + wc),
+                bias_a if heads == 4 else bias_b,
+            )
+            for wc in range(2)
+            for start, heads in GROUPS_ONE
+        ]
+
     @pl.loop(0, 2)
     def _(row):
-        for wc in range(2):
-            window = row * 2 + wc
-            rows = pl.ds(pl.multiple_of(row * 288 + wc * WINDOW, WINDOW), WINDOW)
-            for start, heads in GROUPS_ONE:
-                lanes = slice(start * HEAD, (start + heads) * HEAD)
-                bias = bias_a[1 + row] if heads == 4 else bias_b[1 + row]
-                taken, chances = attend(
-                    q_ref[rows, lanes], k_ref[rows, lanes], v_ref[rows, lanes],
-                    bias, mask, mask_t, fold, heads,
-                )
-                att_ref[rows, lanes] = taken.astype(BF16)
-                if heads == 4:
-                    pa_ref[window] = chances
-                else:
-                    pb_ref[window] = chances
-
-    @pl.loop(0, 4)
-    def _(window):
-        rows = pl.ds(pl.multiple_of(window * WINDOW, WINDOW), WINDOW)
-        cells = xw[1 + window // 2, pl.ds(pl.multiple_of(window % 2 * WINDOW, WINDOW), WINDOW), :]
-        middle = cells.astype(F32) + nn(att_ref[rows, :], proj_one[...])
+        parts = [
+            (q_ref[rows, at], k_ref[rows, at], v_ref[rows, at], bias[1 + row], heads)
+            for rows, at, heads, _, bias in places(row)
+        ]
+        taken, chances = attend(parts, mask, mask_t, fold)
+        for (rows, at, _, (kept, window), _), value, chance in zip(places(row), taken, chances):
+            att_ref[rows, at] = value.astype(BF16)
+            kept[window] = chance
+
+    for row, rows in enumerate(row_slices):
+        middle = xw[1 + row, :288, :].astype(F32) + nn(att_ref[rows, :], proj_one[...])
         full, scale = layer_norm(middle)
         normed_two = full.astype(BF16)
         normed_two_ref[rows, :] = normed_two
         active, slope = gelu_both(nn(normed_two, up_one[...]))
         act_ref[rows, :] = active.astype(BF16)
         grad = gs_ref[rows, :]
-        grad_raised = (nt(grad.astype(BF16), down_one[...]) * slope).astype(BF16)
+        grad_raised = (nn(grad.astype(BF16), down_one[...]) * slope).astype(BF16)
         raised_ref[rows, :] = grad_raised
         grad_middle = grad + layer_norm_back(nt(grad_raised, up_one[...]), full, scale)
         gm_ref[rows, :] = grad_middle
         low = grad_middle.astype(BF16)
         gml_ref[rows, :] = low
-        grad_attended = nt(low, proj_one[...]).astype(BF16)
-        for start, heads in GROUPS_ONE:
-            lanes = slice(start * HEAD, (start + heads) * HEAD)
-            chances = pa_ref[window] if heads == 4 else pb_ref[window]
-            gq, gk, gv = attend_back(
-                q_ref[rows, lanes], k_ref[rows, lanes], v_ref[rows, lanes], chances,
-                grad_attended[:, lanes], mask, mask_t, fold, heads,
-            )
-            gq_ref[rows, lanes] = gq.astype(BF16)
-            gk_ref[rows, lanes] = gk.astype(BF16)
-            gv_ref[rows, lanes] = gv.astype(BF16)
+        ga_ref[rows, :] = nt(low, proj_one[...]).astype(BF16)
+
+    @pl.loop(0, 2)
+    def _(row):
+        parts = [
+            (q_ref[rows, at], k_ref[rows, at], v_ref[rows, at], kept[window], ga_ref[rows, at], heads)
+            for rows, at, heads, (kept, window), _ in places(row)
+        ]
+        grads = attend_back(parts, mask, mask_t, fold)
+        for target, values in zip((gq_ref, gk_ref, gv_ref), grads):
+            for (rows, at, _, _, _), value in zip(places(row), values):
+                target[rows, at] = value.astype(BF16)
+
+    normed = normed_ref[...]
+    grads = [tn(normed, ref[...]) for ref in (gq_ref, gk_ref, gv_ref)]
+    grads = jnp.concatenate(grads + [tn(att_ref[...], gml_ref[...])], axis=1)
+    put(packed, 0, grads.astype(BF16))
+    put(packed, 1152, tn(normed_two_ref[...], raised_ref[...]).astype(BF16))
+    put(packed, 2304, tn(gs_ref[...].astype(BF16), act_ref[...]).astype(BF16))
+    packed[1, 3456 - packed.shape[1] :, :] = jnp.zeros((640, LANES), BF16)
+    for half in range(2):
+        send_half(ids, packed, half, mine_ref, theirs_ref, sems, True)
+
+    for rows in row_slices:
         grad_normed = (
             nt(gq_ref[rows, :], qkv_one[:, :C1])
             + nt(gk_ref[rows, :], qkv_one[:, C1 : 2 * C1])
             + nt(gv_ref[rows, :], qkv_one[:, 2 * C1 :])
         )
-        out_ref[rows, :] = grad_middle + layer_norm_back(
+        gx_ref[rows, :] = gm_ref[rows, :] + layer_norm_back(
             grad_normed, full_ref[rows, :], scale_ref[rows, :]
         )
-
-    normed = normed_ref[...]
-    grads = [tn(normed, ref[...]) for ref in (gq_ref, gk_ref, gv_ref)]
-    grads = jnp.concatenate(grads + [tn(att_ref[...], gml_ref[...])], axis=1)
-    put(packed, 0, grads.astype(BF16))
-    put(packed, 1152, tn(normed_two_ref[...], raised_ref[...]).astype(BF16))
-    low = gs_ref[...].astype(BF16)
-    grads = [tn(act_ref[:, j * C1 : (j + 1) * C1], low) for j in range(4)]
-    put(packed, 2304, jnp.concatenate(grads, axis=1).astype(BF16))
-    packed[1, 3456 - packed.shape[1] :, :] = jnp.zeros((640, LANES), BF16)
-    send_halves(ids, packed, mine_ref, theirs_ref, sems)
+    high, low = halves(gx_ref[...])
+    cells = jnp.concatenate(
+        [nn(to_tokens[level], high) + nn(to_tokens[level], low) for level in range(2)], axis=1
+    )
+    high, low = halves(out_two[...])
+    two = nn(to_two[...], high) + nn(to_two[...], low)
+    out_ref[...] = cells[:288]
+    out_two_ref[...] = two[:144]
+    at = 288
+    for kind, ref in enumerate((lon_ref, lat_ref, corner_ref)):
+        count = SHIFT_TOKENS[kind]
+        ref[:count, :] = cells[at : at + count]
+        ref[count:, :] = two[144 + kind * 40 : 144 + (kind + 1) * 40]
+        at += count
+    for half in range(2):
+        send_half(ids, packed, half, mine_ref, theirs_ref, sems, False)
 
 
 def lower(*operands):
@@ -559,9 +679,13 @@
     return pl.pallas_call(
         lower_kernel,
         in_specs=specs(len(operands)),
-        out_specs=out_specs(3, 2),
+        out_specs=out_specs(7, 2),
         out_shape=(
-            shape((576, C1), F32), packed_shape(LOWER_BLOCK), packed_shape(LOWER_BLOCK)
+            shape((288, C2), F32),
+            shape((144, C2), F32),
+            *(shape((count, C2), F32) for count in SHIFT),
+            packed_shape(LOWER_BLOCK),
+            packed_shape(LOWER_BLOCK),
         ),
         scratch_shapes=[
             pltpu.VMEM((576, C1), F32),
@@ -576,60 +700,88 @@
             pltpu.VMEM((576, 768), BF16),
             pltpu.VMEM((576, 768), BF16),
             pltpu.VMEM((576, C1), F32),
-            wide, wide, wide, wide,
+            wide, wide, wide, wide, wide,
+            pltpu.VMEM((576, C1), F32),
             pltpu.VMEM((2, CHIPS * LOWER_BLOCK, LANES), BF16),
             pltpu.SemaphoreType.DMA((2,)),
         ],
-        compiler_params=pltpu.CompilerParams(vmem_limit_bytes=VMEM_BYTES),
+        **params(15, 60),
         name="lower",
     )(*operands)
 
 
-def call(kernel, name, out_shape, operands, scratch=()):
+def call(kernel, name, microseconds, vmem, out_shape, operands, scratch=()):
     return pl.pallas_call(
         kernel,
         in_specs=specs(len(operands)),
         out_shape=out_shape,
         scratch_shapes=scratch,
-        compiler_params=pltpu.CompilerParams(vmem_limit_bytes=VMEM_BYTES),
         name=name,
+        **params(microseconds, vmem),
     )(*operands)
 
 
-def chip_kernel(ids, mine_two, theirs_two, mine_one, theirs_one, out):
-    for low, mine, theirs in ((0, mine_two, theirs_two), (UPPER_BLOCK, mine_one, theirs_one)):
-        rows = mine.shape[0] // CHIPS
-        for block in range(CHIPS):
-            at = slice(block * rows, (block + 1) * rows)
-            value = mine[at].astype(F32) + theirs[at].astype(F32)
-            out[block, low : low + rows, :] = value.astype(BF16)
+def chip_kernel(ids, mine, theirs, out):
+    rows = out.shape[1]
+    for block in range(CHIPS):
+        at = slice(block * rows, (block + 1) * rows)
+        out[block] = (mine[at].astype(F32) + theirs[at].astype(F32)).astype(BF16)
+
+
+def total(blocks, low, rows):
+    value = blocks[0, low : low + rows, :].astype(F32)
+    for block in range(1, CHIPS):
+        value = value + blocks[block, low : low + rows, :].astype(F32)
+    return value.astype(BF16)
+
+
+def middle_kernel(ids, blocks, packed_one, out):
+    value = total(blocks, 0, UPPER_BLOCK)
+    for block in range(CHIPS):
+        out[block, :UPPER_BLOCK, :] = value
+        out[block, UPPER_BLOCK:, :] = packed_one[block]
 
 
 def total_kernel(ids, blocks, out):
-    value = blocks[0].astype(F32)
-    for block in range(1, CHIPS):
-        value = value + blocks[block].astype(F32)
-    value = value.astype(BF16)
+    value = total(blocks, UPPER_BLOCK, LOWER_BLOCK)
     for block in range(CHIPS):
         out[block] = value
 
 
-def last_kernel(factor, ids, mine, theirs, qkv, proj, up, down, merge, qkv_two, proj_two, up_two, down_two, upper, lower):
+def join_halves(ids, mine, theirs, packed):
+    rows = packed.shape[1] // CHIPS
     for half, source in ((ids[2], mine), (1 - ids[2], theirs)):
         for block in range(CHIPS):
-            upper[half, block * UPPER_BLOCK : (block + 1) * UPPER_BLOCK, :] = source[block, :UPPER_BLOCK, :]
-            lower[half, block * LOWER_BLOCK : (block + 1) * LOWER_BLOCK, :] = source[block, UPPER_BLOCK:, :]
-    for out, base in ((up_two, 0), (down_two, 4608), (proj_two, 9216), (merge, 13824)):
-        out[...] = take(upper, base, out.shape[0], out.shape[1] // LANES) * factor
+            packed[half, block * rows : (block + 1) * rows, :] = source[block, :rows, :]
+
+
+def upper_last_kernel(factor, ids, mine, theirs, merge, qkv, proj, up, down, packed):
+    join_halves(ids, mine, theirs, packed)
+    for out, base in ((up, 0), (down, 4608), (proj, 9216), (merge, 13824)):
+        out[...] = take(packed, base, out.shape[0], out.shape[1] // LANES) * factor
     for j in range(3):
-        qkv_two[:, j * C2 : (j + 1) * C2] = take(upper, 10368 + j * 1152, C2, 3) * factor
-    joined = take(lower, 0, C1, 6) * factor
+        qkv[:, j * C2 : (j + 1) * C2] = take(packed, 10368 + j * 1152, C2, 3) * factor
+
+
+def lower_last_kernel(factor, ids, mine, theirs, qkv, proj, up, down, packed):
+    join_halves(ids, mine, theirs, packed)
+    joined = take(packed, 0, C1, 6) * factor
     qkv[...] = joined[:, : 3 * C1]
     proj[...] = joined[:, 3 * C1 :]
-    up[...] = take(lower, 1152, C1, 6) * factor
-    joined = take(lower, 2304, C1, 6) * factor
-    for j in range(4):
-        down[j * C1 : (j + 1) * C1, :] = joined[:, j * C1 : (j + 1) * C1]
+    up[...] = take(packed, 1152, C1, 6) * factor
+    down[...] = take(packed, 2304, C1, 6) * factor
+
+
+def assemble_kernel(ids, own, own_two, lon, lat, corner, place, place_two, tokens, two):
+    high, low = halves(jnp.concatenate([lon[...], lat[...], corner[...]], axis=0))
+    cells = own[...] + (nn(place[...], high) + nn(place[...], low))
+    for row in range(12):
+        tokens[row] = cells[row * 24 : (row + 1) * 24]
+    cells = own_two[...] + (nn(place_two[...], high) + nn(place_two[...], low))
+    for row in range(6):
+        for level in range(2):
+            at = level * 72 + row * 12
+            two[row, :, level * C2 : (level + 1) * C2] = cells[at : at + 12]
 
 
 def per_device(
@@ -645,7 +797,7 @@
     to_right = [(i, (i + 1) % lons) for i in range(lons)]
     from_up = [(i, (i + 1) % lats) for i in range(lats)]
     to_up = [((i + 1) % lats, i) for i in range(lats)]
-    other_core = [(i, 1 - i) for i in range(2)]
+    down_one = down_one.T
     corner_in = [
         (i * lons + (j + 1) % lons, (i + 1) % lats * lons + j) for i in range(lats) for j in range(lons)
     ]
@@ -668,42 +820,56 @@
     lon_strip = lax.ppermute(lon_strip, lon, to_right)
     lat_strip = lax.ppermute(lat_strip, "lat", to_up)
     corner = lax.ppermute(corner, both, corner_out)
+    other_core = [(i, 1 - i) for i in range(2)]
     theirs_two = lax.ppermute(theirs_two, "core", other_core)
-    grad_cells, mine_one, theirs_one = lower(
-        ids, xw, grad_own, lon_strip, lat_strip, corner, bias_a, bias_b,
+    result = lambda *dims: jax.ShapeDtypeStruct(dims, F32)
+    blocks = lambda rows: jax.ShapeDtypeStruct((CHIPS, rows, LANES), BF16)
+    chips = ("lat", "chip")
+    packed_two = call(chip_kernel, "chip_two", 3, 16, blocks(UPPER_BLOCK), (ids, mine_two, theirs_two))
+    packed_two, lon_strip, lat_strip, corner = lax.optimization_barrier(
+        (packed_two, lon_strip, lat_strip, corner)
+    )
+    packed_two = lax.all_to_all(packed_two, chips, 0, 0, tiled=True)
+
+    to_tokens, to_two, place, place_two = output_constants()
+    own_cells, own_two, lon_strip, lat_strip, corner, mine_one, theirs_one = lower(
+        ids, xw, out_two, grad_own, lon_strip, lat_strip, corner, bias_a, bias_b,
         qkv_one, proj_one, up_one, down_one,
-        back_own, back_strips, mask, mask_t, fold,
+        back_own, back_strips, to_tokens, to_two, mask, mask_t, fold,
     )
     theirs_one = lax.ppermute(theirs_one, "core", other_core)
-    result = jax.ShapeDtypeStruct
-    blocks = result((CHIPS, UPPER_BLOCK + LOWER_BLOCK, LANES), BF16)
-    packed = call(chip_kernel, "chip", blocks, (ids, mine_two, theirs_two, mine_one, theirs_one))
-    packed = lax.all_to_all(packed, ("lat", "chip"), 0, 0, tiled=True)
-    packed = call(total_kernel, "total", blocks, (ids, packed))
-    packed = lax.all_to_all(packed, ("lat", "chip"), 0, 0, tiled=True)
-    weights = (
-        qkv_one, proj_one, up_one, down_one, merge_weight, qkv_two, proj_two, up_two, down_two
-    )
-    sums = call(
-        functools.partial(last_kernel, factor), "last", tuple(result(w.shape, F32) for w in weights),
-        (ids, packed, lax.ppermute(packed, "core", other_core)),
-        [
-            pltpu.VMEM((2, CHIPS * UPPER_BLOCK, LANES), BF16),
-            pltpu.VMEM((2, CHIPS * LOWER_BLOCK, LANES), BF16),
-        ],
-    )
-
-    def shift_back(value, half_rows, half_cols):
-        arrived = lax.ppermute(value[:, value.shape[1] - half_cols :], lon, to_right)
-        value = jnp.concatenate([arrived, value[:, : value.shape[1] - half_cols]], axis=1)
-        arrived = lax.ppermute(value[:half_rows], "lat", to_up)
-        return jnp.concatenate([value[half_rows:], arrived], axis=0)
-
-    out_two = out_two.reshape(12, LEVELS, WLAT, C2).transpose(2, 0, 1, 3).reshape(6, 12, LEVELS * C2)
-    out_two = shift_back(out_two, WLAT // 2, WLON // 2)[None]
-    grad_cells = grad_cells.reshape(2, 24, LEVELS, WLAT, C1).transpose(0, 3, 1, 2, 4)
-    grad_tokens = shift_back(grad_cells.reshape(12, 24, LEVELS * C1), WLAT // 2, WLON // 2)[None]
-    return (out_two, grad_tokens, *sums)
+    packed_one = call(chip_kernel, "chip_one", 1, 16, blocks(LOWER_BLOCK), (ids, mine_one, theirs_one))
+    packed_two, packed_one = lax.optimization_barrier((packed_two, packed_one))
+    merged = call(
+        middle_kernel, "middle", 2, 16, blocks(UPPER_BLOCK + LOWER_BLOCK), (ids, packed_two, packed_one)
+    )
+    merged = lax.all_to_all(merged, chips, 0, 0, tiled=True)
+    summed_one = call(total_kernel, "total_one", 1, 16, blocks(LOWER_BLOCK), (ids, merged))
+    gathered_one = lax.all_to_all(summed_one, chips, 0, 0, tiled=True)
+
+    sums_two = call(
+        functools.partial(upper_last_kernel, factor), "last_two", 5, 32,
+        tuple(result(*w.shape) for w in (merge_weight, qkv_two, proj_two, up_two, down_two)),
+        (ids, merged, lax.ppermute(merged, "core", other_core)),
+        [pltpu.VMEM((2, CHIPS * UPPER_BLOCK, LANES), BF16)],
+    )
+    lon_strip = lax.ppermute(lon_strip, lon, to_right)
+    lat_strip = lax.ppermute(lat_strip, "lat", to_up)
+    corner = lax.ppermute(corner, both, corner_out)
+    grad_tokens, out_two = call(
+        assemble_kernel, "assemble", 3, 8, (result(12, 24, 2 * C1), result(6, 12, 2 * C2)),
+        (ids, own_cells, own_two, lon_strip, lat_strip, corner, place, place_two),
+    )
+    gathered_one, grad_tokens, out_two, *sums_two = lax.optimization_barrier(
+        (gathered_one, grad_tokens, out_two, *sums_two)
+    )
+    sums_one = call(
+        functools.partial(lower_last_kernel, factor), "last_one", 2, 32,
+        tuple(result(*w.shape) for w in (qkv_one, proj_one, up_one, down_one)),
+        (ids, gathered_one, lax.ppermute(gathered_one, "core", other_core)),
+        [pltpu.VMEM((2, CHIPS * LOWER_BLOCK, LANES), BF16)],
+    )
+    return (out_two[None], grad_tokens[None], *sums_one[:3], sums_one[3].T, *sums_two)
 
 
 def solution(mesh):

time: 210 us -> 165 us (0.79); the launches traced: 207 us -> 164 us
  blocking collectives: 81 us -> 39.1 us
  Pallas kernels: 76.4 us -> 53.8 us
  starting transfers between devices: 22.3 us -> 37.6 us
  local copies, waits for them, and re-layouts: 12.7 us -> 19.8 us
  other arithmetic: 2.51 us -> 0.08 us
    all_to_all x2 -> x1, blocking collectives: 81 us -> 39.1 us  [per_device(): merged = lax.all_to_all(merged, chips, 0, 0, tiled=True)]
    all_to_all x0 -> x2, starting transfers between devices: none -> 15.3 us  [the longest x1 9.46 us: per_device(): packed_two = lax.all_to_all(packed_two, chips, 0, 0, tiled=True)]
    unnamed x23 -> x97, local copies, waits for them, and re-layouts: 7.91 us -> 19.8 us
    all_to_all x0 -> x2, waiting for transfers between devices: none -> 9.93 us  [the longest x1 9.92 us: per_device(): packed_two = lax.all_to_all(packed_two, chips, 0, 0, tiled=True)]
    pallas_call x1, Pallas kernels: 29 us -> 20.1 us  [upper(): pl.pallas_call(upper_kernel, in_specs=specs(len(operands)), out_specs=out...]
    pallas_call x1, Pallas kernels: 11 us -> 3.65 us  [expand_bias(): pl.pallas_call(bias_kernel, in_specs=specs(len(operands)), out_shape=(jax...]
    ppermute x1, starting transfers between devices: 6.82 us -> 1.23 us  [per_device(): diag = lax.ppermute(for_down, both, corner_in)]
    ppermute x1 -> x2, waiting for transfers between devices: 4.96 us -> 0.46 us  [per_device(): corner = lax.ppermute(corner, both, corner_out)]
  transfers between devices with their start and end apart: 13 -> 15, of which waited for: 5 -> 4; matrix products, arithmetic and copies ran while one was open for 5% -> 1% of each run, Pallas kernels for 15% -> 18%
where the time goes in v2:
time: 165 us; the launch traced here: 164 us
  Pallas kernels  53.8 us (33%)
  blocking collectives  39.1 us (24%)
  starting transfers between devices  37.6 us (23%)
  local copies, waits for them, and re-layouts  19.8 us (12%)
  waiting for transfers between devices  12.9 us (8%)
    all_to_all x1, blocking collectives, per_device(): merged = lax.all_to_all(merged, chips, 0, 0, tiled=True)  39.1 us
    pallas_call x1, Pallas kernels, upper(): pl.pallas_call(upper_kernel, in_specs=specs(len(operands)), out_specs=out...  20.1 us
    unnamed x97, local copies, waits for them, and re-layouts  19.8 us
    pallas_call x1, Pallas kernels, lower(): pl.pallas_call(lower_kernel, in_specs=specs(len(operands)), out_specs=out...  15.7 us
    pallas_call x7, Pallas kernels, call(): pl.pallas_call(kernel, in_specs=specs(len(operands)), out_shape=out_shape...  13.6 us
    all_to_all x1, waiting for transfers between devices, per_device(): packed_two = lax.all_to_all(packed_two, chips, 0, 0, tiled=True)  9.92 us
    all_to_all x1, starting transfers between devices, per_device(): packed_two = lax.all_to_all(packed_two, chips, 0, 0, tiled=True)  9.46 us
    all_to_all x1, starting transfers between devices, per_device(): gathered_one = lax.all_to_all(summed_one, chips, 0, 0, tiled=True)  5.87 us
  transfers between devices with their start and end apart: 15, of which 4 were waited for; matrix products, arithmetic and copies ran while one was open for 1% of the time, Pallas kernels for 18%

profile of v2, /device:TPU:1, one launch (start us, length us, event | category | flops | bytes accessed | tf_op | source)
XLA Modules:
  0.0 164.5 jit_solution(9434116377583844291)
XLA Ops:
  0.7 0.9 copy-done.13
  1.6 0.9 copy-done.15
  2.5 0.8 pack.1
  3.3 4.4 %collective-permute-start.1 = (bf16[12,24,384]{2,1,0:T(8,128)(2,1)}, bf16[12,24,384]{2,1,0:T(8,128)(2,1)S(1)}, u32[]{:S(2)}, u32[]{:S(2)}) collective-permute-start(bf16[12,24,384]{2,1,0:T(8,128)(2,1)} %get-tuple-element.57), channel_id=1, source_target_pairs={{0,16},{16,32},{32,48},{48,64},{64,80},{80,96},{96,112},{112,0},{1... | collective-permute-start | bytes 663560 | tf_op jit(solution)/shard_map/ppermute | solution.py:809
  7.7 1.2 collective-permute-start.2
  8.9 2.8 %collective-permute-start = (bf16[12,24,384]{2,1,0:T(8,128)(2,1)}, bf16[12,24,384]{2,1,0:T(8,128)(2,1)}, u32[]{:S(2)}, u32[]{:S(2)}) collective-permute-start(bf16[12,24,384]{2,1,0:T(8,128)(2,1)} %get-tuple-element.56), channel_id=1, source_target_pairs={{1,0},{2,1},{3,2},{4,3},{5,4},{6,5},{7,6},{8,7},{9,8},{10,9},{11,1... | collective-permute-start | bytes 663560 | tf_op jit(solution)/shard_map/ppermute | solution.py:808
  11.8 0.1 pad_add_fusion.ids
  11.8 1.5 copy-done.4
  13.3 1.7 %copy-done.22 = bf16[3312,276]{1,0:T(8,128)(2,1)S(1)} copy-done((bf16[3312,276]{1,0:T(8,128)(2,1)S(1)}, bf16[3312,276]{1,0:T(8,128)(2,1)}, u32[]{:S(2)}) %copy-start.22) | copy-done | bytes 1828248
  15.1 0.9 copy-done.26
  16.0 0.0 copy-start.10
  16.0 0.0 copy-start.11
  16.1 0.0 copy-start.16
  16.1 0.0 copy-start.23
  16.1 0.0 copy-start.24
  16.1 0.0 copy-start.25
  16.1 0.0 copy-start.27
  16.1 0.0 copy-start.28
  16.2 0.0 copy-start.30
  16.2 0.0 copy-start.31
  16.2 3.7 %bias_expand.1 = (f32[3,144,576]{2,1,0:T(8,128)S(1)}, f32[3,144,288]{2,1,0:T(8,128)S(1)}, f32[3,144,576]{2,1,0:T(8,128)S(1)}) custom-call(s32[3]{0:T(128)S(1)} %pad_add_fusion.ids, f32[17,6,3312]{2,1,0:T(8,128)S(1)} %copy-done.4, f32[9,12,3312]{2,1,0:T(8,128)S(1)} %copy-done.3, f32[1,3312]{1,0:T(1,128)S(1)} %copy-done.33, f32[2,8,3312]{2,1,0:T(8,128)S(1)} %copy-done.26, ...), custom_call_target="tpu_custom_call" | custom-call | flops 7000000000 | bytes 21000000 | tf_op jit(solution)/shard_map/bias_expand/pallas_call | solution.py:301
  20.1 20.1 %upper.1 = (f32[144,384]{1,0:T(8,128)S(1)}, bf16[3,432,192]{2,1,0:T(8,128)(2,1)S(1)}, bf16[576,192]{1,0:T(8,128)(2,1)S(1)}, bf16[112,192]{1,0:T(8,128)(2,1)S(1)}...) custom-call(s32[3]{0:T(128)S(1)} %pad_add_fusion.ids, ...), custom_call_target="tpu_custom_call" | custom-call | flops 24999999488 | bytes 75000000 | tf_op jit(solution)/shard_map/upper/pallas_call | solution.py:527
  40.2 1.6 collective-permute-start.3
  41.8 1.0 collective-permute-start.4
  42.8 3.3 %collective-permute-start.5 = (bf16[112,192]{1,0:T(8,128)(2,1)S(1)}, bf16[112,192]{1,0:T(8,128)(2,1)S(1)}, u32[]{:S(2)}, u32[]{:S(2)}) collective-permute-start(bf16[112,192]{1,0:T(8,128)(2,1)S(1)} %get-tuple-element.64), channel_id=1, source_target_pairs={{16,0},{32,16},{48,32},{64,48},{80,64},{96,80},{112,96},{0,112},{1... | collective-permute-start | bytes 129032 | tf_op jit(solution)/shard_map/ppermute | solution.py:821
  46.1 0.4 collective-permute-start.6
  46.5 1.6 copy-done.37
  48.1 2.3 %chip_two.1 = bf16[64,128,128]{2,1,0:T(8,128)(2,1)} custom-call(s32[3]{0:T(128)S(1)} %pad_add_fusion.ids, bf16[8192,128]{1,0:T(8,128)(2,1)S(1)} %copy-done.37, bf16[8192,128]{1,0:T(8,128)(2,1)S(1)} %collective-permute-done.3.theirs), custom_call_target="tpu_custom_call" | custom-call | flops 3000000000 | bytes 9000000 | tf_op jit(solution)/shard_map/chip_two/pallas_call | solution.py:714
  50.4 0.5 collective-permute-done.6.corner
  50.9 0.6 copy-done.47
  51.5 0.0 copy-done.45
  51.5 0.0 copy-done.46
  51.5 9.5 %all-to-all-start = ((bf16[64,128,128]{2,1,0:T(8,128)(2,1)}), bf16[64,128,128]{2,1,0:T(8,128)(2,1)S(1)}, u32[]{:S(2)}, u32[]{:S(2)}) async-start(bf16[64,128,128]{2,1,0:T(8,128)(2,1)} %chip_two.1), calls=%async_computation | async-start | bytes 4194304 | tf_op jit(solution)/shard_map/all_to_all | solution.py:832
  61.0 15.7 %lower.1 = (f32[288,384]{1,0:T(8,128)}, f32[144,384]{1,0:T(8,128)}, f32[96,384]{1,0:T(8,128)}, f32[96,384]{1,0:T(8,128)}, f32[64,384]{1,0:T(8,128)}, /*index=5*/...) custom-call(s32[3]{0:T(128)} %copy-done.1, bf16[3,432,192]{2,1,0:T(8,128)(2,1)} %copy-done.42, f32[144,384]{1,0:T(8,128)} %copy-done.44, ...), custom_call_target="tpu_custom_call" | custom-call | flops 15000000512 | bytes 45000000 | tf_op jit(solution)/shard_map/lower/pallas_call | solution.py:679
  76.7 0.3 collective-permute-start.7
  77.1 1.9 %collective-permute-done.7.theirs = bf16[2048,128]{1,0:T(8,128)(2,1)S(1)} collective-permute-done((bf16[2048,128]{1,0:T(8,128)(2,1)}, bf16[2048,128]{1,0:T(8,128)(2,1)S(1)}, u32[]{:S(2)}, u32[]{:S(2)}) %collective-permute-start.7) | collective-permute-done | bytes 524320 | tf_op jit(solution)/shard_map/ppermute | solution.py:840
  78.9 1.0 copy-done.34
  80.0 0.7 chip_one.1.packed_one
  80.7 0.8 copy-done.35
  81.4 9.9 %all-to-all-done.blocks = bf16[64,128,128]{2,1,0:T(8,128)(2,1)S(1)} async-done(((bf16[64,128,128]{2,1,0:T(8,128)(2,1)}), bf16[64,128,128]{2,1,0:T(8,128)(2,1)S(1)}, u32[]{:S(2)}, u32[]{:S(2)}) %all-to-all-start) | async-done | bytes 2097184 | tf_op jit(solution)/shard_map/all_to_all | solution.py:832
  91.4 1.0 copy-done.36
  92.4 0.9 middle.1
  93.3 39.1 %all_to_all.15.blocks.mine = bf16[64,160,128]{2,1,0:T(8,128)(2,1)S(1)} all-to-all(bf16[64,160,128]{2,1,0:T(8,128)(2,1)S(1)} %middle.1), channel_id=1, replica_groups=mesh['lat'=8,'chip'=8,'core'=2] {'lat','chip'}, dimensions={0} | all-to-all | bytes 5242880 | tf_op jit(solution)/shard_map/all_to_all | solution.py:846
  132.4 2.3 %collective-permute-start.11 = (bf16[64,160,128]{2,1,0:T(8,128)(2,1)S(1)}, bf16[64,160,128]{2,1,0:T(8,128)(2,1)}, u32[]{:S(2)}, u32[]{:S(2)}) collective-permute-start(bf16[64,160,128]{2,1,0:T(8,128)(2,1)S(1)} %all_to_all.15.blocks.mine), channel_id=1, source_target_pairs={{0,1},{1,0},{2,3},{3,2},{4,5},{5,4},{6,7},{7,6},{8,9},{9,8},{10,11... | collective-permute-start | bytes 7864328 | tf_op jit(solution)/shard_map/ppermute | solution.py:853
  134.8 0.1 collective-permute-start.8
  134.9 0.6 collective-permute-start.9
  135.5 3.1 %collective-permute-start.10 = (f32[64,384]{1,0:T(8,128)}, f32[64,384]{1,0:T(8,128)S(1)}, u32[]{:S(2)}, u32[]{:S(2)}) collective-permute-start(f32[64,384]{1,0:T(8,128)} %get-tuple-element.81), channel_id=1, source_target_pairs={{16,1},{17,2},{18,3},{19,4},{20,5},{21,6},{22,7},{23,8},{24,9},{25... | collective-permute-start | bytes 294920 | tf_op jit(solution)/shard_map/ppermute | solution.py:858
  138.6 0.7 total_one.1
  139.3 0.8 copy-done
  140.1 5.9 %all-to-all-start.2 = ((bf16[64,32,128]{2,1,0:T(8,128)(2,1)}), bf16[64,32,128]{2,1,0:T(8,128)(2,1)S(1)}, u32[]{:S(2)}, u32[]{:S(2)}) async-start(bf16[64,32,128]{2,1,0:T(8,128)(2,1)} %copy-done), calls=%async_computation.2 | async-start | bytes 1048576 | tf_op jit(solution)/shard_map/all_to_all | solution.py:848
  146.0 0.7 copy-done.17
  146.6 0.7 copy-done.19
  147.3 0.9 copy-done.18
  148.2 0.9 copy-done.20
  149.1 0.9 copy-done.29
  150.0 0.9 copy-done.32
  150.9 1.0 copy-done.38
  151.9 0.9 copy-done.40
  152.9 1.6 assemble.1
  154.5 5.5 %last_two.1 = (f32[768,384]{1,0:T(8,128)}, f32[384,1152]{1,0:T(8,128)}, f32[384,384]{1,0:T(8,128)}, f32[384,1536]{1,0:T(8,128)}, f32[1536,384]{1,0:T(8,128)}) custom-call(s32[3]{0:T(128)S(1)} %copy-done.2, bf16[64,160,128]{2,1,0:T(8,128)(2,1)S(1)} %all_to_all.15.blocks.mine, bf16[64,160,128]{2,1,0:T(8,128)(2,1)} %collective-permute-done.11.theirs), custom_call_target="tpu_custom_call" | custom-call | flops 5000000000 | bytes 15000000 | tf_op jit(solution)/shard_map/last_two/pallas_call | solution.py:714
  160.0 1.0 collective-permute-start.12
  161.0 0.9 copy.40
  161.9 0.6 collective-permute-done.12.theirs
  162.6 1.9 %last_one.1 = (f32[192,576]{1,0:T(8,128)}, f32[192,192]{1,0:T(8,128)}, f32[192,768]{1,0:T(8,128)}, f32[192,768]{1,0:T(8,128)}) custom-call(s32[3]{0:T(128)S(1)} %copy-done.2, bf16[64,32,128]{2,1,0:T(8,128)(2,1)S(1)} %all-to-all-done.2.mine, bf16[64,32,128]{2,1,0:T(8,128)(2,1)S(1)} %collective-permute-done.12.theirs), custom_call_target="tpu_custom_call" | custom-call | flops 2000000000 | bytes 6000000 | tf_op jit(solution)/shard_map/last_one/pallas_call | solution.py:714
  (76 shorter events, 0.2 us)
Async XLA Ops:
  0.6 0.9 copy-start.13
  1.6 0.9 copy-start.15
  2.5 9.3 %copy-start.3 = (f32[9,12,3312]{2,1,0:T(8,128)S(1)}, f32[9,12,3312]{2,1,0:T(8,128)}, u32[]{:S(2)}) copy-start(f32[9,12,3312]{2,1,0:T(8,128)} %two.1) | copy-start | bytes 4292356
  2.5 9.3 %copy-start.33 = (f32[1,3312]{1,0:T(1,128)S(1)}, f32[1,3312]{1,0:T(1,128)}, u32[]{:S(2)}) copy-start(f32[1,3312]{1,0:T(1,128)} %constant.44.clone.kind) | copy-start | bytes 39748
  3.3 16.6 %collective-permute-start.1 = (bf16[12,24,384]{2,1,0:T(8,128)(2,1)}, bf16[12,24,384]{2,1,0:T(8,128)(2,1)S(1)}, u32[]{:S(2)}, u32[]{:S(2)}) collective-permute-start(bf16[12,24,384]{2,1,0:T(8,128)(2,1)} %get-tuple-element.57), channel_id=1, source_target_pairs={{0,16},{16,32},{32,48},{48,64},{64,80},{80,96},{96,112},{112,0},{1... | collective-permute-start | bytes 663560 | tf_op jit(solution)/shard_map/ppermute | solution.py:809
  7.7 12.2 %collective-permute-start.2 = (bf16[12,24,384]{2,1,0:T(8,128)(2,1)}, bf16[12,24,384]{2,1,0:T(8,128)(2,1)S(1)}, u32[]{:S(2)}, u32[]{:S(2)}) collective-permute-start(bf16[12,24,384]{2,1,0:T(8,128)(2,1)} %get-tuple-element.57), channel_id=1, source_target_pairs={{1,16},{2,17},{3,18},{4,19},{5,20},{6,21},{7,22},{8,23},{9,24},{10... | collective-permute-start | bytes 663560 | tf_op jit(solution)/shard_map/ppermute | solution.py:810
  8.9 10.9 %collective-permute-start = (bf16[12,24,384]{2,1,0:T(8,128)(2,1)}, bf16[12,24,384]{2,1,0:T(8,128)(2,1)}, u32[]{:S(2)}, u32[]{:S(2)}) collective-permute-start(bf16[12,24,384]{2,1,0:T(8,128)(2,1)} %get-tuple-element.56), channel_id=1, source_target_pairs={{1,0},{2,1},{3,2},{4,3},{5,4},{6,5},{7,6},{8,7},{9,8},{10,9},{11,1... | collective-permute-start | bytes 663560 | tf_op jit(solution)/shard_map/ppermute | solution.py:808
  11.8 1.5 copy-start.4
  13.3 1.7 %copy-start.22 = (bf16[3312,276]{1,0:T(8,128)(2,1)S(1)}, bf16[3312,276]{1,0:T(8,128)(2,1)}, u32[]{:S(2)}) copy-start(bf16[3312,276]{1,0:T(8,128)(2,1)} %constant.46.clone.lanes) | copy-start | bytes 5484676
  15.0 0.9 copy-start.26
  16.0 30.5 %copy-start.1 = (s32[3]{0:T(128)}, s32[3]{0:T(128)S(1)}, u32[]{:S(2)}) copy-start(s32[3]{0:T(128)S(1)} %pad_add_fusion.ids) | copy-start | bytes 40
  16.0 3.9 %copy-start.5 = (bf16[384,1536]{1,0:T(8,128)(2,1)S(1)}, bf16[384,1536]{1,0:T(8,128)(2,1)}, u32[]{:S(2)}) copy-start(bf16[384,1536]{1,0:T(8,128)(2,1)} %up_two.1) | copy-start | bytes 3538948
  16.0 3.9 %copy-start.6 = (bf16[1536,384]{1,0:T(8,128)(2,1)S(1)}, bf16[1536,384]{1,0:T(8,128)(2,1)}, u32[]{:S(2)}) copy-start(bf16[1536,384]{1,0:T(8,128)(2,1)} %down_two.1) | copy-start | bytes 3538948
  16.0 3.9 %copy-start.7 = (bf16[384,1152]{1,0:T(8,128)(2,1)S(1)}, bf16[384,1152]{1,0:T(8,128)(2,1)}, u32[]{:S(2)}) copy-start(bf16[384,1152]{1,0:T(8,128)(2,1)} %qkv_two.1) | copy-start | bytes 2654212
  16.0 3.9 %copy-start.8 = (bf16[768,384]{1,0:T(8,128)(2,1)S(1)}, bf16[768,384]{1,0:T(8,128)(2,1)}, u32[]{:S(2)}) copy-start(bf16[768,384]{1,0:T(8,128)(2,1)} %merge.1) | copy-start | bytes 1769476
  16.0 3.9 %copy-start.9 = (bf16[384,384]{1,0:T(8,128)(2,1)S(1)}, bf16[384,384]{1,0:T(8,128)(2,1)}, u32[]{:S(2)}) copy-start(bf16[384,384]{1,0:T(8,128)(2,1)} %proj_two.1) | copy-start | bytes 884740
  16.0 3.9 %copy-start.10 = (bf16[192,768]{1,0:T(8,128)(2,1)S(1)}, bf16[192,768]{1,0:T(8,128)(2,1)}, u32[]{:S(2)}) copy-start(bf16[192,768]{1,0:T(8,128)(2,1)} %up_one.3) | copy-start | bytes 884740
  16.0 3.9 %copy-start.11 = (bf16[768,192]{0,1:T(8,128)(2,1)S(1)}, bf16[768,192]{0,1:T(8,128)(2,1)}, u32[]{:S(2)}) copy-start(bf16[768,192]{0,1:T(8,128)(2,1)} %param.35) | copy-start | bytes 884740
  16.0 3.9 %copy-start.12 = (bf16[192,576]{1,0:T(8,128)(2,1)S(1)}, bf16[192,576]{1,0:T(8,128)(2,1)}, u32[]{:S(2)}) copy-start(bf16[192,576]{1,0:T(8,128)(2,1)} %qkv_one.3) | copy-start | bytes 663556
  16.1 3.9 %copy-start.14 = (bf16[1,12,24,384]{3,2,1,0:T(8,128)(2,1)S(1)}, bf16[1,12,24,384]{3,2,1,0:T(8,128)(2,1)}, u32[]{:S(2)}) copy-start(bf16[1,12,24,384]{3,2,1,0:T(8,128)(2,1)} %param.29) | copy-start | bytes 663556
  16.1 3.9 %copy-start.16 = (bf16[1,6,12,768]{3,2,1,0:T(8,128)(2,1)S(1)}, bf16[1,6,12,768]{3,2,1,0:T(8,128)(2,1)}, u32[]{:S(2)}) copy-start(bf16[1,6,12,768]{3,2,1,0:T(8,128)(2,1)} %param.30) | copy-start | bytes 331780
  16.1 3.9 %copy-start.21 = (bf16[192,192]{1,0:T(8,128)(2,1)S(1)}, bf16[192,192]{1,0:T(8,128)(2,1)}, u32[]{:S(2)}) copy-start(bf16[192,192]{1,0:T(8,128)(2,1)} %proj_one.3) | copy-start | bytes 221188
  16.1 3.9 %copy-start.23 = (bf16[3,576,432]{2,1,0:T(8,128)(2,1)S(1)}, bf16[3,576,432]{2,1,0:T(8,128)(2,1)}, u32[]{:S(2)}) copy-start(bf16[3,576,432]{2,1,0:T(8,128)(2,1)} %constant.48.clone.gather) | copy-start | bytes 4478980
  16.1 3.9 %copy-start.24 = (bf16[2,432,288]{2,1,0:T(8,128)(2,1)S(1)}, bf16[2,432,288]{2,1,0:T(8,128)(2,1)}, u32[]{:S(2)}) copy-start(bf16[2,432,288]{2,1,0:T(8,128)(2,1)} %constant.47.clone.select) | copy-start | bytes 1492996
  16.1 3.9 %copy-start.25 = (bf16[272,576]{1,0:T(8,128)(2,1)S(1)}, bf16[272,576]{1,0:T(8,128)(2,1)}, u32[]{:S(2)}) copy-start(bf16[272,576]{1,0:T(8,128)(2,1)} %constant.50.clone.strips) | copy-start | bytes 940036
  16.1 3.9 %copy-start.27 = (bf16[144,576]{1,0:T(8,128)(2,1)S(1)}, bf16[144,576]{1,0:T(8,128)(2,1)}, u32[]{:S(2)}) copy-start(bf16[144,576]{1,0:T(8,128)(2,1)} %constant.55.clone.fold_ref) | copy-start | bytes 497668
  16.1 3.9 %copy-start.28 = (bf16[128,576]{1,0:T(8,128)(2,1)S(1)}, bf16[128,576]{1,0:T(8,128)(2,1)}, u32[]{:S(2)}) copy-start(bf16[128,576]{1,0:T(8,128)(2,1)} %constant.54.clone.mask_t_ref) | copy-start | bytes 442372
  16.2 3.9 %copy-start.30 = (bf16[576,128]{1,0:T(8,128)(2,1)S(1)}, bf16[576,128]{1,0:T(8,128)(2,1)}, u32[]{:S(2)}) copy-start(bf16[576,128]{1,0:T(8,128)(2,1)} %constant.53.clone.mask_ref) | copy-start | bytes 442372
  16.2 3.9 %copy-start.31 = (bf16[144,288]{1,0:T(8,128)(2,1)S(1)}, bf16[144,288]{1,0:T(8,128)(2,1)}, u32[]{:S(2)}) copy-start(bf16[144,288]{1,0:T(8,128)(2,1)} %constant.49.clone.cot_select) | copy-start | bytes 248836
  19.8 20.3 %copy-start.39 = (f32[3,144,576]{2,1,0:T(8,128)}, f32[3,144,576]{2,1,0:T(8,128)S(1)}, u32[]{:S(2)}) copy-start(f32[3,144,576]{2,1,0:T(8,128)S(1)} %get-tuple-element.58.bias_a) | copy-start | bytes 2985988
  19.9 20.3 %copy-start.41 = (f32[3,144,288]{2,1,0:T(8,128)}, f32[3,144,288]{2,1,0:T(8,128)S(1)}, u32[]{:S(2)}) copy-start(f32[3,144,288]{2,1,0:T(8,128)S(1)} %get-tuple-element.59.bias_b) | copy-start | bytes 1492996
  40.2 10.2 %copy-start.42 = (bf16[3,432,192]{2,1,0:T(8,128)(2,1)}, bf16[3,432,192]{2,1,0:T(8,128)(2,1)S(1)}, u32[]{:S(2)}) copy-start(bf16[3,432,192]{2,1,0:T(8,128)(2,1)S(1)} %get-tuple-element.67.xw) | copy-start | bytes 1492996
  40.2 10.2 %copy-start.43 = (bf16[576,192]{1,0:T(8,128)(2,1)}, bf16[576,192]{1,0:T(8,128)(2,1)S(1)}, u32[]{:S(2)}) copy-start(bf16[576,192]{1,0:T(8,128)(2,1)S(1)} %get-tuple-element.69.own) | copy-start | bytes 663556
  40.2 10.2 %copy-start.44 = (f32[144,384]{1,0:T(8,128)}, f32[144,384]{1,0:T(8,128)S(1)}, u32[]{:S(2)}) copy-start(f32[144,384]{1,0:T(8,128)S(1)} %get-tuple-element.68.out_two) | copy-start | bytes 663556
  40.2 6.3 %collective-permute-start.3 = (bf16[8192,128]{1,0:T(8,128)(2,1)}, bf16[8192,128]{1,0:T(8,128)(2,1)S(1)}, u32[]{:S(2)}, u32[]{:S(2)}) collective-permute-start(bf16[8192,128]{1,0:T(8,128)(2,1)} %get-tuple-element.62), channel_id=1, source_target_pairs={{0,1},{1,0},{2,3},{3,2},{4,5},{5,4},{6,7},{7,6},{8,9},{9,8},{10,11... | collective-permute-start | bytes 6291464 | tf_op jit(solution)/shard_map/ppermute | solution.py:824
  41.8 9.1 %collective-permute-start.4 = (bf16[112,192]{1,0:T(8,128)(2,1)S(1)}, bf16[112,192]{1,0:T(8,128)(2,1)S(1)}, u32[]{:S(2)}, u32[]{:S(2)}) collective-permute-start(bf16[112,192]{1,0:T(8,128)(2,1)S(1)} %get-tuple-element.63), channel_id=1, source_target_pairs={{0,1},{1,2},{2,3},{3,4},{4,5},{5,6},{6,7},{7,8},{8,9},{9,10},{10,1... | collective-permute-start | bytes 129032 | tf_op jit(solution)/shard_map/ppermute | solution.py:820
  42.8 8.1 %collective-permute-start.5 = (bf16[112,192]{1,0:T(8,128)(2,1)S(1)}, bf16[112,192]{1,0:T(8,128)(2,1)S(1)}, u32[]{:S(2)}, u32[]{:S(2)}) collective-permute-start(bf16[112,192]{1,0:T(8,128)(2,1)S(1)} %get-tuple-element.64), channel_id=1, source_target_pairs={{16,0},{32,16},{48,32},{64,48},{80,64},{96,80},{112,96},{0,112},{1... | collective-permute-start | bytes 129032 | tf_op jit(solution)/shard_map/ppermute | solution.py:821
  46.1 4.8 %collective-permute-start.6 = (bf16[48,192]{1,0:T(8,128)(2,1)S(1)}, bf16[48,192]{1,0:T(8,128)(2,1)S(1)}, u32[]{:S(2)}, u32[]{:S(2)}) collective-permute-start(bf16[48,192]{1,0:T(8,128)(2,1)S(1)} %get-tuple-element.65), channel_id=1, source_target_pairs={{16,1},{17,2},{18,3},{19,4},{20,5},{21,6},{22,7},{23,8},{24,9},{25... | collective-permute-start | bytes 55304 | tf_op jit(solution)/shard_map/ppermute | solution.py:822
  46.5 1.6 copy-start.37
  50.9 0.6 copy-start.47
  50.9 0.6 copy-start.45
  50.9 0.6 copy-start.46
  51.5 39.8 %all-to-all-start = ((bf16[64,128,128]{2,1,0:T(8,128)(2,1)}), bf16[64,128,128]{2,1,0:T(8,128)(2,1)S(1)}, u32[]{:S(2)}, u32[]{:S(2)}) async-start(bf16[64,128,128]{2,1,0:T(8,128)(2,1)} %chip_two.1), calls=%async_computation | async-start | bytes 4194304 | tf_op jit(solution)/shard_map/all_to_all | solution.py:832
  61.0 17.9 %copy-start.2 = (s32[3]{0:T(128)S(1)}, s32[3]{0:T(128)}, u32[]{:S(2)}) copy-start(s32[3]{0:T(128)} %copy-done.1) | copy-start | bytes 40
  76.7 2.2 %collective-permute-start.7 = (bf16[2048,128]{1,0:T(8,128)(2,1)}, bf16[2048,128]{1,0:T(8,128)(2,1)S(1)}, u32[]{:S(2)}, u32[]{:S(2)}) collective-permute-start(bf16[2048,128]{1,0:T(8,128)(2,1)} %get-tuple-element.74), channel_id=1, source_target_pairs={{0,1},{1,0},{2,3},{3,2},{4,5},{5,4},{6,7},{7,6},{8,9},{9,8},{10,11... | collective-permute-start | bytes 1572872 | tf_op jit(solution)/shard_map/ppermute | solution.py:840
  78.9 1.0 copy-start.34
  80.6 0.8 copy-start.35
  91.4 1.0 copy-start.36
  132.4 22.1 %collective-permute-start.11 = (bf16[64,160,128]{2,1,0:T(8,128)(2,1)S(1)}, bf16[64,160,128]{2,1,0:T(8,128)(2,1)}, u32[]{:S(2)}, u32[]{:S(2)}) collective-permute-start(bf16[64,160,128]{2,1,0:T(8,128)(2,1)S(1)} %all_to_all.15.blocks.mine), channel_id=1, source_target_pairs={{0,1},{1,0},{2,3},{3,2},{4,5},{5,4},{6,7},{7,6},{8,9},{9,8},{10,11... | collective-permute-start | bytes 7864328 | tf_op jit(solution)/shard_map/ppermute | solution.py:853
  134.8 11.2 %collective-permute-start.8 = (f32[96,384]{1,0:T(8,128)}, f32[96,384]{1,0:T(8,128)S(1)}, u32[]{:S(2)}, u32[]{:S(2)}) collective-permute-start(f32[96,384]{1,0:T(8,128)} %get-tuple-element.79), channel_id=1, source_target_pairs={{0,1},{1,2},{2,3},{3,4},{4,5},{5,6},{6,7},{7,8},{8,9},{9,10},{10,1... | collective-permute-start | bytes 442376 | tf_op jit(solution)/shard_map/ppermute | solution.py:856
  134.9 11.8 %collective-permute-start.9 = (f32[96,384]{1,0:T(8,128)}, f32[96,384]{1,0:T(8,128)S(1)}, u32[]{:S(2)}, u32[]{:S(2)}) collective-permute-start(f32[96,384]{1,0:T(8,128)} %get-tuple-element.80), channel_id=1, source_target_pairs={{16,0},{32,16},{48,32},{64,48},{80,64},{96,80},{112,96},{0,112},{1... | collective-permute-start | bytes 442376 | tf_op jit(solution)/shard_map/ppermute | solution.py:857
  135.5 10.5 %collective-permute-start.10 = (f32[64,384]{1,0:T(8,128)}, f32[64,384]{1,0:T(8,128)S(1)}, u32[]{:S(2)}, u32[]{:S(2)}) collective-permute-start(f32[64,384]{1,0:T(8,128)} %get-tuple-element.81), channel_id=1, source_target_pairs={{16,1},{17,2},{18,3},{19,4},{20,5},{21,6},{22,7},{23,8},{24,9},{25... | collective-permute-start | bytes 294920 | tf_op jit(solution)/shard_map/ppermute | solution.py:858
  139.3 0.8 copy-start
  140.1 19.9 %all-to-all-start.2 = ((bf16[64,32,128]{2,1,0:T(8,128)(2,1)}), bf16[64,32,128]{2,1,0:T(8,128)(2,1)S(1)}, u32[]{:S(2)}, u32[]{:S(2)}) async-start(bf16[64,32,128]{2,1,0:T(8,128)(2,1)} %copy-done), calls=%async_computation.2 | async-start | bytes 1048576 | tf_op jit(solution)/shard_map/all_to_all | solution.py:848
  146.0 0.7 copy-start.17
  146.6 0.7 copy-start.19
  147.3 0.9 copy-start.18
  148.2 0.9 copy-start.20
  149.1 0.9 copy-start.29
  150.0 0.9 copy-start.32
  150.9 1.0 copy-start.38
  151.9 0.9 copy-start.40
  160.0 2.6 %collective-permute-start.12 = (bf16[64,32,128]{2,1,0:T(8,128)(2,1)S(1)}, bf16[64,32,128]{2,1,0:T(8,128)(2,1)S(1)}, u32[]{:S(2)}, u32[]{:S(2)}) collective-permute-start(bf16[64,32,128]{2,1,0:T(8,128)(2,1)S(1)} %all-to-all-done.2.mine), channel_id=1, source_target_pairs={{0,1},{1,0},{2,3},{3,2},{4,5},{5,4},{6,7},{7,6},{8,9},{9,8},{10,11... | collective-permute-start | bytes 1572872 | tf_op jit(solution)/shard_map/ppermute | solution.py:869

commit v3 on v2

--- a/solution.py
+++ b/solution.py
@@ -130,16 +130,9 @@
 def bias_constants():
     z1, z2, a1, a2, r = (v.reshape(-1) for v in np.indices((LEVELS, LEVELS, WLAT, WLAT, REL)))
     half = WLAT // 2
-    kind = np.where((a1 < half) & (a2 < half), 0.0, np.where((a1 >= half) & (a2 >= half), 1.0, 2.0))
-    rows = np.stack(
-        [(z2 == level)[None] & (a2[None] + 2 * (1 - level) == np.arange(8)[:, None]) for level in range(2)]
-    )
-    lanes = (r * COLUMN + z1 * WLAT + a1)[:, None] == np.arange(REL * COLUMN)[None]
-    return (
-        jnp.asarray(kind[None], F32),
-        jnp.asarray(rows, F32),
-        jnp.asarray(lanes.astype(np.float32), BF16),
-    )
+    kind = np.where((a1 < half) & (a2 < half), 0, np.where((a1 >= half) & (a2 >= half), 1, 2))
+    codes = np.stack([kind, z2, a2 + 2 * (1 - z2), r * COLUMN + z1 * WLAT + a1])
+    return jnp.asarray(codes, F32)
 
 
 def blocks_of_heads():
@@ -239,14 +232,18 @@
 SPANS = (((0, 896), (1536, 2560)), ((768, 1664), (2432, 3312)))
 
 
-def bias_kernel(ids, one, two, kind, rows, lanes, first_ref, second_ref, two_out_ref, pieces, table):
+def bias_kernel(ids, one, two, codes, first_ref, second_ref, two_out_ref, pieces, table):
     band = ids[0]
+    kind, level_of, row_of, place_of = (codes[i : i + 1, :] for i in range(4))
+    places = lax.broadcasted_iota(jnp.int32, (REL * COLUMN, codes.shape[1]), 0).astype(F32)
+    lanes = jnp.where(places == place_of, 1.0, 0.0).astype(BF16)
+    row = lax.broadcasted_iota(jnp.int32, (8, codes.shape[1]), 0).astype(F32)
 
     def window(source, index):
         count = source.shape[0] - 1
         index = lax.rem(index + count, count)
         mixed = jnp.where(
-            kind[...] == 0.0, source[count], jnp.where(kind[...] == 1.0, source[0], MASKED)
+            kind == 0.0, source[count], jnp.where(kind == 1.0, source[0], MASKED)
         )
         return jnp.where(index == 0, mixed, source[index])
 
@@ -256,6 +253,7 @@
     heads = sum(value.shape[0] for value in values)
     for level in range(2):
         slot = 0
+        rows = (row == row_of) & (level_of == float(level))
         for value in values:
             high = value.astype(BF16).astype(F32)
             low = value - high
@@ -263,7 +261,7 @@
                 for piece, taken in enumerate((high, low)):
                     at = 0
                     for start, stop in SPANS[level]:
-                        chosen = rows[level, :, start:stop] > 0.0
+                        chosen = rows[:, start:stop]
                         pair = [
                             jnp.where(chosen, taken[h + i : h + i + 1, start:stop], 0.0) for i in range(2)
                         ]
@@ -276,7 +274,7 @@
         for piece in range(2):
             at = 0
             for start, stop in SPANS[level]:
-                term = nn(pieces[piece, :, at : at + stop - start], lanes[start:stop, :])
+                term = nt(pieces[piece, :, at : at + stop - start], lanes[:, start:stop])
                 total = term if total is None else total + term
                 at += stop - start
         for h in range(heads):
@@ -555,25 +553,31 @@
     )(*operands)
 
 
+def window_places(row, pa_ref, pb_ref):
+    return [
+        (
+            pl.ds(pl.multiple_of(row * 288 + wc * WINDOW, WINDOW), WINDOW),
+            slice(start * HEAD, (start + heads) * HEAD),
+            heads,
+            (pa_ref if heads == 4 else pb_ref, row * 2 + wc),
+        )
+        for wc in range(2)
+        for start, heads in GROUPS_ONE
+    ]
+
+
 def halves(value):
     high = value.astype(BF16)
     return high, (value - high.astype(F32)).astype(BF16)
 
 
-def lower_kernel(
-    ids, xw, out_two, own, lon, lat, corner, bias_a, bias_b,
-    qkv_one, proj_one, up_one, down_one,
-    back_own, back_strips, to_tokens, to_two, mask_ref, mask_t_ref, fold_ref,
-    out_ref, out_two_ref, lon_ref, lat_ref, corner_ref, mine_ref, theirs_ref,
-    gs_ref, normed_ref, full_ref, scale_ref, q_ref, k_ref, v_ref, pa_ref, pb_ref, att_ref,
-    normed_two_ref, act_ref, raised_ref, gm_ref, gml_ref, ga_ref, gq_ref, gk_ref, gv_ref, gx_ref,
-    packed, sems,
+def lower_forward_kernel(
+    xw, bias_a, bias_b, qkv_one, proj_one, up_one, mask_ref, mask_t_ref, fold_ref,
+    normed_ref, full_ref, scale_ref, q_ref, k_ref, v_ref, pa_ref, pb_ref, att_ref,
+    normed_two_ref, full_two_ref, scale_two_ref, act_ref, slope_ref,
 ):
     mask, mask_t, fold = mask_ref[...], mask_t_ref[...], fold_ref[...]
-    arrived = jnp.concatenate([lon[...], lat[...], corner[...]], axis=0)
-    gs_ref[...] = nn(back_own[...], own[...]) + nn(back_strips[...], arrived)
     row_slices = [slice(row * 288, (row + 1) * 288) for row in range(2)]
-
     for row, rows in enumerate(row_slices):
         full, scale = layer_norm(xw[1 + row, :288, :].astype(F32))
         full_ref[rows, :] = full
@@ -585,41 +589,70 @@
         k_ref[rows, :] = projected[:, C1 : 2 * C1]
         v_ref[rows, :] = projected[:, 2 * C1 :]
 
-    def places(row):
-        return [
-            (
-                pl.ds(pl.multiple_of(row * 288 + wc * WINDOW, WINDOW), WINDOW),
-                slice(start * HEAD, (start + heads) * HEAD),
-                heads,
-                (pa_ref if heads == 4 else pb_ref, row * 2 + wc),
-                bias_a if heads == 4 else bias_b,
-            )
-            for wc in range(2)
-            for start, heads in GROUPS_ONE
-        ]
-
     @pl.loop(0, 2)
     def _(row):
+        places = window_places(row, pa_ref, pb_ref)
         parts = [
-            (q_ref[rows, at], k_ref[rows, at], v_ref[rows, at], bias[1 + row], heads)
-            for rows, at, heads, _, bias in places(row)
+            (
+                q_ref[rows, at], k_ref[rows, at], v_ref[rows, at],
+                bias_a[1 + row] if heads == 4 else bias_b[1 + row], heads,
+            )
+            for rows, at, heads, _ in places
         ]
         taken, chances = attend(parts, mask, mask_t, fold)
-        for (rows, at, _, (kept, window), _), value, chance in zip(places(row), taken, chances):
+        for (rows, at, _, (kept, window)), value, chance in zip(places, taken, chances):
             att_ref[rows, at] = value.astype(BF16)
             kept[window] = chance
 
     for row, rows in enumerate(row_slices):
         middle = xw[1 + row, :288, :].astype(F32) + nn(att_ref[rows, :], proj_one[...])
         full, scale = layer_norm(middle)
+        full_two_ref[rows, :] = full
+        scale_two_ref[rows, :] = scale
         normed_two = full.astype(BF16)
         normed_two_ref[rows, :] = normed_two
         active, slope = gelu_both(nn(normed_two, up_one[...]))
         act_ref[rows, :] = active.astype(BF16)
+        slope_ref[rows, :] = slope
+
+
+def lower_forward(*operands):
+    shape = jax.ShapeDtypeStruct
+    wide, full, scale = shape((576, C1), BF16), shape((576, C1), F32), shape((576, 1), F32)
+    return pl.pallas_call(
+        lower_forward_kernel,
+        out_shape=(
+            wide, full, scale, wide, wide, wide,
+            shape((4, WINDOW, 576), F32), shape((4, WINDOW, 288), F32), wide,
+            wide, full, scale, shape((576, 768), BF16), shape((576, 768), F32),
+        ),
+        name="lower_forward",
+        **params(5, 32),
+    )(*operands)
+
+
+def lower_kernel(
+    ids, out_two, own, lon, lat, corner,
+    normed_ref, full_ref, scale_ref, q_ref, k_ref, v_ref, pa_ref, pb_ref, att_ref,
+    normed_two_ref, full_two_ref, scale_two_ref, act_ref, slope_ref,
+    qkv_one, proj_one, up_one, down_one,
+    back_own, back_strips, to_tokens, to_two, mask_ref, mask_t_ref, fold_ref,
+    out_ref, out_two_ref, lon_ref, lat_ref, corner_ref, mine_ref, theirs_ref,
+    gs_ref, raised_ref, gm_ref, gml_ref, ga_ref, gq_ref, gk_ref, gv_ref, gx_ref,
+    packed, sems,
+):
+    mask, mask_t, fold = mask_ref[...], mask_t_ref[...], fold_ref[...]
+    arrived = jnp.concatenate([lon[...], lat[...], corner[...]], axis=0)
+    gs_ref[...] = nn(back_own[...], own[...]) + nn(back_strips[...], arrived)
+    row_slices = [slice(row * 288, (row + 1) * 288) for row in range(2)]
+
+    for rows in row_slices:
         grad = gs_ref[rows, :]
-        grad_raised = (nn(grad.astype(BF16), down_one[...]) * slope).astype(BF16)
+        grad_raised = (nn(grad.astype(BF16), down_one[...]) * slope_ref[rows, :]).astype(BF16)
         raised_ref[rows, :] = grad_raised
-        grad_middle = grad + layer_norm_back(nt(grad_raised, up_one[...]), full, scale)
+        grad_middle = grad + layer_norm_back(
+            nt(grad_raised, up_one[...]), full_two_ref[rows, :], scale_two_ref[rows, :]
+        )
         gm_ref[rows, :] = grad_middle
         low = grad_middle.astype(BF16)
         gml_ref[rows, :] = low
@@ -627,13 +660,14 @@
 
     @pl.loop(0, 2)
     def _(row):
+        places = window_places(row, pa_ref, pb_ref)
         parts = [
             (q_ref[rows, at], k_ref[rows, at], v_ref[rows, at], kept[window], ga_ref[rows, at], heads)
-            for rows, at, heads, (kept, window), _ in places(row)
+            for rows, at, heads, (kept, window) in places
         ]
         grads = attend_back(parts, mask, mask_t, fold)
         for target, values in zip((gq_ref, gk_ref, gv_ref), grads):
-            for (rows, at, _, _, _), value in zip(places(row), values):
+            for (rows, at, _, _), value in zip(places, values):
                 target[rows, at] = value.astype(BF16)
 
     normed = normed_ref[...]
@@ -666,8 +700,8 @@
     at = 288
     for kind, ref in enumerate((lon_ref, lat_ref, corner_ref)):
         count = SHIFT_TOKENS[kind]
-        ref[:count, :] = cells[at : at + count]
-        ref[count:, :] = two[144 + kind * 40 : 144 + (kind + 1) * 40]
+        strip = [cells[at : at + count], two[144 + kind * 40 : 144 + (kind + 1) * 40]]
+        ref[...] = jnp.concatenate(strip, axis=0).astype(BF16)
         at += count
     for half in range(2):
         send_half(ids, packed, half, mine_ref, theirs_ref, sems, False)
@@ -683,21 +717,12 @@
         out_shape=(
             shape((288, C2), F32),
             shape((144, C2), F32),
-            *(shape((count, C2), F32) for count in SHIFT),
+            *(shape((count, C2), BF16) for count in SHIFT),
             packed_shape(LOWER_BLOCK),
             packed_shape(LOWER_BLOCK),
         ),
         scratch_shapes=[
             pltpu.VMEM((576, C1), F32),
-            wide,
-            pltpu.VMEM((576, C1), F32),
-            pltpu.VMEM((576, 1), F32),
-            wide, wide, wide,
-            pltpu.VMEM((4, WINDOW, 576), F32),
-            pltpu.VMEM((4, WINDOW, 288), F32),
-            wide,
-            wide,
-            pltpu.VMEM((576, 768), BF16),
             pltpu.VMEM((576, 768), BF16),
             pltpu.VMEM((576, C1), F32),
             wide, wide, wide, wide, wide,
@@ -705,7 +730,7 @@
             pltpu.VMEM((2, CHIPS * LOWER_BLOCK, LANES), BF16),
             pltpu.SemaphoreType.DMA((2,)),
         ],
-        **params(15, 60),
+        **params(10, 32),
         name="lower",
     )(*operands)
 
@@ -735,53 +760,50 @@
     return value.astype(BF16)
 
 
-def middle_kernel(ids, blocks, packed_one, out):
-    value = total(blocks, 0, UPPER_BLOCK)
+def chip_one_kernel(ids, mine, theirs, upper, out):
     for block in range(CHIPS):
-        out[block, :UPPER_BLOCK, :] = value
-        out[block, UPPER_BLOCK:, :] = packed_one[block]
+        at = slice(block * LOWER_BLOCK, (block + 1) * LOWER_BLOCK)
+        out[block, :UPPER_BLOCK, :] = upper[block]
+        out[block, UPPER_BLOCK:, :] = (mine[at].astype(F32) + theirs[at].astype(F32)).astype(BF16)
 
 
 def total_kernel(ids, blocks, out):
-    value = total(blocks, UPPER_BLOCK, LOWER_BLOCK)
+    value = total(blocks, 0, blocks.shape[1])
     for block in range(CHIPS):
         out[block] = value
 
 
-def join_halves(ids, mine, theirs, packed):
+def join_halves(ids, mine, theirs, packed, low):
     rows = packed.shape[1] // CHIPS
     for half, source in ((ids[2], mine), (1 - ids[2], theirs)):
         for block in range(CHIPS):
-            packed[half, block * rows : (block + 1) * rows, :] = source[block, :rows, :]
-
-
-def upper_last_kernel(factor, ids, mine, theirs, merge, qkv, proj, up, down, packed):
-    join_halves(ids, mine, theirs, packed)
-    for out, base in ((up, 0), (down, 4608), (proj, 9216), (merge, 13824)):
-        out[...] = take(packed, base, out.shape[0], out.shape[1] // LANES) * factor
+            packed[half, block * rows : (block + 1) * rows, :] = source[block, low : low + rows, :]
+
+
+def last_kernel(
+    factor, ids, mine, theirs, qkv, proj, up, down, merge, qkv_two, proj_two, up_two, down_two, lower, upper
+):
+    join_halves(ids, mine, theirs, upper, 0)
+    for out, base in ((up_two, 0), (down_two, 4608), (proj_two, 9216), (merge, 13824)):
+        out[...] = take(upper, base, out.shape[0], out.shape[1] // LANES) * factor
     for j in range(3):
-        qkv[:, j * C2 : (j + 1) * C2] = take(packed, 10368 + j * 1152, C2, 3) * factor
-
-
-def lower_last_kernel(factor, ids, mine, theirs, qkv, proj, up, down, packed):
-    join_halves(ids, mine, theirs, packed)
-    joined = take(packed, 0, C1, 6) * factor
+        qkv_two[:, j * C2 : (j + 1) * C2] = take(upper, 10368 + j * 1152, C2, 3) * factor
+    join_halves(ids, mine, theirs, lower, UPPER_BLOCK)
+    joined = take(lower, 0, C1, 6) * factor
     qkv[...] = joined[:, : 3 * C1]
     proj[...] = joined[:, 3 * C1 :]
-    up[...] = take(packed, 1152, C1, 6) * factor
-    down[...] = take(packed, 2304, C1, 6) * factor
+    up[...] = take(lower, 1152, C1, 6) * factor
+    down[...] = take(lower, 2304, C1, 6) * factor
 
 
 def assemble_kernel(ids, own, own_two, lon, lat, corner, place, place_two, tokens, two):
-    high, low = halves(jnp.concatenate([lon[...], lat[...], corner[...]], axis=0))
-    cells = own[...] + (nn(place[...], high) + nn(place[...], low))
+    arrived = jnp.concatenate([lon[...], lat[...], corner[...]], axis=0)
+    cells = own[...] + nn(place[...], arrived)
     for row in range(12):
         tokens[row] = cells[row * 24 : (row + 1) * 24]
-    cells = own_two[...] + (nn(place_two[...], high) + nn(place_two[...], low))
-    for row in range(6):
-        for level in range(2):
-            at = level * 72 + row * 12
-            two[row, :, level * C2 : (level + 1) * C2] = cells[at : at + 12]
+    cells = own_two[...] + nn(place_two[...], arrived)
+    for level in range(2):
+        two[:, 0, level * C2 : (level + 1) * C2] = cells[level * 72 : (level + 1) * 72]
 
 
 def per_device(
@@ -809,7 +831,7 @@
     up = lax.ppermute(for_down, "lat", from_up)
     diag = lax.ppermute(for_down, both, corner_in)
 
-    bias_a, bias_b, bias_c = expand_bias(ids, bias_one, bias_two, *bias_constants())
+    bias_a, bias_b, bias_c = expand_bias(ids, bias_one, bias_two, bias_constants())
     select, gather, cot_select, strips, back_own, back_strips = constants()
     mask, mask_t, fold = blocks_of_heads()
     out_two, xw, grad_own, lon_strip, lat_strip, corner, mine_two, theirs_two = upper(
@@ -826,50 +848,39 @@
     blocks = lambda rows: jax.ShapeDtypeStruct((CHIPS, rows, LANES), BF16)
     chips = ("lat", "chip")
     packed_two = call(chip_kernel, "chip_two", 3, 16, blocks(UPPER_BLOCK), (ids, mine_two, theirs_two))
-    packed_two, lon_strip, lat_strip, corner = lax.optimization_barrier(
-        (packed_two, lon_strip, lat_strip, corner)
-    )
-    packed_two = lax.all_to_all(packed_two, chips, 0, 0, tiled=True)
-
     to_tokens, to_two, place, place_two = output_constants()
+    kept = lower_forward(xw, bias_a, bias_b, qkv_one, proj_one, up_one, mask, mask_t, fold)
     own_cells, own_two, lon_strip, lat_strip, corner, mine_one, theirs_one = lower(
-        ids, xw, out_two, grad_own, lon_strip, lat_strip, corner, bias_a, bias_b,
+        ids, out_two, grad_own, lon_strip, lat_strip, corner, *kept,
         qkv_one, proj_one, up_one, down_one,
         back_own, back_strips, to_tokens, to_two, mask, mask_t, fold,
     )
     theirs_one = lax.ppermute(theirs_one, "core", other_core)
-    packed_one = call(chip_kernel, "chip_one", 1, 16, blocks(LOWER_BLOCK), (ids, mine_one, theirs_one))
-    packed_two, packed_one = lax.optimization_barrier((packed_two, packed_one))
-    merged = call(
-        middle_kernel, "middle", 2, 16, blocks(UPPER_BLOCK + LOWER_BLOCK), (ids, packed_two, packed_one)
+    packed = call(
+        chip_one_kernel, "chip_one", 1, 16, blocks(UPPER_BLOCK + LOWER_BLOCK),
+        (ids, mine_one, theirs_one, packed_two),
     )
-    merged = lax.all_to_all(merged, chips, 0, 0, tiled=True)
-    summed_one = call(total_kernel, "total_one", 1, 16, blocks(LOWER_BLOCK), (ids, merged))
-    gathered_one = lax.all_to_all(summed_one, chips, 0, 0, tiled=True)
-
-    sums_two = call(
-        functools.partial(upper_last_kernel, factor), "last_two", 5, 32,
-        tuple(result(*w.shape) for w in (merge_weight, qkv_two, proj_two, up_two, down_two)),
-        (ids, merged, lax.ppermute(merged, "core", other_core)),
-        [pltpu.VMEM((2, CHIPS * UPPER_BLOCK, LANES), BF16)],
-    )
+    packed = lax.all_to_all(packed, chips, 0, 0, tiled=True)
     lon_strip = lax.ppermute(lon_strip, lon, to_right)
     lat_strip = lax.ppermute(lat_strip, "lat", to_up)
     corner = lax.ppermute(corner, both, corner_out)
+    summed = call(total_kernel, "total", 2, 16, blocks(UPPER_BLOCK + LOWER_BLOCK), (ids, packed))
+    gathered = lax.all_to_all(summed, chips, 0, 0, tiled=True)
+    weights = (qkv_one, proj_one, up_one, down_one, merge_weight, qkv_two, proj_two, up_two, down_two)
+    sums = call(
+        functools.partial(last_kernel, factor), "last", 6, 40, tuple(result(*w.shape) for w in weights),
+        (ids, gathered, lax.ppermute(gathered, "core", other_core)),
+        [
+            pltpu.VMEM((2, CHIPS * LOWER_BLOCK, LANES), BF16),
+            pltpu.VMEM((2, CHIPS * UPPER_BLOCK, LANES), BF16),
+        ],
+    )
+    own_cells, *sums = lax.optimization_barrier((own_cells, *sums))
     grad_tokens, out_two = call(
-        assemble_kernel, "assemble", 3, 8, (result(12, 24, 2 * C1), result(6, 12, 2 * C2)),
+        assemble_kernel, "assemble", 3, 8, (result(12, 24, 2 * C1), result(72, 1, 2 * C2)),
         (ids, own_cells, own_two, lon_strip, lat_strip, corner, place, place_two),
     )
-    gathered_one, grad_tokens, out_two, *sums_two = lax.optimization_barrier(
-        (gathered_one, grad_tokens, out_two, *sums_two)
-    )
-    sums_one = call(
-        functools.partial(lower_last_kernel, factor), "last_one", 2, 32,
-        tuple(result(*w.shape) for w in (qkv_one, proj_one, up_one, down_one)),
-        (ids, gathered_one, lax.ppermute(gathered_one, "core", other_core)),
-        [pltpu.VMEM((2, CHIPS * LOWER_BLOCK, LANES), BF16)],
-    )
-    return (out_two[None], grad_tokens[None], *sums_one[:3], sums_one[3].T, *sums_two)
+    return (out_two.reshape(1, 6, 12, 2 * C2), grad_tokens[None], *sums[:3], sums[3].T, *sums[4:])
 
 
 def solution(mesh):

time: 165 us -> 161 us (0.976)
  blocking collectives: 39.1 us -> 84.7 us
  local copies, waits for them, and re-layouts: 19.8 us -> 3.47 us
  starting transfers between devices: 37.6 us -> 21.6 us
  waiting for transfers between devices: 12.9 us -> 4.04 us
  Pallas kernels: 53.8 us -> 45.7 us
    all_to_all x1 -> x2, blocking collectives: 39.1 us -> 84.7 us  [the longest x1 45 us: per_device(): packed = lax.all_to_all(packed, chips, 0, 0, tiled=True)]
    unnamed x97 -> x60, local copies, waits for them, and re-layouts: 19.8 us -> 3.47 us
    all_to_all x2 -> x0, starting transfers between devices: 15.3 us -> none  [the longest x1 9.46 us: per_device(): packed_two = lax.all_to_all(packed_two, chips, 0, 0, tiled=True)]
    all_to_all x2 -> x0, waiting for transfers between devices: 9.93 us -> none  [the longest x1 9.92 us: per_device(): packed_two = lax.all_to_all(packed_two, chips, 0, 0, tiled=True)]
    pallas_call x1, Pallas kernels: 15.7 us -> 8.27 us  [lower(): pl.pallas_call(lower_kernel, in_specs=specs(len(operands)), out_specs=out...]
    pallas_call x0 -> x1, Pallas kernels: none -> 4.91 us  [lower_forward(): pl.pallas_call(lower_forward_kernel, out_shape=(wide, full, scale, wide,...]
    pallas_call x7 -> x5, Pallas kernels: 13.6 us -> 9.16 us  [call(): pl.pallas_call(kernel, in_specs=specs(len(operands)), out_shape=out_shape...]
    ppermute x1, starting transfers between devices: 4.43 us -> 0.39 us  [per_device(): up = lax.ppermute(for_down, 'lat', from_up)]
  transfers between devices with their start and end apart: 15 -> 12, of which waited for: 4 -> 3; matrix products, arithmetic and copies ran while one was open for 1% -> 0% of each run, Pallas kernels for 18% -> 14%
where the time goes in v3:
time: 161 us
  blocking collectives  84.7 us (53%)
  Pallas kernels  45.7 us (28%)
  starting transfers between devices  21.6 us (13%)
  waiting for transfers between devices  4.04 us (3%)
  local copies, waits for them, and re-layouts  3.47 us (2%)
    all_to_all x1, blocking collectives, per_device(): packed = lax.all_to_all(packed, chips, 0, 0, tiled=True)  45 us
    all_to_all x1, blocking collectives, per_device(): gathered = lax.all_to_all(summed, chips, 0, 0, tiled=True)  39.7 us
    pallas_call x1, Pallas kernels, upper(): pl.pallas_call(upper_kernel, in_specs=specs(len(operands)), out_specs=out...  19.5 us
    pallas_call x5, Pallas kernels, call(): pl.pallas_call(kernel, in_specs=specs(len(operands)), out_shape=out_shape...  9.16 us
    pallas_call x1, Pallas kernels, lower(): pl.pallas_call(lower_kernel, in_specs=specs(len(operands)), out_specs=out...  8.27 us
    ppermute x1, starting transfers between devices, per_device(): diag = lax.ppermute(for_down, both, corner_in)  5.06 us
    pallas_call x1, Pallas kernels, lower_forward(): pl.pallas_call(lower_forward_kernel, out_shape=(wide, full, scale, wide,...  4.91 us
    ppermute x2, starting transfers between devices, per_device(): corner = lax.ppermute(corner, both, corner_out)  4.58 us
  transfers between devices with their start and end apart: 12, of which 3 were waited for; matrix products, arithmetic and copies ran while one was open for 0% of the time, Pallas kernels for 14%

profile of v3, /device:TPU:1, one launch (start us, length us, event | category | flops | bytes accessed | tf_op | source)
XLA Modules:
  0.0 160.6 jit_solution(17976636996621159424)
XLA Ops:
  0.6 0.0 copy-start.10
  0.7 0.9 copy-done.10
  1.6 0.9 copy-done.12
  2.5 5.1 %collective-permute-start.2 = (bf16[12,24,384]{2,1,0:T(8,128)(2,1)S(1)}, bf16[12,24,384]{2,1,0:T(8,128)(2,1)S(1)}, u32[]{:S(2)}, u32[]{:S(2)}) collective-permute-start(bf16[12,24,384]{2,1,0:T(8,128)(2,1)S(1)} %get-tuple-element.67), channel_id=1, source_target_pairs={{1,16},{2,17},{3,18},{4,19},{5,20},{6,21},{7,22},{8,23},{9,24},{10... | collective-permute-start | bytes 663560 | tf_op jit(solution)/shard_map/ppermute | solution.py:832
  7.6 0.4 collective-permute-start.1
  8.0 2.8 %collective-permute-start = (bf16[12,24,384]{2,1,0:T(8,128)(2,1)S(1)}, bf16[12,24,384]{2,1,0:T(8,128)(2,1)S(1)}, u32[]{:S(2)}, u32[]{:S(2)}) collective-permute-start(bf16[12,24,384]{2,1,0:T(8,128)(2,1)S(1)} %get-tuple-element.66), channel_id=1, source_target_pairs={{1,0},{2,1},{3,2},{4,3},{5,4},{6,5},{7,6},{8,7},{9,8},{10,9},{11,1... | collective-permute-start | bytes 663560 | tf_op jit(solution)/shard_map/ppermute | solution.py:830
  10.7 0.1 pad_add_fusion.ids
  10.8 0.0 copy-done
  10.8 0.0 copy-done.28
  10.8 1.5 copy-done.1
  12.3 0.0 copy-start.6
  12.3 0.0 copy-start.7
  12.4 0.0 copy-start.8
  12.4 0.0 copy-start.9
  12.4 0.0 copy-start.11
  12.4 0.0 copy-start.13
  12.4 0.0 copy-start.14
  12.4 0.0 copy-start.15
  12.4 0.0 copy-start.18
  12.4 0.0 copy-start.20
  12.5 0.0 copy-start.21
  12.5 0.0 copy-start.22
  12.5 0.0 copy-start.24
  12.5 0.0 copy-start.26
  12.5 3.8 %bias_expand.1 = (f32[3,144,576]{2,1,0:T(8,128)S(1)}, f32[3,144,288]{2,1,0:T(8,128)S(1)}, f32[3,144,576]{2,1,0:T(8,128)S(1)}) custom-call(s32[3]{0:T(128)S(1)} %pad_add_fusion.ids, f32[17,6,3312]{2,1,0:T(8,128)S(1)} %copy-done.1, f32[9,12,3312]{2,1,0:T(8,128)S(1)} %copy-done, f32[4,3312]{1,0:T(4,128)S(1)} %copy-done.28), custom_call_target="tpu_custom_call" | custom-call | flops 7000000000 | bytes 21000000 | tf_op jit(solution)/shard_map/bias_expand/pallas_call | solution.py:299
  16.3 0.0 collective-permute-done.right
  16.3 0.0 collective-permute-done.2.diag
  16.3 2.8 %collective-permute-done.1.up = bf16[12,24,384]{2,1,0:T(8,128)(2,1)S(1)} collective-permute-done((bf16[12,24,384]{2,1,0:T(8,128)(2,1)S(1)}, bf16[12,24,384]{2,1,0:T(8,128)(2,1)S(1)}, u32[]{:S(2)}, u32[]{:S(2)}) %collective-permute-start.1) | collective-permute-done | bytes 221216 | tf_op jit(solution)/shard_map/ppermute | solution.py:831
  19.1 0.0 copy-done.2
  19.1 0.0 copy-done.3
  19.1 0.0 copy-done.4
  19.1 0.0 copy-done.5
  19.1 0.0 copy-done.6
  19.2 19.5 %upper.1 = (f32[144,384]{1,0:T(8,128)S(1)}, bf16[3,432,192]{2,1,0:T(8,128)(2,1)S(1)}, bf16[576,192]{1,0:T(8,128)(2,1)S(1)}, bf16[112,192]{1,0:T(8,128)(2,1)S(1)}...) custom-call(s32[3]{0:T(128)S(1)} %pad_add_fusion.ids, ...), custom_call_target="tpu_custom_call" | custom-call | flops 24999999488 | bytes 75000000 | tf_op jit(solution)/shard_map/upper/pallas_call | solution.py:525
  38.8 1.6 %collective-permute-start.7 = (bf16[8192,128]{1,0:T(8,128)(2,1)}, bf16[8192,128]{1,0:T(8,128)(2,1)S(1)}, u32[]{:S(2)}, u32[]{:S(2)}) collective-permute-start(bf16[8192,128]{1,0:T(8,128)(2,1)} %get-tuple-element.95), channel_id=1, source_target_pairs={{0,1},{1,0},{2,3},{3,2},{4,5},{5,4},{6,7},{7,6},{8,9},{9,8},{10,11... | collective-permute-start | bytes 6291464 | tf_op jit(solution)/shard_map/ppermute | solution.py:846
  40.4 4.2 %collective-permute-start.5 = (bf16[48,192]{1,0:T(8,128)(2,1)S(1)}, bf16[48,192]{1,0:T(8,128)(2,1)S(1)}, u32[]{:S(2)}, u32[]{:S(2)}) collective-permute-start(bf16[48,192]{1,0:T(8,128)(2,1)S(1)} %get-tuple-element.75), channel_id=1, source_target_pairs={{16,1},{17,2},{18,3},{19,4},{20,5},{21,6},{22,7},{23,8},{24,9},{25... | collective-permute-start | bytes 55304 | tf_op jit(solution)/shard_map/ppermute | solution.py:844
  44.6 0.2 collective-permute-start.3
  44.8 0.3 collective-permute-start.4
  45.1 4.9 %lower_forward.1 = (bf16[576,192]{1,0:T(8,128)(2,1)S(1)}, f32[576,192]{1,0:T(8,128)S(1)}, f32[576,1]{1,0:T(8,128)S(1)}, bf16[576,192]{1,0:T(8,128)(2,1)S(1)}, bf...) custom-call(bf16[3,432,192]{2,1,0:T(8,128)(2,1)S(1)} %get-tuple-elem, ...), custom_call_target="tpu_custom_call" | custom-call | flops 5000000000 | bytes 15000000 | tf_op jit(solution)/shard_map/lower_forward/pallas_call | solution.py:622
  50.0 0.0 collective-permute-done.5.corner
  50.0 0.0 collective-permute-done.3.lon
  50.0 0.0 collective-permute-done.4.lat
  50.1 0.0 copy-start.29
  50.1 8.3 %lower.1 = (f32[288,384]{1,0:T(8,128)S(1)}, f32[144,384]{1,0:T(8,128)S(1)}, bf16[96,384]{1,0:T(8,128)(2,1)S(1)}, bf16[96,384]{1,0:T(8,128)(2,1)S(1)}, bf16[64,38...) custom-call(s32[3]{0:T(128)S(1)} %pad_add_fusion.ids, ...), custom_call_target="tpu_custom_call" | custom-call | flops 10000000000 | bytes 30000000 | tf_op jit(solution)/shard_map/lower/pallas_call | solution.py:713
  58.4 0.8 collective-permute-start.6
  59.2 0.0 collective-permute-done.7.theirs
  59.2 1.1 chip_two.1.upper
  60.3 0.4 collective-permute-done.6.theirs
  60.7 0.7 chip_one.1
  61.5 45.0 %all_to_all.10.blocks = bf16[64,160,128]{2,1,0:T(8,128)(2,1)S(1)} all-to-all(bf16[64,160,128]{2,1,0:T(8,128)(2,1)S(1)} %chip_one.1), channel_id=1, replica_groups=mesh['lat'=8,'chip'=8,'core'=2] {'lat','chip'}, dimensions={0} | all-to-all | bytes 5242880 | tf_op jit(solution)/shard_map/all_to_all | solution.py:863
  106.4 1.0 total.1
  107.4 39.7 %all_to_all.11.mine = bf16[64,160,128]{2,1,0:T(8,128)(2,1)S(1)} all-to-all(bf16[64,160,128]{2,1,0:T(8,128)(2,1)S(1)} %total.1), channel_id=1, replica_groups=mesh['lat'=8,'chip'=8,'core'=2] {'lat','chip'}, dimensions={0} | all-to-all | bytes 5242880 | tf_op jit(solution)/shard_map/all_to_all | solution.py:868
  147.1 2.6 %collective-permute-start.8 = (bf16[64,160,128]{2,1,0:T(8,128)(2,1)S(1)}, bf16[64,160,128]{2,1,0:T(8,128)(2,1)S(1)}, u32[]{:S(2)}, u32[]{:S(2)}) collective-permute-start(bf16[64,160,128]{2,1,0:T(8,128)(2,1)S(1)} %all_to_all.11.mine), channel_id=1, source_target_pairs={{0,1},{1,0},{2,3},{3,2},{4,5},{5,4},{6,7},{7,6},{8,9},{9,8},{10,11... | collective-permute-start | bytes 7864328 | tf_op jit(solution)/shard_map/ppermute | solution.py:872
  149.7 0.4 collective-permute-start.11
  150.1 0.7 collective-permute-start.9
  150.8 2.6 %collective-permute-start.10 = (bf16[96,384]{1,0:T(8,128)(2,1)S(1)}, bf16[96,384]{1,0:T(8,128)(2,1)S(1)}, u32[]{:S(2)}, u32[]{:S(2)}) collective-permute-start(bf16[96,384]{1,0:T(8,128)(2,1)S(1)} %get-tuple-element.108), channel_id=1, source_target_pairs={{16,0},{32,16},{48,32},{64,48},{80,64},{96,80},{112,96},{0,112},{1... | collective-permute-start | bytes 221192 | tf_op jit(solution)/shard_map/ppermute | solution.py:865
  153.4 0.8 collective-permute-done.8.theirs
  154.2 4.7 %last.1 = (f32[192,576]{1,0:T(8,128)}, f32[192,192]{1,0:T(8,128)}, f32[192,768]{1,0:T(8,128)}, f32[192,768]{1,0:T(8,128)}, f32[768,384]{1,0:T(8,128)}, /*index=5...) custom-call(s32[3]{0:T(128)S(1)} %pad_add_fusion.ids, ...), custom_call_target="tpu_custom_call" | custom-call | flops 6000000000 | bytes 18000000 | tf_op jit(solution)/shard_map/last/pallas_call | solution.py:739
  159.0 0.0 collective-permute-done.11.corner
  159.0 0.0 collective-permute-done.9.lon
  159.0 0.0 collective-permute-done.10.lat
  159.0 0.0 copy-done.23
  159.0 0.0 copy-done.27
  159.0 1.6 %assemble.1 = (f32[12,24,384]{2,1,0:T(8,128)}, f32[72,1,768]{2,1,0:T(1,128)}) custom-call(s32[3]{0:T(128)S(1)} %pad_add_fusion.ids, f32[288,384]{1,0:T(8,128)S(1)} %get-tuple-element.105.own, f32[144,384]{1,0:T(8,128)S(1)} %get-tuple-element.106.own_two, bf16[96,384]{1,0:T(8,128)(2,1)S(1)} %collective-permute-done.9.lon, ...), custom_call_target="tpu_custom_call" | custom-call | flops 3000000000 | bytes 9000000 | tf_op jit(solution)/shard_map/assemble/pallas_call | solution.py:739
  (33 shorter events, 0.1 us)
Async XLA Ops:
  0.6 0.9 copy-start.10
  1.6 0.9 copy-start.12
  2.5 8.3 %copy-start = (f32[9,12,3312]{2,1,0:T(8,128)S(1)}, f32[9,12,3312]{2,1,0:T(8,128)}, u32[]{:S(2)}) copy-start(f32[9,12,3312]{2,1,0:T(8,128)} %two.1) | copy-start | bytes 4292356
  2.5 8.3 %copy-start.28 = (f32[4,3312]{1,0:T(4,128)S(1)}, f32[4,3312]{1,0:T(4,128)}, u32[]{:S(2)}) copy-start(f32[4,3312]{1,0:T(4,128)} %constant.40.clone.codes) | copy-start | bytes 158980
  2.5 13.7 %collective-permute-start.2 = (bf16[12,24,384]{2,1,0:T(8,128)(2,1)S(1)}, bf16[12,24,384]{2,1,0:T(8,128)(2,1)S(1)}, u32[]{:S(2)}, u32[]{:S(2)}) collective-permute-start(bf16[12,24,384]{2,1,0:T(8,128)(2,1)S(1)} %get-tuple-element.67), channel_id=1, source_target_pairs={{1,16},{2,17},{3,18},{4,19},{5,20},{6,21},{7,22},{8,23},{9,24},{10... | collective-permute-start | bytes 663560 | tf_op jit(solution)/shard_map/ppermute | solution.py:832
  7.6 11.5 %collective-permute-start.1 = (bf16[12,24,384]{2,1,0:T(8,128)(2,1)S(1)}, bf16[12,24,384]{2,1,0:T(8,128)(2,1)S(1)}, u32[]{:S(2)}, u32[]{:S(2)}) collective-permute-start(bf16[12,24,384]{2,1,0:T(8,128)(2,1)S(1)} %get-tuple-element.67), channel_id=1, source_target_pairs={{0,16},{16,32},{32,48},{48,64},{64,80},{80,96},{96,112},{112,0},{1... | collective-permute-start | bytes 663560 | tf_op jit(solution)/shard_map/ppermute | solution.py:831
  8.0 8.3 %collective-permute-start = (bf16[12,24,384]{2,1,0:T(8,128)(2,1)S(1)}, bf16[12,24,384]{2,1,0:T(8,128)(2,1)S(1)}, u32[]{:S(2)}, u32[]{:S(2)}) collective-permute-start(bf16[12,24,384]{2,1,0:T(8,128)(2,1)S(1)} %get-tuple-element.66), channel_id=1, source_target_pairs={{1,0},{2,1},{3,2},{4,3},{5,4},{6,5},{7,6},{8,7},{9,8},{10,9},{11,1... | collective-permute-start | bytes 663560 | tf_op jit(solution)/shard_map/ppermute | solution.py:830
  10.8 1.5 copy-start.1
  12.3 6.7 %copy-start.2 = (bf16[384,1536]{1,0:T(8,128)(2,1)S(1)}, bf16[384,1536]{1,0:T(8,128)(2,1)}, u32[]{:S(2)}) copy-start(bf16[384,1536]{1,0:T(8,128)(2,1)} %up_two.1) | copy-start | bytes 3538948
  12.3 6.7 %copy-start.3 = (bf16[1536,384]{1,0:T(8,128)(2,1)S(1)}, bf16[1536,384]{1,0:T(8,128)(2,1)}, u32[]{:S(2)}) copy-start(bf16[1536,384]{1,0:T(8,128)(2,1)} %down_two.1) | copy-start | bytes 3538948
  12.3 6.7 %copy-start.4 = (bf16[384,1152]{1,0:T(8,128)(2,1)S(1)}, bf16[384,1152]{1,0:T(8,128)(2,1)}, u32[]{:S(2)}) copy-start(bf16[384,1152]{1,0:T(8,128)(2,1)} %qkv_two.1) | copy-start | bytes 2654212
  12.3 6.7 %copy-start.5 = (bf16[768,384]{1,0:T(8,128)(2,1)S(1)}, bf16[768,384]{1,0:T(8,128)(2,1)}, u32[]{:S(2)}) copy-start(bf16[768,384]{1,0:T(8,128)(2,1)} %merge.1) | copy-start | bytes 1769476
  12.3 6.7 %copy-start.6 = (bf16[384,384]{1,0:T(8,128)(2,1)S(1)}, bf16[384,384]{1,0:T(8,128)(2,1)}, u32[]{:S(2)}) copy-start(bf16[384,384]{1,0:T(8,128)(2,1)} %proj_two.1) | copy-start | bytes 884740
  12.3 6.7 %copy-start.7 = (bf16[192,768]{1,0:T(8,128)(2,1)S(1)}, bf16[192,768]{1,0:T(8,128)(2,1)}, u32[]{:S(2)}) copy-start(bf16[192,768]{1,0:T(8,128)(2,1)} %up_one.5) | copy-start | bytes 884740
  12.4 6.7 %copy-start.8 = (bf16[768,192]{0,1:T(8,128)(2,1)S(1)}, bf16[768,192]{0,1:T(8,128)(2,1)}, u32[]{:S(2)}) copy-start(bf16[768,192]{0,1:T(8,128)(2,1)} %param.33) | copy-start | bytes 884740
  12.4 6.7 %copy-start.9 = (bf16[192,576]{1,0:T(8,128)(2,1)S(1)}, bf16[192,576]{1,0:T(8,128)(2,1)}, u32[]{:S(2)}) copy-start(bf16[192,576]{1,0:T(8,128)(2,1)} %qkv_one.5) | copy-start | bytes 663556
  12.4 6.7 %copy-start.11 = (bf16[1,12,24,384]{3,2,1,0:T(8,128)(2,1)S(1)}, bf16[1,12,24,384]{3,2,1,0:T(8,128)(2,1)}, u32[]{:S(2)}) copy-start(bf16[1,12,24,384]{3,2,1,0:T(8,128)(2,1)} %param.27) | copy-start | bytes 663556
  12.4 6.7 %copy-start.13 = (bf16[1,6,12,768]{3,2,1,0:T(8,128)(2,1)S(1)}, bf16[1,6,12,768]{3,2,1,0:T(8,128)(2,1)}, u32[]{:S(2)}) copy-start(bf16[1,6,12,768]{3,2,1,0:T(8,128)(2,1)} %param.28) | copy-start | bytes 331780
  12.4 6.7 %copy-start.14 = (bf16[192,192]{1,0:T(8,128)(2,1)S(1)}, bf16[192,192]{1,0:T(8,128)(2,1)}, u32[]{:S(2)}) copy-start(bf16[192,192]{1,0:T(8,128)(2,1)} %proj_one.5) | copy-start | bytes 221188
  12.4 6.7 %copy-start.15 = (bf16[3,576,432]{2,1,0:T(8,128)(2,1)S(1)}, bf16[3,576,432]{2,1,0:T(8,128)(2,1)}, u32[]{:S(2)}) copy-start(bf16[3,576,432]{2,1,0:T(8,128)(2,1)} %constant.42.clone.gather) | copy-start | bytes 4478980
  12.4 6.7 %copy-start.18 = (bf16[2,432,288]{2,1,0:T(8,128)(2,1)S(1)}, bf16[2,432,288]{2,1,0:T(8,128)(2,1)}, u32[]{:S(2)}) copy-start(bf16[2,432,288]{2,1,0:T(8,128)(2,1)} %constant.41.clone.select) | copy-start | bytes 1492996
  12.4 6.7 %copy-start.20 = (bf16[272,576]{1,0:T(8,128)(2,1)S(1)}, bf16[272,576]{1,0:T(8,128)(2,1)}, u32[]{:S(2)}) copy-start(bf16[272,576]{1,0:T(8,128)(2,1)} %constant.44.clone.strips) | copy-start | bytes 940036
  12.5 6.7 %copy-start.21 = (bf16[144,576]{1,0:T(8,128)(2,1)S(1)}, bf16[144,576]{1,0:T(8,128)(2,1)}, u32[]{:S(2)}) copy-start(bf16[144,576]{1,0:T(8,128)(2,1)} %constant.49.clone.fold_ref) | copy-start | bytes 497668
  12.5 6.7 %copy-start.22 = (bf16[128,576]{1,0:T(8,128)(2,1)S(1)}, bf16[128,576]{1,0:T(8,128)(2,1)}, u32[]{:S(2)}) copy-start(bf16[128,576]{1,0:T(8,128)(2,1)} %constant.48.clone.mask_t_ref) | copy-start | bytes 442372
  12.5 6.7 %copy-start.24 = (bf16[576,128]{1,0:T(8,128)(2,1)S(1)}, bf16[576,128]{1,0:T(8,128)(2,1)}, u32[]{:S(2)}) copy-start(bf16[576,128]{1,0:T(8,128)(2,1)} %constant.47.clone.mask_ref) | copy-start | bytes 442372
  12.5 6.7 %copy-start.26 = (bf16[144,288]{1,0:T(8,128)(2,1)S(1)}, bf16[144,288]{1,0:T(8,128)(2,1)}, u32[]{:S(2)}) copy-start(bf16[144,288]{1,0:T(8,128)(2,1)} %constant.43.clone.cot_select) | copy-start | bytes 248836
  38.8 20.4 %collective-permute-start.7 = (bf16[8192,128]{1,0:T(8,128)(2,1)}, bf16[8192,128]{1,0:T(8,128)(2,1)S(1)}, u32[]{:S(2)}, u32[]{:S(2)}) collective-permute-start(bf16[8192,128]{1,0:T(8,128)(2,1)} %get-tuple-element.95), channel_id=1, source_target_pairs={{0,1},{1,0},{2,3},{3,2},{4,5},{5,4},{6,7},{7,6},{8,9},{9,8},{10,11... | collective-permute-start | bytes 6291464 | tf_op jit(solution)/shard_map/ppermute | solution.py:846
  40.4 9.6 %collective-permute-start.5 = (bf16[48,192]{1,0:T(8,128)(2,1)S(1)}, bf16[48,192]{1,0:T(8,128)(2,1)S(1)}, u32[]{:S(2)}, u32[]{:S(2)}) collective-permute-start(bf16[48,192]{1,0:T(8,128)(2,1)S(1)} %get-tuple-element.75), channel_id=1, source_target_pairs={{16,1},{17,2},{18,3},{19,4},{20,5},{21,6},{22,7},{23,8},{24,9},{25... | collective-permute-start | bytes 55304 | tf_op jit(solution)/shard_map/ppermute | solution.py:844
  44.6 5.5 %collective-permute-start.3 = (bf16[112,192]{1,0:T(8,128)(2,1)S(1)}, bf16[112,192]{1,0:T(8,128)(2,1)S(1)}, u32[]{:S(2)}, u32[]{:S(2)}) collective-permute-start(bf16[112,192]{1,0:T(8,128)(2,1)S(1)} %get-tuple-element.73), channel_id=1, source_target_pairs={{0,1},{1,2},{2,3},{3,4},{4,5},{5,6},{6,7},{7,8},{8,9},{9,10},{10,1... | collective-permute-start | bytes 129032 | tf_op jit(solution)/shard_map/ppermute | solution.py:842
  44.8 5.2 %collective-permute-start.4 = (bf16[112,192]{1,0:T(8,128)(2,1)S(1)}, bf16[112,192]{1,0:T(8,128)(2,1)S(1)}, u32[]{:S(2)}, u32[]{:S(2)}) collective-permute-start(bf16[112,192]{1,0:T(8,128)(2,1)S(1)} %get-tuple-element.74), channel_id=1, source_target_pairs={{16,0},{32,16},{48,32},{64,48},{80,64},{96,80},{112,96},{0,112},{1... | collective-permute-start | bytes 129032 | tf_op jit(solution)/shard_map/ppermute | solution.py:843
  45.1 5.0 %copy-start.16 = (bf16[2,424,576]{2,1,0:T(8,128)(2,1)S(1)}, bf16[2,424,576]{2,1,0:T(8,128)(2,1)}, u32[]{:S(2)}) copy-start(bf16[2,424,576]{2,1,0:T(8,128)(2,1)} %constant.50.clone.to_tokens) | copy-start | bytes 2930692
  45.1 5.0 %copy-start.17 = (bf16[576,576]{1,0:T(8,128)(2,1)S(1)}, bf16[576,576]{1,0:T(8,128)(2,1)}, u32[]{:S(2)}) copy-start(bf16[576,576]{1,0:T(8,128)(2,1)} %constant.45.clone.back_own) | copy-start | bytes 1990660
  45.1 5.0 %copy-start.19 = (bf16[576,272]{1,0:T(8,128)(2,1)S(1)}, bf16[576,272]{1,0:T(8,128)(2,1)}, u32[]{:S(2)}) copy-start(bf16[576,272]{1,0:T(8,128)(2,1)} %constant.46.clone.back_strips) | copy-start | bytes 940036
  45.1 5.0 %copy-start.25 = (bf16[264,144]{1,0:T(8,128)(2,1)S(1)}, bf16[264,144]{1,0:T(8,128)(2,1)}, u32[]{:S(2)}) copy-start(bf16[264,144]{1,0:T(8,128)(2,1)} %constant.51.clone.to_two) | copy-start | bytes 228100
  50.1 9.1 %copy-start.29 = (bf16[8192,128]{1,0:T(8,128)(2,1)S(1)}, bf16[8192,128]{1,0:T(8,128)(2,1)}, u32[]{:S(2)}) copy-start(bf16[8192,128]{1,0:T(8,128)(2,1)} %get-tuple-element.94.mine) | copy-start | bytes 6291460
  58.4 2.3 %collective-permute-start.6 = (bf16[2048,128]{1,0:T(8,128)(2,1)S(1)}, bf16[2048,128]{1,0:T(8,128)(2,1)S(1)}, u32[]{:S(2)}, u32[]{:S(2)}) collective-permute-start(bf16[2048,128]{1,0:T(8,128)(2,1)S(1)} %get-tuple-element.93), channel_id=1, source_target_pairs={{0,1},{1,0},{2,3},{3,2},{4,5},{5,4},{6,7},{7,6},{8,9},{9,8},{10,11... | collective-permute-start | bytes 1572872 | tf_op jit(solution)/shard_map/ppermute | solution.py:858
  147.1 7.1 %collective-permute-start.8 = (bf16[64,160,128]{2,1,0:T(8,128)(2,1)S(1)}, bf16[64,160,128]{2,1,0:T(8,128)(2,1)S(1)}, u32[]{:S(2)}, u32[]{:S(2)}) collective-permute-start(bf16[64,160,128]{2,1,0:T(8,128)(2,1)S(1)} %all_to_all.11.mine), channel_id=1, source_target_pairs={{0,1},{1,0},{2,3},{3,2},{4,5},{5,4},{6,7},{7,6},{8,9},{9,8},{10,11... | collective-permute-start | bytes 7864328 | tf_op jit(solution)/shard_map/ppermute | solution.py:872
  149.7 9.3 %collective-permute-start.11 = (bf16[64,384]{1,0:T(8,128)(2,1)S(1)}, bf16[64,384]{1,0:T(8,128)(2,1)S(1)}, u32[]{:S(2)}, u32[]{:S(2)}) collective-permute-start(bf16[64,384]{1,0:T(8,128)(2,1)S(1)} %get-tuple-element.109), channel_id=1, source_target_pairs={{16,1},{17,2},{18,3},{19,4},{20,5},{21,6},{22,7},{23,8},{24,9},{25... | collective-permute-start | bytes 147464 | tf_op jit(solution)/shard_map/ppermute | solution.py:866
  150.1 8.9 %collective-permute-start.9 = (bf16[96,384]{1,0:T(8,128)(2,1)S(1)}, bf16[96,384]{1,0:T(8,128)(2,1)S(1)}, u32[]{:S(2)}, u32[]{:S(2)}) collective-permute-start(bf16[96,384]{1,0:T(8,128)(2,1)S(1)} %get-tuple-element.107), channel_id=1, source_target_pairs={{0,1},{1,2},{2,3},{3,4},{4,5},{5,6},{6,7},{7,8},{8,9},{9,10},{10,1... | collective-permute-start | bytes 221192 | tf_op jit(solution)/shard_map/ppermute | solution.py:864
  150.8 8.2 %copy-start.23 = (bf16[288,256]{1,0:T(8,128)(2,1)S(1)}, bf16[288,256]{1,0:T(8,128)(2,1)}, u32[]{:S(2)}) copy-start(bf16[288,256]{1,0:T(8,128)(2,1)} %constant.52.clone.place) | copy-start | bytes 442372
  150.8 8.2 %copy-start.27 = (bf16[144,256]{1,0:T(8,128)(2,1)S(1)}, bf16[144,256]{1,0:T(8,128)(2,1)}, u32[]{:S(2)}) copy-start(bf16[144,256]{1,0:T(8,128)(2,1)} %constant.53.clone.place_two) | copy-start | bytes 221188
  150.8 8.2 %collective-permute-start.10 = (bf16[96,384]{1,0:T(8,128)(2,1)S(1)}, bf16[96,384]{1,0:T(8,128)(2,1)S(1)}, u32[]{:S(2)}, u32[]{:S(2)}) collective-permute-start(bf16[96,384]{1,0:T(8,128)(2,1)S(1)} %get-tuple-element.108), channel_id=1, source_target_pairs={{16,0},{32,16},{48,32},{64,48},{80,64},{96,80},{112,96},{0,112},{1... | collective-permute-start | bytes 221192 | tf_op jit(solution)/shard_map/ppermute | solution.py:865

commit v4 on v3

--- a/solution.py
+++ b/solution.py
@@ -141,6 +141,16 @@
     return tuple(jnp.asarray(v, BF16) for v in (mask, mask.T, fold))
 
 
+def blocks_of_pairs():
+    masks = []
+    for heads in (4, 2):
+        row, lane = np.arange(heads * WINDOW)[:, None], np.arange(2 * heads * HEAD)[None]
+        same = row // WINDOW == lane % (heads * HEAD) // HEAD
+        part = (row % WINDOW >= WINDOW // 2) == (lane >= heads * HEAD)
+        masks += [(same & part).astype(np.float32), (same & part).astype(np.float32).T]
+    return tuple(jnp.asarray(v, BF16) for v in masks)
+
+
 def params(microseconds, vmem):
     return {
         "compiler_params": pltpu.CompilerParams(vmem_limit_bytes=vmem * MIB),
@@ -202,13 +212,19 @@
 
 
 def attend(parts, mask, mask_t, fold):
+    masks = [
+        part[5] if len(part) > 5 else (mask[: part[4] * WINDOW, : part[4] * HEAD], mask_t[: part[4] * HEAD, : part[4] * WINDOW])
+        for part in parts
+    ]
     scores = [
-        nt(keys, spread(queries, mask, heads)) * FACTOR + bias for queries, keys, _, bias, heads in parts
+        nt(part[1], jnp.concatenate([part[0]] * part[4], axis=0) * own[0]) * FACTOR + part[3]
+        for part, own in zip(parts, masks)
     ]
     powers = [jnp.exp(score - jnp.max(score, axis=0, keepdims=True)) for score in scores]
     chances = [power * (1.0 / jnp.sum(power, axis=0, keepdims=True)) for power in powers]
     taken = [
-        pull(part[2], chance.astype(BF16), mask_t, fold, part[4]) for part, chance in zip(parts, chances)
+        nt(fold[:, : part[4] * WINDOW], tn(part[2], chance.astype(BF16)).astype(BF16) * own[1])
+        for part, own, chance in zip(parts, masks, chances)
     ]
     return taken, chances
 
@@ -369,6 +385,7 @@
     bias_a, bias_b, bias_two,
     qkv_one, proj_one, up_one, down_one, merge, qkv_two, proj_two, up_two, down_two,
     select, gather, cot_select, strips, mask_ref, mask_t_ref, fold_ref,
+    pair_four, pair_four_t, pair_two, pair_two_t,
     out_ref, xw_ref, grad_ref, lon_ref, lat_ref, corner_ref, mine_ref, theirs_ref,
     q_ref, k_ref, v_ref, att_ref, xm_ref, am_ref, one_ref, p_ref, packed, sems,
 ):
@@ -396,21 +413,24 @@
 
     @pl.loop(0, 3)
     def _(wr):
-        places = [
-            (slice(wc * WINDOW, (wc + 1) * WINDOW), slice(start * HEAD, (start + heads) * HEAD), heads)
-            for wc in range(3)
-            for start, heads in GROUPS_ONE
-        ]
-        parts = [
-            (
-                q_ref[wr, rows, lanes], k_ref[wr, rows, lanes], v_ref[wr, rows, lanes],
-                bias_a[wr] if heads == 4 else bias_b[wr], heads,
-            )
-            for rows, lanes, heads in places
-        ]
+        first, second, third = (slice(wc * WINDOW, (wc + 1) * WINDOW) for wc in range(3))
+        parts = []
+        for start, heads in GROUPS_ONE:
+            lanes = slice(start * HEAD, (start + heads) * HEAD)
+            bias = bias_a[wr] if heads == 4 else bias_b[wr]
+            refs = (q_ref, k_ref, v_ref)
+            pair = (pair_four[...], pair_four_t[...]) if heads == 4 else (pair_two[...], pair_two_t[...])
+            joined = [
+                jnp.concatenate([ref[wr, third, lanes], ref[wr, first, lanes]], axis=1) for ref in refs
+            ]
+            parts.append((*(ref[wr, second, lanes] for ref in refs), bias, heads))
+            parts.append((*joined, bias, heads, pair))
         taken, _ = attend(parts, mask, mask_t, fold)
-        for (rows, lanes, heads), value in zip(places, taken):
-            att_ref[wr, rows, lanes] = value.astype(BF16)
+        for index, (start, heads) in enumerate(GROUPS_ONE):
+            lanes, width = slice(start * HEAD, (start + heads) * HEAD), heads * HEAD
+            att_ref[wr, second, lanes] = taken[2 * index].astype(BF16)
+            att_ref[wr, third, lanes] = taken[2 * index + 1][:, :width].astype(BF16)
+            att_ref[wr, first, lanes] = taken[2 * index + 1][:, width:].astype(BF16)
 
     xm_ref[...] = nn(gather[0], xw_ref[0]) + nn(gather[1], xw_ref[1]) + nn(gather[2], xw_ref[2])
     am_ref[...] = (
@@ -632,14 +652,12 @@
 
 
 def lower_kernel(
-    ids, out_two, own, lon, lat, corner,
-    normed_ref, full_ref, scale_ref, q_ref, k_ref, v_ref, pa_ref, pb_ref, att_ref,
+    ids, own, lon, lat, corner,
+    normed_ref, q_ref, k_ref, v_ref, pa_ref, pb_ref, att_ref,
     normed_two_ref, full_two_ref, scale_two_ref, act_ref, slope_ref,
-    qkv_one, proj_one, up_one, down_one,
-    back_own, back_strips, to_tokens, to_two, mask_ref, mask_t_ref, fold_ref,
-    out_ref, out_two_ref, lon_ref, lat_ref, corner_ref, mine_ref, theirs_ref,
-    gs_ref, raised_ref, gm_ref, gml_ref, ga_ref, gq_ref, gk_ref, gv_ref, gx_ref,
-    packed, sems,
+    proj_one, up_one, down_one, back_own, back_strips, mask_ref, mask_t_ref, fold_ref,
+    gm_ref, gq_ref, gk_ref, gv_ref, mine_ref, theirs_ref,
+    gs_ref, raised_ref, gml_ref, ga_ref, packed, sems,
 ):
     mask, mask_t, fold = mask_ref[...], mask_t_ref[...], fold_ref[...]
     arrived = jnp.concatenate([lon[...], lat[...], corner[...]], axis=0)
@@ -679,8 +697,16 @@
     packed[1, 3456 - packed.shape[1] :, :] = jnp.zeros((640, LANES), BF16)
     for half in range(2):
         send_half(ids, packed, half, mine_ref, theirs_ref, sems, True)
-
-    for rows in row_slices:
+    for half in range(2):
+        send_half(ids, packed, half, mine_ref, theirs_ref, sems, False)
+
+
+def finish_kernel(
+    ids, gm_ref, gq_ref, gk_ref, gv_ref, full_ref, scale_ref, out_two, qkv_one, to_tokens, to_two,
+    out_ref, out_two_ref, lon_ref, lat_ref, corner_ref, gx_ref,
+):
+    for row in range(2):
+        rows = slice(row * 288, (row + 1) * 288)
         grad_normed = (
             nt(gq_ref[rows, :], qkv_one[:, :C1])
             + nt(gk_ref[rows, :], qkv_one[:, C1 : 2 * C1])
@@ -703,35 +729,29 @@
         strip = [cells[at : at + count], two[144 + kind * 40 : 144 + (kind + 1) * 40]]
         ref[...] = jnp.concatenate(strip, axis=0).astype(BF16)
         at += count
-    for half in range(2):
-        send_half(ids, packed, half, mine_ref, theirs_ref, sems, False)
 
 
 def lower(*operands):
     shape = jax.ShapeDtypeStruct
-    wide = pltpu.VMEM((576, C1), BF16)
+    wide = shape((576, C1), BF16)
     return pl.pallas_call(
         lower_kernel,
         in_specs=specs(len(operands)),
-        out_specs=out_specs(7, 2),
+        out_specs=out_specs(6, 2),
         out_shape=(
-            shape((288, C2), F32),
-            shape((144, C2), F32),
-            *(shape((count, C2), BF16) for count in SHIFT),
-            packed_shape(LOWER_BLOCK),
-            packed_shape(LOWER_BLOCK),
+            shape((576, C1), F32), wide, wide, wide,
+            packed_shape(LOWER_BLOCK), packed_shape(LOWER_BLOCK),
         ),
         scratch_shapes=[
             pltpu.VMEM((576, C1), F32),
             pltpu.VMEM((576, 768), BF16),
-            pltpu.VMEM((576, C1), F32),
-            wide, wide, wide, wide, wide,
-            pltpu.VMEM((576, C1), F32),
+            pltpu.VMEM((576, C1), BF16),
+            pltpu.VMEM((576, C1), BF16),
             pltpu.VMEM((2, CHIPS * LOWER_BLOCK, LANES), BF16),
             pltpu.SemaphoreType.DMA((2,)),
         ],
+        name="lower",
         **params(10, 32),
-        name="lower",
     )(*operands)
 
 
@@ -746,11 +766,13 @@
     )(*operands)
 
 
-def chip_kernel(ids, mine, theirs, out):
-    rows = out.shape[1]
-    for block in range(CHIPS):
-        at = slice(block * rows, (block + 1) * rows)
-        out[block] = (mine[at].astype(F32) + theirs[at].astype(F32)).astype(BF16)
+def chip_kernel(ids, mine_two, theirs_two, mine_one, theirs_one, out):
+    for low, mine, theirs in ((0, mine_two, theirs_two), (UPPER_BLOCK, mine_one, theirs_one)):
+        rows = mine.shape[0] // CHIPS
+        for block in range(CHIPS):
+            at = slice(block * rows, (block + 1) * rows)
+            value = mine[at].astype(F32) + theirs[at].astype(F32)
+            out[block, low : low + rows, :] = value.astype(BF16)
 
 
 def total(blocks, low, rows):
@@ -758,13 +780,6 @@
     for block in range(1, CHIPS):
         value = value + blocks[block, low : low + rows, :].astype(F32)
     return value.astype(BF16)
-
-
-def chip_one_kernel(ids, mine, theirs, upper, out):
-    for block in range(CHIPS):
-        at = slice(block * LOWER_BLOCK, (block + 1) * LOWER_BLOCK)
-        out[block, :UPPER_BLOCK, :] = upper[block]
-        out[block, UPPER_BLOCK:, :] = (mine[at].astype(F32) + theirs[at].astype(F32)).astype(BF16)
 
 
 def total_kernel(ids, blocks, out):
@@ -837,7 +852,7 @@
     out_two, xw, grad_own, lon_strip, lat_strip, corner, mine_two, theirs_two = upper(
         ids, tokens[0], cotangent[0], right, up, diag, bias_a, bias_b, bias_c,
         qkv_one, proj_one, up_one, down_one, merge_weight, qkv_two, proj_two, up_two, down_two,
-        select, gather, cot_select, strips, mask, mask_t, fold,
+        select, gather, cot_select, strips, mask, mask_t, fold, *blocks_of_pairs(),
     )
     lon_strip = lax.ppermute(lon_strip, lon, to_right)
     lat_strip = lax.ppermute(lat_strip, "lat", to_up)
@@ -847,20 +862,27 @@
     result = lambda *dims: jax.ShapeDtypeStruct(dims, F32)
     blocks = lambda rows: jax.ShapeDtypeStruct((CHIPS, rows, LANES), BF16)
     chips = ("lat", "chip")
-    packed_two = call(chip_kernel, "chip_two", 3, 16, blocks(UPPER_BLOCK), (ids, mine_two, theirs_two))
     to_tokens, to_two, place, place_two = output_constants()
     kept = lower_forward(xw, bias_a, bias_b, qkv_one, proj_one, up_one, mask, mask_t, fold)
-    own_cells, own_two, lon_strip, lat_strip, corner, mine_one, theirs_one = lower(
-        ids, out_two, grad_own, lon_strip, lat_strip, corner, *kept,
-        qkv_one, proj_one, up_one, down_one,
-        back_own, back_strips, to_tokens, to_two, mask, mask_t, fold,
+    normed, full, scale, *others = kept
+    *gradients, mine_one, theirs_one = lower(
+        ids, grad_own, lon_strip, lat_strip, corner, normed, *others,
+        proj_one, up_one, down_one, back_own, back_strips, mask, mask_t, fold,
     )
     theirs_one = lax.ppermute(theirs_one, "core", other_core)
     packed = call(
-        chip_one_kernel, "chip_one", 1, 16, blocks(UPPER_BLOCK + LOWER_BLOCK),
-        (ids, mine_one, theirs_one, packed_two),
+        chip_kernel, "chip", 3, 24, blocks(UPPER_BLOCK + LOWER_BLOCK),
+        (ids, mine_two, theirs_two, mine_one, theirs_one),
     )
     packed = lax.all_to_all(packed, chips, 0, 0, tiled=True)
+    strip = lambda count: jax.ShapeDtypeStruct((count, C2), BF16)
+    own_cells, own_two, lon_strip, lat_strip, corner = call(
+        finish_kernel, "finish", 4, 12,
+        (result(288, C2), result(144, C2), *(strip(count) for count in SHIFT)),
+        (ids, *gradients, full, scale, out_two, qkv_one, to_tokens, to_two),
+        [pltpu.VMEM((576, C1), F32)],
+    )
+    packed, own_cells = lax.optimization_barrier((packed, own_cells))
     lon_strip = lax.ppermute(lon_strip, lon, to_right)
     lat_strip = lax.ppermute(lat_strip, "lat", to_up)
     corner = lax.ppermute(corner, both, corner_out)

time: 161 us -> 165 us (1.025)
  blocking collectives: 84.7 us -> 40.5 us
  waiting for transfers between devices: 4.04 us -> 28.8 us
  local copies, waits for them, and re-layouts: 3.47 us -> 18 us
  starting transfers between devices: 21.6 us -> 31.1 us
    all_to_all x1 -> x0, blocking collectives: 45 us -> none  [per_device(): packed = lax.all_to_all(packed, chips, 0, 0, tiled=True)]
    all_to_all x0 -> x1, waiting for transfers between devices: none -> 23.8 us  [per_device(): packed = lax.all_to_all(packed, chips, 0, 0, tiled=True)]
    unnamed x60 -> x102, local copies, waits for them, and re-layouts: 3.47 us -> 18 us
    all_to_all x0 -> x1, starting transfers between devices: none -> 9.77 us  [per_device(): packed = lax.all_to_all(packed, chips, 0, 0, tiled=True)]
    pallas_call x1, Pallas kernels: 8.27 us -> 6.59 us  [lower(): pl.pallas_call(lower_kernel, in_specs=specs(len(operands)), out_specs=out...]
  transfers between devices with their start and end apart: 12 -> 13, of which waited for: 3 -> 4; matrix products, arithmetic and copies ran while one was open for 0% -> 0% of each run, Pallas kernels for 14% -> 13%
where the time goes in v4:
time: 165 us
  Pallas kernels  45 us (27%)
  blocking collectives  40.5 us (25%)
  starting transfers between devices  31.1 us (19%)
  waiting for transfers between devices  28.8 us (17%)
  local copies, waits for them, and re-layouts  18 us (11%)
    all_to_all x1, blocking collectives, per_device(): gathered = lax.all_to_all(summed, chips, 0, 0, tiled=True)  40.5 us
    all_to_all x1, waiting for transfers between devices, per_device(): packed = lax.all_to_all(packed, chips, 0, 0, tiled=True)  23.8 us
    pallas_call x1, Pallas kernels, upper(): pl.pallas_call(upper_kernel, in_specs=specs(len(operands)), out_specs=out...  19.1 us
    unnamed x102, local copies, waits for them, and re-layouts  18 us
    pallas_call x5, Pallas kernels, call(): pl.pallas_call(kernel, in_specs=specs(len(operands)), out_shape=out_shape...  10.7 us
    all_to_all x1, starting transfers between devices, per_device(): packed = lax.all_to_all(packed, chips, 0, 0, tiled=True)  9.77 us
    pallas_call x1, Pallas kernels, lower(): pl.pallas_call(lower_kernel, in_specs=specs(len(operands)), out_specs=out...  6.59 us
    ppermute x1, starting transfers between devices, per_device(): diag = lax.ppermute(for_down, both, corner_in)  5.06 us
  transfers between devices with their start and end apart: 13, of which 4 were waited for; matrix products, arithmetic and copies ran while one was open for 0% of the time, Pallas kernels for 13%

profile of v4, /device:TPU:1, one launch (start us, length us, event | category | flops | bytes accessed | tf_op | source)
XLA Modules:
  0.0 164.7 jit_solution(17165323303920783783)
XLA Ops:
  0.6 0.0 copy-start.11
  0.7 0.9 copy-done.11
  1.6 0.9 copy-done.13
  2.5 5.1 %collective-permute-start.2 = (bf16[12,24,384]{2,1,0:T(8,128)(2,1)S(1)}, bf16[12,24,384]{2,1,0:T(8,128)(2,1)S(1)}, u32[]{:S(2)}, u32[]{:S(2)}) collective-permute-start(bf16[12,24,384]{2,1,0:T(8,128)(2,1)S(1)} %get-tuple-element.73), channel_id=1, source_target_pairs={{1,16},{2,17},{3,18},{4,19},{5,20},{6,21},{7,22},{8,23},{9,24},{10... | collective-permute-start | bytes 663560 | tf_op jit(solution)/shard_map/ppermute | solution.py:847
  7.6 0.4 collective-permute-start.1
  8.0 2.8 %collective-permute-start = (bf16[12,24,384]{2,1,0:T(8,128)(2,1)S(1)}, bf16[12,24,384]{2,1,0:T(8,128)(2,1)S(1)}, u32[]{:S(2)}, u32[]{:S(2)}) collective-permute-start(bf16[12,24,384]{2,1,0:T(8,128)(2,1)S(1)} %get-tuple-element.72), channel_id=1, source_target_pairs={{1,0},{2,1},{3,2},{4,3},{5,4},{6,5},{7,6},{8,7},{9,8},{10,9},{11,1... | collective-permute-start | bytes 663560 | tf_op jit(solution)/shard_map/ppermute | solution.py:845
  10.7 0.1 pad_add_fusion.ids
  10.8 1.5 copy-done.2
  12.3 0.0 copy-start.7
  12.3 0.0 copy-start.8
  12.4 0.0 copy-start.12
  12.4 0.0 copy-start.14
  12.4 0.0 copy-start.16
  12.4 0.0 copy-start.19
  12.4 0.0 copy-start.21
  12.5 0.0 copy-start.22
  12.5 0.0 copy-start.23
  12.5 0.0 copy-start.24
  12.5 0.0 copy-start.25
  12.5 0.0 copy-start.27
  12.5 0.0 copy-start.29
  12.5 0.0 copy-start.30
  12.5 0.0 copy-start.32
  12.6 3.8 %bias_expand.1 = (f32[3,144,576]{2,1,0:T(8,128)S(1)}, f32[3,144,288]{2,1,0:T(8,128)S(1)}, f32[3,144,576]{2,1,0:T(8,128)S(1)}) custom-call(s32[3]{0:T(128)S(1)} %pad_add_fusion.ids, f32[17,6,3312]{2,1,0:T(8,128)S(1)} %copy-done.2, f32[9,12,3312]{2,1,0:T(8,128)S(1)} %copy-done.1, f32[4,3312]{1,0:T(4,128)S(1)} %copy-done.33), custom_call_target="tpu_custom_call" | custom-call | flops 7000000000 | bytes 21000000 | tf_op jit(solution)/shard_map/bias_expand/pallas_call | solution.py:315
  16.3 2.7 %collective-permute-done.1.up = bf16[12,24,384]{2,1,0:T(8,128)(2,1)S(1)} collective-permute-done((bf16[12,24,384]{2,1,0:T(8,128)(2,1)S(1)}, bf16[12,24,384]{2,1,0:T(8,128)(2,1)S(1)}, u32[]{:S(2)}, u32[]{:S(2)}) %collective-permute-start.1) | collective-permute-done | bytes 221216 | tf_op jit(solution)/shard_map/ppermute | solution.py:846
  19.3 19.1 %upper.1 = (f32[144,384]{1,0:T(8,128)S(1)}, bf16[3,432,192]{2,1,0:T(8,128)(2,1)S(1)}, bf16[576,192]{1,0:T(8,128)(2,1)S(1)}, bf16[112,192]{1,0:T(8,128)(2,1)S(1)}...) custom-call(s32[3]{0:T(128)S(1)} %pad_add_fusion.ids, ...), custom_call_target="tpu_custom_call" | custom-call | flops 24999999488 | bytes 75000000 | tf_op jit(solution)/shard_map/upper/pallas_call | solution.py:545
  38.4 0.7 copy-done.49
  39.0 1.6 collective-permute-start.3
  40.6 4.1 %collective-permute-start.6 = (bf16[48,192]{1,0:T(8,128)(2,1)S(1)}, bf16[48,192]{1,0:T(8,128)(2,1)S(1)}, u32[]{:S(2)}, u32[]{:S(2)}) collective-permute-start(bf16[48,192]{1,0:T(8,128)(2,1)S(1)} %get-tuple-element.82), channel_id=1, source_target_pairs={{16,1},{17,2},{18,3},{19,4},{20,5},{21,6},{22,7},{23,8},{24,9},{25... | collective-permute-start | bytes 55304 | tf_op jit(solution)/shard_map/ppermute | solution.py:859
  44.7 0.2 collective-permute-start.4
  44.9 0.3 collective-permute-start.5
  45.2 4.9 %lower_forward.1 = (bf16[576,192]{1,0:T(8,128)(2,1)S(1)}, f32[576,192]{1,0:T(8,128)S(1)}, f32[576,1]{1,0:T(8,128)S(1)}, bf16[576,192]{1,0:T(8,128)(2,1)S(1)}, bf...) custom-call(bf16[3,432,192]{2,1,0:T(8,128)(2,1)S(1)} %get-tuple-elem, ...), custom_call_target="tpu_custom_call" | custom-call | flops 5000000000 | bytes 15000000 | tf_op jit(solution)/shard_map/lower_forward/pallas_call | solution.py:642
  50.1 0.8 copy-done.35
  51.0 6.6 %lower.1 = (f32[576,192]{1,0:T(8,128)S(1)}, bf16[576,192]{1,0:T(8,128)(2,1)S(1)}, bf16[576,192]{1,0:T(8,128)(2,1)S(1)}, bf16[576,192]{1,0:T(8,128)(2,1)S(1)}, bf...) custom-call(s32[3]{0:T(128)S(1)} %pad_add_fusion.ids, bf16[576,192]{1,0:T(8,128)(2,1)S(1)} %get-tuple-element.79.own, ...), custom_call_target="tpu_custom_call" | custom-call | flops 10000000000 | bytes 30000000 | tf_op jit(solution)/shard_map/lower/pallas_call | solution.py:737
  57.6 0.8 copy-done.37
  58.4 0.7 copy-done.41
  59.1 0.7 copy-done.43
  59.8 0.7 copy-done.45
  60.5 0.6 collective-permute-start.7
  61.1 1.5 collective-permute-done.7.theirs_one
  62.7 1.1 chip.1
  63.8 1.5 copy-done
  65.3 9.8 %all-to-all-start = ((bf16[64,160,128]{2,1,0:T(8,128)(2,1)}), bf16[64,160,128]{2,1,0:T(8,128)(2,1)S(1)}, u32[]{:S(2)}, u32[]{:S(2)}) async-start(bf16[64,160,128]{2,1,0:T(8,128)(2,1)} %copy-done), calls=%async_computation | async-start | bytes 5242880 | tf_op jit(solution)/shard_map/all_to_all | solution.py:877
  75.1 0.0 copy-start.17
  75.1 1.2 copy-done.17
  76.3 1.1 copy-done.36
  77.4 1.1 copy-done.38
  78.5 1.0 copy-done.42
  79.4 1.0 copy-done.44
  80.4 1.0 copy-done.46
  81.4 0.9 copy-done.50
  82.3 2.2 %finish.1 = (f32[288,384]{1,0:T(8,128)S(1)}, f32[144,384]{1,0:T(8,128)S(1)}, bf16[96,384]{1,0:T(8,128)(2,1)S(1)}, bf16[96,384]{1,0:T(8,128)(2,1)S(1)}, bf16[64,384]{1,0:T(8,128)(2,1)S(1)}) custom-call(s32[3]{0:T(128)S(1)} %pad_add_fusion.ids, f32[576,192]{1,0:T(8,128)S(1)} %copy-done.38, bf16[576,192]{1,0:T(8,128)(2,1)S(1)} %copy-done.42, ...), custom_call_target="tpu_custom_call" | custom-call | flops 4000000000 | bytes 12000000 | tf_op jit(solution)/shard_map/finish/pallas_call | solution.py:759
  84.5 0.8 copy-done.39
  85.3 0.7 copy-done.47
  85.9 23.8 %all-to-all-done.blocks = bf16[64,160,128]{2,1,0:T(8,128)(2,1)S(1)} async-done(((bf16[64,160,128]{2,1,0:T(8,128)(2,1)}), bf16[64,160,128]{2,1,0:T(8,128)(2,1)S(1)}, u32[]{:S(2)}, u32[]{:S(2)}) %all-to-all-start) | async-done | bytes 2621472 | tf_op jit(solution)/shard_map/all_to_all | solution.py:877
  109.7 1.0 total.1
  110.7 40.5 %all_to_all.10.mine = bf16[64,160,128]{2,1,0:T(8,128)(2,1)S(1)} all-to-all(bf16[64,160,128]{2,1,0:T(8,128)(2,1)S(1)} %total.1), channel_id=1, replica_groups=mesh['lat'=8,'chip'=8,'core'=2] {'lat','chip'}, dimensions={0} | all-to-all | bytes 5242880 | tf_op jit(solution)/shard_map/all_to_all | solution.py:890
  151.2 2.5 %collective-permute-start.8 = (bf16[64,160,128]{2,1,0:T(8,128)(2,1)S(1)}, bf16[64,160,128]{2,1,0:T(8,128)(2,1)S(1)}, u32[]{:S(2)}, u32[]{:S(2)}) collective-permute-start(bf16[64,160,128]{2,1,0:T(8,128)(2,1)S(1)} %all_to_all.10.mine), channel_id=1, source_target_pairs={{0,1},{1,0},{2,3},{3,2},{4,5},{5,4},{6,7},{7,6},{8,9},{9,8},{10,11... | collective-permute-start | bytes 7864328 | tf_op jit(solution)/shard_map/ppermute | solution.py:894
  153.7 0.4 collective-permute-start.11
  154.2 0.7 collective-permute-start.9
  154.9 2.7 %collective-permute-start.10 = (bf16[96,384]{1,0:T(8,128)(2,1)S(1)}, bf16[96,384]{1,0:T(8,128)(2,1)S(1)}, u32[]{:S(2)}, u32[]{:S(2)}) collective-permute-start(bf16[96,384]{1,0:T(8,128)(2,1)S(1)} %get-tuple-element.120), channel_id=1, source_target_pairs={{16,0},{32,16},{48,32},{64,48},{80,64},{96,80},{112,96},{0,112},{1... | collective-permute-start | bytes 221192 | tf_op jit(solution)/shard_map/ppermute | solution.py:887
  157.6 0.7 collective-permute-done.8.theirs
  158.3 4.7 %last.1 = (f32[192,576]{1,0:T(8,128)}, f32[192,192]{1,0:T(8,128)}, f32[192,768]{1,0:T(8,128)}, f32[192,768]{1,0:T(8,128)}, f32[768,384]{1,0:T(8,128)}, /*index=5...) custom-call(s32[3]{0:T(128)S(1)} %pad_add_fusion.ids, ...), custom_call_target="tpu_custom_call" | custom-call | flops 6000000000 | bytes 18000000 | tf_op jit(solution)/shard_map/last/pallas_call | solution.py:759
  163.1 1.6 assemble.1
  (76 shorter events, 0.2 us)
Async XLA Ops:
  0.6 0.9 copy-start.11
  1.6 0.9 copy-start.13
  2.5 8.3 %copy-start.1 = (f32[9,12,3312]{2,1,0:T(8,128)S(1)}, f32[9,12,3312]{2,1,0:T(8,128)}, u32[]{:S(2)}) copy-start(f32[9,12,3312]{2,1,0:T(8,128)} %two.1) | copy-start | bytes 4292356
  2.5 8.3 %copy-start.33 = (f32[4,3312]{1,0:T(4,128)S(1)}, f32[4,3312]{1,0:T(4,128)}, u32[]{:S(2)}) copy-start(f32[4,3312]{1,0:T(4,128)} %constant.48.clone.codes) | copy-start | bytes 158980
  2.5 13.8 %collective-permute-start.2 = (bf16[12,24,384]{2,1,0:T(8,128)(2,1)S(1)}, bf16[12,24,384]{2,1,0:T(8,128)(2,1)S(1)}, u32[]{:S(2)}, u32[]{:S(2)}) collective-permute-start(bf16[12,24,384]{2,1,0:T(8,128)(2,1)S(1)} %get-tuple-element.73), channel_id=1, source_target_pairs={{1,16},{2,17},{3,18},{4,19},{5,20},{6,21},{7,22},{8,23},{9,24},{10... | collective-permute-start | bytes 663560 | tf_op jit(solution)/shard_map/ppermute | solution.py:847
  7.6 11.5 %collective-permute-start.1 = (bf16[12,24,384]{2,1,0:T(8,128)(2,1)S(1)}, bf16[12,24,384]{2,1,0:T(8,128)(2,1)S(1)}, u32[]{:S(2)}, u32[]{:S(2)}) collective-permute-start(bf16[12,24,384]{2,1,0:T(8,128)(2,1)S(1)} %get-tuple-element.73), channel_id=1, source_target_pairs={{0,16},{16,32},{32,48},{48,64},{64,80},{80,96},{96,112},{112,0},{1... | collective-permute-start | bytes 663560 | tf_op jit(solution)/shard_map/ppermute | solution.py:846
  8.0 8.3 %collective-permute-start = (bf16[12,24,384]{2,1,0:T(8,128)(2,1)S(1)}, bf16[12,24,384]{2,1,0:T(8,128)(2,1)S(1)}, u32[]{:S(2)}, u32[]{:S(2)}) collective-permute-start(bf16[12,24,384]{2,1,0:T(8,128)(2,1)S(1)} %get-tuple-element.72), channel_id=1, source_target_pairs={{1,0},{2,1},{3,2},{4,3},{5,4},{6,5},{7,6},{8,7},{9,8},{10,9},{11,1... | collective-permute-start | bytes 663560 | tf_op jit(solution)/shard_map/ppermute | solution.py:845
  10.8 1.5 copy-start.2
  12.3 6.7 %copy-start.3 = (bf16[384,1536]{1,0:T(8,128)(2,1)S(1)}, bf16[384,1536]{1,0:T(8,128)(2,1)}, u32[]{:S(2)}) copy-start(bf16[384,1536]{1,0:T(8,128)(2,1)} %up_two.1) | copy-start | bytes 3538948
  12.3 6.7 %copy-start.4 = (bf16[1536,384]{1,0:T(8,128)(2,1)S(1)}, bf16[1536,384]{1,0:T(8,128)(2,1)}, u32[]{:S(2)}) copy-start(bf16[1536,384]{1,0:T(8,128)(2,1)} %down_two.1) | copy-start | bytes 3538948
  12.3 6.7 %copy-start.5 = (bf16[384,1152]{1,0:T(8,128)(2,1)S(1)}, bf16[384,1152]{1,0:T(8,128)(2,1)}, u32[]{:S(2)}) copy-start(bf16[384,1152]{1,0:T(8,128)(2,1)} %qkv_two.1) | copy-start | bytes 2654212
  12.3 6.7 %copy-start.6 = (bf16[768,384]{1,0:T(8,128)(2,1)S(1)}, bf16[768,384]{1,0:T(8,128)(2,1)}, u32[]{:S(2)}) copy-start(bf16[768,384]{1,0:T(8,128)(2,1)} %merge.1) | copy-start | bytes 1769476
  12.3 6.7 %copy-start.7 = (bf16[384,384]{1,0:T(8,128)(2,1)S(1)}, bf16[384,384]{1,0:T(8,128)(2,1)}, u32[]{:S(2)}) copy-start(bf16[384,384]{1,0:T(8,128)(2,1)} %proj_two.1) | copy-start | bytes 884740
  12.3 6.7 %copy-start.8 = (bf16[192,768]{1,0:T(8,128)(2,1)S(1)}, bf16[192,768]{1,0:T(8,128)(2,1)}, u32[]{:S(2)}) copy-start(bf16[192,768]{1,0:T(8,128)(2,1)} %up_one.5) | copy-start | bytes 884740
  12.4 6.7 %copy-start.9 = (bf16[768,192]{0,1:T(8,128)(2,1)S(1)}, bf16[768,192]{0,1:T(8,128)(2,1)}, u32[]{:S(2)}) copy-start(bf16[768,192]{0,1:T(8,128)(2,1)} %param.37) | copy-start | bytes 884740
  12.4 6.7 %copy-start.10 = (bf16[192,576]{1,0:T(8,128)(2,1)S(1)}, bf16[192,576]{1,0:T(8,128)(2,1)}, u32[]{:S(2)}) copy-start(bf16[192,576]{1,0:T(8,128)(2,1)} %qkv_one.5) | copy-start | bytes 663556
  12.4 6.7 %copy-start.12 = (bf16[1,12,24,384]{3,2,1,0:T(8,128)(2,1)S(1)}, bf16[1,12,24,384]{3,2,1,0:T(8,128)(2,1)}, u32[]{:S(2)}) copy-start(bf16[1,12,24,384]{3,2,1,0:T(8,128)(2,1)} %param.31) | copy-start | bytes 663556
  12.4 6.7 %copy-start.14 = (bf16[1,6,12,768]{3,2,1,0:T(8,128)(2,1)S(1)}, bf16[1,6,12,768]{3,2,1,0:T(8,128)(2,1)}, u32[]{:S(2)}) copy-start(bf16[1,6,12,768]{3,2,1,0:T(8,128)(2,1)} %param.32) | copy-start | bytes 331780
  12.4 6.7 %copy-start.15 = (bf16[192,192]{1,0:T(8,128)(2,1)S(1)}, bf16[192,192]{1,0:T(8,128)(2,1)}, u32[]{:S(2)}) copy-start(bf16[192,192]{1,0:T(8,128)(2,1)} %proj_one.5) | copy-start | bytes 221188
  12.4 6.7 %copy-start.16 = (bf16[3,576,432]{2,1,0:T(8,128)(2,1)S(1)}, bf16[3,576,432]{2,1,0:T(8,128)(2,1)}, u32[]{:S(2)}) copy-start(bf16[3,576,432]{2,1,0:T(8,128)(2,1)} %constant.50.clone.gather) | copy-start | bytes 4478980
  12.4 6.7 %copy-start.19 = (bf16[2,432,288]{2,1,0:T(8,128)(2,1)S(1)}, bf16[2,432,288]{2,1,0:T(8,128)(2,1)}, u32[]{:S(2)}) copy-start(bf16[2,432,288]{2,1,0:T(8,128)(2,1)} %constant.49.clone.select) | copy-start | bytes 1492996
  12.4 6.7 %copy-start.21 = (bf16[272,576]{1,0:T(8,128)(2,1)S(1)}, bf16[272,576]{1,0:T(8,128)(2,1)}, u32[]{:S(2)}) copy-start(bf16[272,576]{1,0:T(8,128)(2,1)} %constant.52.clone.strips) | copy-start | bytes 940036
  12.5 6.7 %copy-start.22 = (bf16[256,576]{1,0:T(8,128)(2,1)S(1)}, bf16[256,576]{1,0:T(8,128)(2,1)}, u32[]{:S(2)}) copy-start(bf16[256,576]{1,0:T(8,128)(2,1)} %constant.59.clone.pair_four_t) | copy-start | bytes 884740
  12.5 6.7 %copy-start.23 = (bf16[576,256]{1,0:T(8,128)(2,1)S(1)}, bf16[576,256]{1,0:T(8,128)(2,1)}, u32[]{:S(2)}) copy-start(bf16[576,256]{1,0:T(8,128)(2,1)} %constant.58.clone.pair_four) | copy-start | bytes 884740
  12.5 6.7 %copy-start.24 = (bf16[144,576]{1,0:T(8,128)(2,1)S(1)}, bf16[144,576]{1,0:T(8,128)(2,1)}, u32[]{:S(2)}) copy-start(bf16[144,576]{1,0:T(8,128)(2,1)} %constant.57.clone.fold_ref) | copy-start | bytes 497668
  12.5 6.7 %copy-start.25 = (bf16[128,576]{1,0:T(8,128)(2,1)S(1)}, bf16[128,576]{1,0:T(8,128)(2,1)}, u32[]{:S(2)}) copy-start(bf16[128,576]{1,0:T(8,128)(2,1)} %constant.56.clone.mask_t_ref) | copy-start | bytes 442372
  12.5 6.7 %copy-start.27 = (bf16[576,128]{1,0:T(8,128)(2,1)S(1)}, bf16[576,128]{1,0:T(8,128)(2,1)}, u32[]{:S(2)}) copy-start(bf16[576,128]{1,0:T(8,128)(2,1)} %constant.55.clone.mask_ref) | copy-start | bytes 442372
  12.5 6.7 %copy-start.29 = (bf16[144,288]{1,0:T(8,128)(2,1)S(1)}, bf16[144,288]{1,0:T(8,128)(2,1)}, u32[]{:S(2)}) copy-start(bf16[144,288]{1,0:T(8,128)(2,1)} %constant.51.clone.cot_select) | copy-start | bytes 248836
  12.5 6.7 %copy-start.30 = (bf16[128,288]{1,0:T(8,128)(2,1)S(1)}, bf16[128,288]{1,0:T(8,128)(2,1)}, u32[]{:S(2)}) copy-start(bf16[128,288]{1,0:T(8,128)(2,1)} %constant.61.clone.pair_two_t) | copy-start | bytes 221188
  12.5 6.7 %copy-start.32 = (bf16[288,128]{1,0:T(8,128)(2,1)S(1)}, bf16[288,128]{1,0:T(8,128)(2,1)}, u32[]{:S(2)}) copy-start(bf16[288,128]{1,0:T(8,128)(2,1)} %constant.60.clone.pair_two) | copy-start | bytes 221188
  38.3 0.7 copy-start.49
  39.0 23.7 %collective-permute-start.3 = (bf16[8192,128]{1,0:T(8,128)(2,1)}, bf16[8192,128]{1,0:T(8,128)(2,1)S(1)}, u32[]{:S(2)}, u32[]{:S(2)}) collective-permute-start(bf16[8192,128]{1,0:T(8,128)(2,1)} %get-tuple-element.78), channel_id=1, source_target_pairs={{0,1},{1,0},{2,3},{3,2},{4,5},{5,4},{6,7},{7,6},{8,9},{9,8},{10,11... | collective-permute-start | bytes 6291464 | tf_op jit(solution)/shard_map/ppermute | solution.py:861
  40.6 10.3 %collective-permute-start.6 = (bf16[48,192]{1,0:T(8,128)(2,1)S(1)}, bf16[48,192]{1,0:T(8,128)(2,1)S(1)}, u32[]{:S(2)}, u32[]{:S(2)}) collective-permute-start(bf16[48,192]{1,0:T(8,128)(2,1)S(1)} %get-tuple-element.82), channel_id=1, source_target_pairs={{16,1},{17,2},{18,3},{19,4},{20,5},{21,6},{22,7},{23,8},{24,9},{25... | collective-permute-start | bytes 55304 | tf_op jit(solution)/shard_map/ppermute | solution.py:859
  44.7 6.2 %collective-permute-start.4 = (bf16[112,192]{1,0:T(8,128)(2,1)S(1)}, bf16[112,192]{1,0:T(8,128)(2,1)S(1)}, u32[]{:S(2)}, u32[]{:S(2)}) collective-permute-start(bf16[112,192]{1,0:T(8,128)(2,1)S(1)} %get-tuple-element.80), channel_id=1, source_target_pairs={{0,1},{1,2},{2,3},{3,4},{4,5},{5,6},{6,7},{7,8},{8,9},{9,10},{10,1... | collective-permute-start | bytes 129032 | tf_op jit(solution)/shard_map/ppermute | solution.py:857
  44.9 6.0 %collective-permute-start.5 = (bf16[112,192]{1,0:T(8,128)(2,1)S(1)}, bf16[112,192]{1,0:T(8,128)(2,1)S(1)}, u32[]{:S(2)}, u32[]{:S(2)}) collective-permute-start(bf16[112,192]{1,0:T(8,128)(2,1)S(1)} %get-tuple-element.81), channel_id=1, source_target_pairs={{16,0},{32,16},{48,32},{64,48},{80,64},{96,80},{112,96},{0,112},{1... | collective-permute-start | bytes 129032 | tf_op jit(solution)/shard_map/ppermute | solution.py:858
  45.2 5.8 %copy-start.18 = (bf16[576,576]{1,0:T(8,128)(2,1)S(1)}, bf16[576,576]{1,0:T(8,128)(2,1)}, u32[]{:S(2)}) copy-start(bf16[576,576]{1,0:T(8,128)(2,1)} %constant.53.clone.back_own) | copy-start | bytes 1990660
  45.2 5.8 %copy-start.20 = (bf16[576,272]{1,0:T(8,128)(2,1)S(1)}, bf16[576,272]{1,0:T(8,128)(2,1)}, u32[]{:S(2)}) copy-start(bf16[576,272]{1,0:T(8,128)(2,1)} %constant.54.clone.back_strips) | copy-start | bytes 940036
  50.1 0.8 copy-start.35
  51.0 11.7 %copy-start.34 = (bf16[8192,128]{1,0:T(8,128)(2,1)S(1)}, bf16[8192,128]{1,0:T(8,128)(2,1)}, u32[]{:S(2)}) copy-start(bf16[8192,128]{1,0:T(8,128)(2,1)} %get-tuple-element.77.mine_two) | copy-start | bytes 6291460
  57.6 0.8 copy-start.37
  58.4 0.7 copy-start.41
  59.1 0.7 copy-start.43
  59.8 0.7 copy-start.45
  60.5 2.2 %collective-permute-start.7 = (bf16[2048,128]{1,0:T(8,128)(2,1)S(1)}, bf16[2048,128]{1,0:T(8,128)(2,1)S(1)}, u32[]{:S(2)}, u32[]{:S(2)}) collective-permute-start(bf16[2048,128]{1,0:T(8,128)(2,1)S(1)} %get-tuple-element.97), channel_id=1, source_target_pairs={{0,1},{1,0},{2,3},{3,2},{4,5},{5,4},{6,7},{7,6},{8,9},{9,8},{10,11... | collective-permute-start | bytes 1572872 | tf_op jit(solution)/shard_map/ppermute | solution.py:872
  63.8 1.5 copy-start
  65.3 9.8 %copy-start.28 = (bf16[264,144]{1,0:T(8,128)(2,1)S(1)}, bf16[264,144]{1,0:T(8,128)(2,1)}, u32[]{:S(2)}) copy-start(bf16[264,144]{1,0:T(8,128)(2,1)} %constant.63.clone.to_two) | copy-start | bytes 228100
  65.3 44.4 %all-to-all-start = ((bf16[64,160,128]{2,1,0:T(8,128)(2,1)}), bf16[64,160,128]{2,1,0:T(8,128)(2,1)S(1)}, u32[]{:S(2)}, u32[]{:S(2)}) async-start(bf16[64,160,128]{2,1,0:T(8,128)(2,1)} %copy-done), calls=%async_computation | async-start | bytes 5242880 | tf_op jit(solution)/shard_map/all_to_all | solution.py:877
  75.1 1.2 copy-start.17
  76.3 1.1 copy-start.36
  77.4 1.1 copy-start.38
  78.5 1.0 copy-start.42
  79.4 1.0 copy-start.44
  80.4 1.0 copy-start.46
  81.4 0.9 copy-start.50
  84.5 0.8 copy-start.39
  85.3 0.7 copy-start.47
  151.2 7.1 %collective-permute-start.8 = (bf16[64,160,128]{2,1,0:T(8,128)(2,1)S(1)}, bf16[64,160,128]{2,1,0:T(8,128)(2,1)S(1)}, u32[]{:S(2)}, u32[]{:S(2)}) collective-permute-start(bf16[64,160,128]{2,1,0:T(8,128)(2,1)S(1)} %all_to_all.10.mine), channel_id=1, source_target_pairs={{0,1},{1,0},{2,3},{3,2},{4,5},{5,4},{6,7},{7,6},{8,9},{9,8},{10,11... | collective-permute-start | bytes 7864328 | tf_op jit(solution)/shard_map/ppermute | solution.py:894
  153.7 9.3 %collective-permute-start.11 = (bf16[64,384]{1,0:T(8,128)(2,1)S(1)}, bf16[64,384]{1,0:T(8,128)(2,1)S(1)}, u32[]{:S(2)}, u32[]{:S(2)}) collective-permute-start(bf16[64,384]{1,0:T(8,128)(2,1)S(1)} %get-tuple-element.121), channel_id=1, source_target_pairs={{16,1},{17,2},{18,3},{19,4},{20,5},{21,6},{22,7},{23,8},{24,9},{25... | collective-permute-start | bytes 147464 | tf_op jit(solution)/shard_map/ppermute | solution.py:888
  154.2 8.9 %collective-permute-start.9 = (bf16[96,384]{1,0:T(8,128)(2,1)S(1)}, bf16[96,384]{1,0:T(8,128)(2,1)S(1)}, u32[]{:S(2)}, u32[]{:S(2)}) collective-permute-start(bf16[96,384]{1,0:T(8,128)(2,1)S(1)} %get-tuple-element.119), channel_id=1, source_target_pairs={{0,1},{1,2},{2,3},{3,4},{4,5},{5,6},{6,7},{7,8},{8,9},{9,10},{10,1... | collective-permute-start | bytes 221192 | tf_op jit(solution)/shard_map/ppermute | solution.py:886
  154.8 8.2 %copy-start.26 = (bf16[288,256]{1,0:T(8,128)(2,1)S(1)}, bf16[288,256]{1,0:T(8,128)(2,1)}, u32[]{:S(2)}) copy-start(bf16[288,256]{1,0:T(8,128)(2,1)} %constant.64.clone.place) | copy-start | bytes 442372
  154.8 8.2 %copy-start.31 = (bf16[144,256]{1,0:T(8,128)(2,1)S(1)}, bf16[144,256]{1,0:T(8,128)(2,1)}, u32[]{:S(2)}) copy-start(bf16[144,256]{1,0:T(8,128)(2,1)} %constant.65.clone.place_two) | copy-start | bytes 221188
  154.8 8.2 %copy-start.40 = (f32[288,384]{1,0:T(8,128)S(1)}, f32[288,384]{1,0:T(8,128)}, u32[]{:S(2)}) copy-start(f32[288,384]{1,0:T(8,128)} %copy-done.39) | copy-start | bytes 1327108
  154.8 8.2 %copy-start.48 = (f32[144,384]{1,0:T(8,128)S(1)}, f32[144,384]{1,0:T(8,128)}, u32[]{:S(2)}) copy-start(f32[144,384]{1,0:T(8,128)} %copy-done.47) | copy-start | bytes 663556
  154.9 8.2 %collective-permute-start.10 = (bf16[96,384]{1,0:T(8,128)(2,1)S(1)}, bf16[96,384]{1,0:T(8,128)(2,1)S(1)}, u32[]{:S(2)}, u32[]{:S(2)}) collective-permute-start(bf16[96,384]{1,0:T(8,128)(2,1)S(1)} %get-tuple-element.120), channel_id=1, source_target_pairs={{16,0},{32,16},{48,32},{64,48},{80,64},{96,80},{112,96},{0,112},{1... | collective-permute-start | bytes 221192 | tf_op jit(solution)/shard_map/ppermute | solution.py:887
